TPU v7x, 32 devices: a whole 2x2x4 slice. The times are simulated.
32 devices in a mesh: rows: 16 (over z, x, core), dirs: 2 (over y).
Axes of the slice: x: 2, y: 2, z: 4, core: 2. Of those that a mesh axis runs over, the one named last changes fastest.
Arguments:
- previous: bfloat16 [24, 32, 128, 512], P('dirs', None, 'rows'), may hold values from -12 to 12
- boundary: float32 [24, 32, 512], P('dirs'), may hold values from -6 to 6
- row_coupling: float32 [24, 128, 512], P('dirs', 'rows'), may hold values from 0 to 1
- cross_gain: float32 [24], P('dirs'), may hold values from 0.5 to 3
- block_inverse: float32 [24, 128, 128], P('dirs'), may hold values from 0 to 1, as said below
- quadrant: int32 [24], P('dirs'), may hold values from 0 to 3
- sea_mask: int32 [128, 512], P('rows'), may hold values from 0 to 1, as said below
- wet_tiles: int32 [128, 4], P('rows'), may hold values 0 or 1
- quad_coef: float32 [32], replicated, may hold values from 0.05 to 0.5
Outputs:
- action: bfloat16 [24, 32, 128, 512], P('dirs', None, 'rows')
Inputs may be any that keep to these rules, and one draw needn't show every extreme that they name: `sea_mask`: in each row the land cells, if any, are the last ones, from a coastline column to the end of the row. block_inverse[d] is the inverse of the 128 x 128 lower bidiagonal matrix with 1 + cross_gain[d] on its diagonal and -cross_gain[d] just below it.
All inputs are finite; a program needn't handle non-finite values. No bound on the sum of `wet_tiles` on one device may be relied on, other than what follows from the above.
Results may differ from a plain program's by a relative error of at most 0.0027.
Values may be sent and summed in bfloat16 or wider, within the bound.
A program may use at most 128 MiB of HBM per device.

v0:
```python
import functools

import jax
import jax.numpy as jnp
from jax import lax
from jax.experimental import pallas as pl
from jax.experimental.pallas import tpu as pltpu
from jax.sharding import PartitionSpec as P

SHIFT = 2
f32 = jnp.float32
bf16 = jnp.bfloat16
MESH = pl.DeviceIdType.MESH
VMEM_BYTES = 48 * 1024 * 1024


def cost(microseconds):
    return pl.CostEstimate(
        flops=0, bytes_accessed=int(microseconds * 3_000_000), transcendentals=0
    )


def weights(coupling, sea):
    return coupling * sea, sea * (1.0 - coupling)


def visit_order(shape, backward):
    row = lax.broadcasted_iota(jnp.int32, shape, 0)
    return shape[0] - 1 - row if backward else row


def rolled(x, steps, backward):
    rows = x.shape[0]
    return pltpu.roll(x, (rows - steps if backward else steps) % rows, 0)


def row_weights(coupling, sea, backward):
    couple, weight = weights(coupling, sea)
    rows = couple.shape[0]
    order = visit_order(couple.shape, backward)
    after = jnp.where(order < rows - 1, rolled(couple, rows - 1, backward), 1.0)
    span = 1
    while span < rows - 1:
        after = after * jnp.where(order < rows - span, rolled(after, rows - span, backward), 1.0)
        span *= 2
    gain = jnp.sum(jnp.where(order == 0, couple * after, 0.0), axis=0, keepdims=True)
    return weight * after, gain


HALO_ARRAYS = 4


def scan_kernel(
    count, dir_count, chunks, boundary, sea_mask, previous, coupling, inverse, marks, out, *refs
):
    shared = (previous, coupling, inverse, marks)
    halos, refs = refs[:HALO_ARRAYS], refs[HALO_ARRAYS:]
    enter_halo, refs = refs[0], refs[1:]
    (
        gain, state, shares,
        gains, got_core, half_total, got_pair, plane, chain_in, chain_out, pair_in, pair_out, core_out,
        gain_send, gain_recv, core_send, core_recv, pair_send, pair_recv,
        chain_send, chain_recv, back_send, back_recv, last_send, last_recv, halo_send, halo_recv,
        enter_send, enter_recv,
    ) = refs
    me = lax.axis_index("rows")
    c, x, z = me % 2, (me // 2) % 2, me // 4
    depth = count // 4
    core_peer = me + 1 - 2 * c
    pair_peer = me + 2 - 4 * x
    cross_peer = core_peer + 2 - 4 * x
    dirs = gain.shape[0]
    size = dirs // chunks
    peers = (core_peer, pair_peer, cross_peer)

    def part(j):
        return pl.ds(j * size, size)

    barrier = pltpu.get_barrier_semaphore()
    for peer in peers:
        pl.semaphore_signal(barrier, inc=1, device_id={"rows": peer}, device_id_type=MESH)

    @pl.when(z > 0)
    def _():
        pl.semaphore_signal(barrier, inc=1, device_id={"rows": me - 4}, device_id_type=MESH)

    @pl.when(z < depth - 1)
    def _():
        pl.semaphore_signal(barrier, inc=1, device_id={"rows": me + 4}, device_id_type=MESH)

    mine = lax.axis_index("dirs")
    higher, lower = (mine + 1) % dir_count, (mine + dir_count - 1) % dir_count
    neighbours = (higher, lower) if dir_count > 2 else (higher,)
    for peer in neighbours:
        pl.semaphore_signal(barrier, inc=1, device_id={"dirs": peer}, device_id_type=MESH)
    pl.semaphore_wait(
        barrier, 3 + len(neighbours) + (z > 0).astype(jnp.int32) + (z < depth - 1).astype(jnp.int32)
    )

    def remote(src, dst, send, recv, peer):
        return pltpu.make_async_remote_copy(
            src_ref=src, dst_ref=dst, send_sem=send, recv_sem=recv,
            device_id={"rows": peer}, device_id_type=MESH,
        )

    gain_copies = [
        remote(gain, gains.at[i], gain_send.at[i], gain_recv.at[i], peer) for i, peer in enumerate(peers)
    ]
    core_copies = [
        remote(state.at[1 - c, :, part(j)], got_core.at[:, part(j)], core_send.at[j], core_recv.at[j], core_peer)
        for j in range(chunks)
    ]
    pair_copies = [
        remote(half_total.at[1 - x, part(j)], got_pair.at[part(j)], pair_send.at[j], pair_recv.at[j], pair_peer)
        for j in range(chunks)
    ]
    back_copies = [
        remote(pair_out.at[part(j)], pair_in.at[x, part(j)], back_send.at[j], back_recv.at[j], pair_peer)
        for j in range(chunks)
    ]
    last_copies = [
        remote(core_out.at[:, part(j)], out.at[c, :, part(j)], last_send.at[j], last_recv.at[j], core_peer)
        for j in range(chunks)
    ]

    halo_copies, enter_copies = [], []
    for way, (peer, start, to) in enumerate(((lower, 0, SHIFT), (higher, dirs - SHIFT, 0))):
        for i, half in enumerate((c, 1 - c)):
            enter_copies.append(
                pltpu.make_async_remote_copy(
                    src_ref=out.at[half, :, pl.ds(start, SHIFT)],
                    dst_ref=enter_halo.at[half, :, pl.ds(to, SHIFT)],
                    send_sem=enter_send.at[way, i], recv_sem=enter_recv.at[way, i],
                    device_id={"dirs": peer}, device_id_type=MESH,
                )
            )
        for i, array in enumerate(shared):
            halo_copies.append(
                pltpu.make_async_remote_copy(
                    src_ref=array.at[pl.ds(start, SHIFT)], dst_ref=halos[i].at[pl.ds(to, SHIFT)],
                    send_sem=halo_send.at[way, i], recv_sem=halo_recv.at[way, i],
                    device_id={"dirs": peer}, device_id_type=MESH,
                )
            )
            halo_copies[-1].start()

    flags = marks[:, 1:2, :]
    flags = flags - 2.0 * jnp.floor(0.5 * flags)
    back = jnp.concatenate([flags] * (gain.shape[-1] // flags.shape[-1]), axis=2)
    sea = sea_mask[...].astype(f32)
    for d in range(dirs):
        onward, onward_gain = row_weights(coupling[d], sea, False)
        against, _ = row_weights(coupling[d], sea, True)
        shares[d] = jnp.where(back[d] > 0.5, against, onward)
        gain[d] = onward_gain
    for copy in gain_copies:
        copy.start()
    order = [0] + list(range(chunks - 1, 0, -1))

    def compose(h, d, _):
        share = shares[d]
        for q in range(2):
            values = previous[d, pl.ds((2 * h + q) * state.shape[3], state.shape[3])].astype(f32)
            state[h, q, d] = jnp.sum(values * share[None], axis=1)
        return 0

    for j in order:
        lax.fori_loop(j * size, (j + 1) * size, functools.partial(compose, 1 - c), 0)
        core_copies[j].start()
    for j in order:
        lax.fori_loop(j * size, (j + 1) * size, functools.partial(compose, c), 0)
    c_bit, x_bit = c.astype(f32), x.astype(f32)
    core_after = c_bit + back - 2.0 * c_bit * back
    pair_after = x_bit + back - 2.0 * x_bit * back
    for copy in gain_copies:
        copy.wait_recv()
    core_mine, core_theirs = gain[...], gains[0]
    pair_mine, pair_theirs = core_mine * core_theirs, gains[1] * gains[2]
    plane_gain = pair_mine * pair_theirs

    def total(after, mine, theirs):
        return after * mine + (1.0 - after), (1.0 - after) * theirs + after

    core_a, core_b = total(core_after, core_mine, core_theirs)
    pair_a, pair_b = total(pair_after, pair_mine, pair_theirs)

    def cut(v, j):
        return v[j * size : (j + 1) * size]

    for j in order:
        core_copies[j].wait_recv()
        half_total[:, part(j)] = (
            cut(core_a, j)[None] * got_core[:, part(j)] + cut(core_b, j)[None] * state[c, :, part(j)]
        )
        pair_copies[j].start()
    for j in order:
        pair_copies[j].wait_recv()
        plane[part(j)] = cut(pair_a, j) * got_pair[part(j)] + cut(pair_b, j) * half_total[x, part(j)]

    upper = (2 * z >= depth).astype(jnp.int32)
    mine_at = 2 * c + x

    def chain(j, way):
        step = 1 - 2 * way
        has_before = jnp.where(way == 0, z > 0, z < depth - 1)
        has_after = jnp.where(way == 0, z < depth - 1, z > 0)
        copy = remote(
            chain_out.at[way, part(j)], chain_in.at[way, part(j)],
            chain_send.at[way, j], chain_recv.at[way, j], me + 4 * step,
        )

        @pl.when(has_before)
        def _():
            copy.wait_recv()

        @pl.when(jnp.logical_not(has_before))
        def _():
            chain_in[way, part(j)] = boundary[part(j), mine_at]

        @pl.when(has_after)
        def _():
            chain_out[way, part(j)] = cut(plane_gain, j) * chain_in[way, part(j)] + plane[part(j)]
            copy.start()

    def split(after, mine, theirs):
        return after * theirs + (1.0 - after), (1.0 - after) * mine + after

    pair_p, pair_q = split(pair_after, pair_mine, pair_theirs)
    core_p, core_q = split(core_after, core_mine, core_theirs)
    for j in order:
        chain(j, upper)
        chain(j, 1 - upper)
        entering = jnp.where(cut(back, j) > 0.5, chain_in[1, part(j)], chain_in[0, part(j)])
        pair_out[part(j)] = cut(pair_q, j) * entering + (1.0 - cut(pair_after, j)) * half_total[x, part(j)]
        back_copies[j].start()
        pair_in[x, part(j)] = cut(pair_p, j) * entering + cut(pair_after, j) * got_pair[part(j)]
    for j in order:
        back_copies[j].wait_recv()
        entering = pair_in[:, part(j)]
        core_out[:, part(j)] = (
            cut(core_q, j)[None] * entering + (1.0 - cut(core_after, j))[None] * state[c, :, part(j)]
        )
        last_copies[j].start()
        out[c, :, part(j)] = cut(core_p, j)[None] * entering + cut(core_after, j)[None] * got_core[:, part(j)]
        if j == 0:
            enter_copies[0].start()
        if j == chunks - 1:
            enter_copies[2].start()
    for j in order:
        last_copies[j].wait_recv()
        if j == 0:
            enter_copies[1].start()
        if j == chunks - 1:
            enter_copies[3].start()
    for copy in halo_copies + enter_copies:
        copy.wait_recv()
    for copy in halo_copies + enter_copies + gain_copies + core_copies + pair_copies + back_copies + last_copies:
        copy.wait_send()

    def drain(j, way):
        copy = remote(
            chain_out.at[way, part(j)], chain_in.at[way, part(j)],
            chain_send.at[way, j], chain_recv.at[way, j], me + 4 * (1 - 2 * way),
        )

        @pl.when(z < depth - 1 if way == 0 else z > 0)
        def _():
            copy.wait_send()

    for j in range(chunks):
        drain(j, 0)
        drain(j, 1)


def scan_devices(count, dir_count, boundary, sea_mask, previous, coupling, inverse, marks):
    dirs, bands, _, columns = previous.shape
    chunks = 1
    quarter = bands // 4
    boundary = boundary.reshape(dirs, 4, quarter, columns)
    vmem = pl.BlockSpec(memory_space=pltpu.VMEM)
    part = (dirs, quarter, columns)
    dma = pltpu.SemaphoreType.DMA
    anywhere = pl.BlockSpec(memory_space=pl.ANY)
    shared = (previous, coupling, inverse, marks)
    halos = [jax.ShapeDtypeStruct((2 * SHIFT,) + a.shape[1:], a.dtype) for a in shared]
    out, *halos = pl.pallas_call(
        functools.partial(scan_kernel, count, dir_count, chunks),
        in_specs=[vmem, vmem, vmem, vmem, anywhere, vmem],
        out_specs=[vmem] + [anywhere] * HALO_ARRAYS + [vmem],
        out_shape=[jax.ShapeDtypeStruct((2, 2) + part, f32)]
        + halos
        + [jax.ShapeDtypeStruct((2, 2, 2 * SHIFT, quarter, columns), f32)],
        scratch_shapes=[
            pltpu.VMEM((dirs, 1, columns), f32),
            pltpu.VMEM((2, 2) + part, f32),
            pltpu.VMEM(coupling.shape, f32),
            pltpu.VMEM((3, dirs, 1, columns), f32),
            pltpu.VMEM((2,) + part, f32),
            pltpu.VMEM((2,) + part, f32),
            pltpu.VMEM(part, f32),
            pltpu.VMEM(part, f32),
            pltpu.VMEM((2,) + part, f32),
            pltpu.VMEM((2,) + part, f32),
            pltpu.VMEM((2,) + part, f32),
            pltpu.VMEM(part, f32),
            pltpu.VMEM((2,) + part, f32),
            dma((3,)), dma((3,)),
            dma((chunks,)), dma((chunks,)),
            dma((chunks,)), dma((chunks,)),
            dma((2, chunks)), dma((2, chunks)),
            dma((chunks,)), dma((chunks,)),
            dma((chunks,)), dma((chunks,)),
            dma((2, HALO_ARRAYS)), dma((2, HALO_ARRAYS)),
            dma((2, 2)), dma((2, 2)),
        ],
        compiler_params=pltpu.CompilerParams(
            collective_id=0, has_side_effects=True, vmem_limit_bytes=VMEM_BYTES
        ),
        cost_estimate=cost(35),
        name="scan_devices",
    )(boundary, sea_mask, previous, coupling, inverse, marks)
    return (
        out.reshape(4, dirs, quarter, columns),
        halos[:HALO_ARRAYS],
        halos[HALO_ARRAYS].reshape(4, 2 * SHIFT, quarter, columns),
    )


def step_kernel(
    dirs, quadrant, cross_gain, halo_marks, coef, sea_mask, wet_tiles,
    previous, coupling, inverse, entering,
    halo_previous, halo_coupling, halo_inverse, halo_entering,
    out, swept, rounded, settled, sea, wet,
):
    t = pl.program_id(0)
    _, bands, rows, columns = previous.shape
    block = inverse.shape[-1]
    pieces = columns // block
    quarter = bands // 4

    @pl.when(t == 0)
    def _():
        sea[...] = sea_mask[...].astype(f32)
        for k in range(pieces):
            flag = wet_tiles[:, k : k + 1].astype(f32)
            wet[:, k * block : (k + 1) * block] = jnp.broadcast_to(flag, (rows, block))

    def sweep(previous, coupling, entering, backward):
        couple, weight = weights(coupling[0], sea[...])
        order = visit_order(couple.shape, backward)
        first = jnp.where(order == 0, couple, 0.0)
        spans, reach, span = [], couple, 1
        while span < rows:
            spans.append((span, jnp.where(order >= span, reach, 0.0)))
            reach = jnp.where(order >= span, reach * rolled(reach, span, backward), reach)
            span *= 2

        def group(q, _):
            inflow = entering[q, 0]
            for r in range(quarter):
                value = weight * previous[0, q * quarter + r].astype(f32) + first * inflow[r : r + 1]
                for span, factor in spans:
                    value = value + factor * rolled(value, span, backward)
                swept[q * quarter + r] = value
            return 0

        lax.fori_loop(0, 4, group, 0)

    def columns_solve(inverse, gain, slot, keep, sideways):
        matrix = inverse[0] if sideways else inverse[0].T
        carry = gain * (matrix[block - 1 :] if sideways else matrix[:1])
        high = matrix.astype(bf16)
        low = (matrix - high.astype(f32)).astype(bf16)
        whole = jnp.concatenate(
            [
                jnp.concatenate([high, low], axis=1),
                jnp.concatenate([high, jnp.zeros_like(low)], axis=1),
            ],
            axis=0,
        )
        before = None
        for k in range(pieces - 1, -1, -1) if sideways else range(pieces):
            here = slice(k * block, (k + 1) * block)
            x = swept[:, :, here].reshape(bands * rows, block)
            upper = x.astype(bf16)
            lower = (x - upper.astype(f32)).astype(bf16)
            both = jnp.dot(
                jnp.concatenate([upper, lower], axis=1), whole, preferred_element_type=f32
            )
            y = both[:, :block] + both[:, block:]
            if before is not None:
                y = y + (before[:, :1] if sideways else before[:, block - 1 :]) * carry
            before = y
            masked = y.reshape(bands, rows, block) * sea[:, here][None]
            rounded[slot, :, :, here] = masked.astype(bf16)
            if keep:
                settled[t, :, :, here] = masked

    def settle(previous, coupling, inverse, entering, corner, gain, slot, keep):
        for flag in (0, 1):
            pl.when(corner % 2 == flag)(
                functools.partial(sweep, previous, coupling, entering, flag == 1)
            )
        for flag in (0, 1):
            pl.when(corner // 2 == flag)(
                functools.partial(columns_solve, inverse, gain, slot, keep, flag == 1)
            )

    @pl.when(t < dirs)
    def _():
        at = jnp.minimum(t, dirs - 1)
        settle(previous, coupling, inverse, entering, quadrant[at], cross_gain[at], t + SHIFT, True)

    @pl.when(t >= dirs)
    def _():
        at = jnp.maximum(t - dirs, 0)
        settle(
            halo_previous, halo_coupling, halo_inverse, halo_entering,
            halo_marks[at, 1, 0].astype(jnp.int32), halo_marks[at, 0, 0],
            jnp.where(t < dirs + SHIFT, t - dirs, t), False,
        )

    @pl.when((t >= dirs) | (t >= 2 * SHIFT))
    def _():
        d = source_place(dirs, t)
        wet_cells = wet[...]

        def one(f, onward, against):
            energy = rounded[d + SHIFT, f].astype(f32)
            source = coef[f] * (
                energy * energy * (onward + against) - 2.0 * energy * onward * against
            )
            out[0, f] = (settled[d, f] + wet_cells * source.astype(bf16).astype(f32)).astype(bf16)

        def above(f):
            return rounded[d + 2 * SHIFT, f + 1].astype(f32)

        def below(f):
            return rounded[d, f - 1].astype(f32)

        nothing = jnp.zeros(wet.shape, f32)
        one(0, above(0), nothing)
        one(bands - 1, nothing, below(bands - 1))

        def body(f, _):
            one(f, above(f), below(f))
            return 0

        lax.fori_loop(1, bands - 1, body, 0, unroll=6 if (bands - 2) % 6 == 0 else 1)


def source_place(dirs, t):
    inner = jnp.clip(t - SHIFT, SHIFT, dirs - SHIFT - 1) if dirs > 2 * SHIFT else 0
    edge = jnp.where(t < dirs + SHIFT, t - dirs, t - 2 * SHIFT)
    return jnp.where(t < dirs, inner, edge)


def add_step(
    quadrant, cross_gain, quad_coef, sea_mask, wet_tiles,
    previous, coupling, inverse, entering, halos, halo_entering,
):
    dirs, bands, rows, columns = previous.shape
    halo_previous, halo_coupling, halo_inverse, halo_marks = halos
    smem = pl.BlockSpec(memory_space=pltpu.SMEM)

    def own(t):
        return jnp.minimum(t, dirs - 1)

    def halo(t):
        return jnp.maximum(t - dirs, 0)

    def specs(at):
        return [
            pl.BlockSpec((1,) + previous.shape[1:], lambda t: (at(t), 0, 0, 0)),
            pl.BlockSpec((1,) + coupling.shape[1:], lambda t: (at(t), 0, 0)),
            pl.BlockSpec((1,) + inverse.shape[1:], lambda t: (at(t), 0, 0)),
            pl.BlockSpec((4, 1) + entering.shape[2:], lambda t: (0, at(t), 0, 0)),
        ]

    return pl.pallas_call(
        functools.partial(step_kernel, dirs),
        grid=(dirs + 2 * SHIFT,),
        in_specs=[
            smem, smem, smem, smem,
            pl.BlockSpec(sea_mask.shape, lambda t: (0, 0)),
            pl.BlockSpec(wet_tiles.shape, lambda t: (0, 0)),
        ]
        + specs(own)
        + specs(halo),
        out_specs=pl.BlockSpec(
            (1,) + previous.shape[1:], lambda t: (source_place(dirs, t), 0, 0, 0)
        ),
        out_shape=jax.ShapeDtypeStruct(previous.shape, bf16),
        scratch_shapes=[
            pltpu.VMEM((bands, rows, columns), f32),
            pltpu.VMEM((dirs + 2 * SHIFT, bands, rows, columns), bf16),
            pltpu.VMEM((dirs, bands, rows, columns), f32),
            pltpu.VMEM((rows, columns), f32),
            pltpu.VMEM((rows, columns), f32),
        ],
        compiler_params=pltpu.CompilerParams(vmem_limit_bytes=VMEM_BYTES),
        cost_estimate=cost(20),
        name="add_step",
    )(
        quadrant, cross_gain, halo_marks, quad_coef, sea_mask, wet_tiles,
        previous, coupling, inverse, entering,
        halo_previous, halo_coupling, halo_inverse, halo_entering,
    )


def on_device(
    row_devices, dir_devices,
    previous, boundary, row_coupling, cross_gain, block_inverse, quadrant, sea_mask, wet_tiles, quad_coef,
):
    dirs = previous.shape[0]
    block = block_inverse.shape[-1]
    which = lax.broadcasted_iota(jnp.int32, (dirs, 2, block), 1)
    marks = jnp.where(
        which == 0, cross_gain[:, None, None], quadrant.astype(f32)[:, None, None]
    )
    entering, halos, halo_entering = scan_devices(
        row_devices, dir_devices, boundary, sea_mask, previous, row_coupling, block_inverse, marks
    )
    return add_step(
        quadrant, cross_gain, quad_coef, sea_mask, wet_tiles,
        previous, row_coupling, block_inverse, entering, halos, halo_entering,
    )


def solution(mesh):
    in_specs = (
        P("dirs", None, "rows", None),
        P("dirs", None, None),
        P("dirs", "rows", None),
        P("dirs"),
        P("dirs", None, None),
        P("dirs"),
        P("rows", None),
        P("rows", None),
        P(),
    )
    out_specs = P("dirs", None, "rows", None)
    return jax.shard_map(
        functools.partial(on_device, mesh.shape["rows"], mesh.shape["dirs"]),
        mesh=mesh, in_specs=in_specs, out_specs=out_specs, check_vma=False,
    )
```

profile of v0, /device:TPU:0, one launch (start us, length us, event | category | flops | bytes accessed | tf_op | source)
XLA Modules:
  0.0 70.5 jit_solution(17704719419133616709)
XLA Ops:
  0.0 0.0 copy-start.6
  0.0 0.0 copy-start.5
  0.0 0.0 copy-start.7
  0.0 0.7 %convert_element_type.3 = f32[12]{0:T(128)S(1)} convert(s32[12]{0:T(128)} %quadrant.1) | non-fusion elementwise | flops 12 | bytes 96 | tf_op jit(solution)/shard_map/convert_element_type | solution.py:519
  0.7 0.8 %copy.10.wet_tiles = s32[8,4]{1,0:T(8,128)S(1)} copy(s32[8,4]{0,1:T(4,128)} %param.16) | data formatting | bytes 256 | tf_op args[7]
  1.5 0.7 %broadcast_select_fusion.marks = f32[12,2,128]{2,1,0:T(2,128)S(1)} fusion(pred[2]{0:T(512)(128)(4,1)S(1)} %iota_compare_fusion, f32[12]{0:T(128)S(1)} %convert_element_type.3, f32[12]{0:T(128)} %cross_gain.1), kind=kLoop, calls=%fused_computation | loop fusion | flops 3072 | bytes 12386 | tf_op jit(solution)/shard_map/jit(_where)/select_n | solution.py:518
  2.2 0.0 copy-start
  2.3 1.1 %copy-done = f32[12,128,128]{2,1,0:T(8,128)S(1)} copy-done((f32[12,128,128]{2,1,0:T(8,128)S(1)}, f32[12,128,128]{2,1,0:T(8,128)}, u32[]{:S(2)}) %copy-start) | copy-done | bytes 786456
  3.4 0.0 copy-start.2
  3.4 0.9 %copy-done.2 = f32[12,8,512]{2,1,0:T(8,128)S(1)} copy-done((f32[12,8,512]{2,1,0:T(8,128)S(1)}, f32[12,8,512]{2,1,0:T(8,128)}, u32[]{:S(2)}) %copy-start.2) | copy-done | bytes 196632
  4.3 0.0 copy-start.3
  4.3 1.1 %copy-done.3 = f32[12,32,512]{2,1,0:T(8,128)S(1)} copy-done((f32[12,32,512]{2,1,0:T(8,128)S(1)}, f32[12,32,512]{2,1,0:T(8,128)}, u32[]{:S(2)}) %copy-start.3) | copy-done | bytes 786456
  5.4 0.0 copy-start.4
  5.4 0.7 %copy-done.4 = s32[8,512]{1,0:T(8,128)S(1)} copy-done((s32[8,512]{1,0:T(8,128)S(1)}, s32[8,512]{1,0:T(8,128)}, u32[]{:S(2)}) %copy-start.4) | copy-done | bytes 16408
  6.2 0.0 copy-start.1
  6.2 44.5 %scan_devices.1 = (f32[2,2,12,8,512]{4,3,2,1,0:T(8,128)S(1)}, bf16[4,32,8,512]{3,2,1,0:T(8,128)(2,1)S(1)}, f32[4,8,512]{2,1,0:T(8,128)S(1)}, f32[4,128,128]{2,1,...) custom-call(f32[12,4,8,512]{3,2,1,0:T(8,128)S(1)} %bitcast.4, s32[8,512]{1,0:T(8,128)S(1)} %copy-done.4, ...), custom_call_target="tpu_custom_call" | custom-call | bytes 105000000 | tf_op jit(solution)/shard_map/scan_devices/pallas_call | solution.py:286
  50.7 0.0 copy-done.6
  50.7 0.0 copy-done.5
  50.7 0.0 copy-done.7
  50.7 0.0 copy-done.1
  50.7 19.8 %add_step.1 = bf16[12,32,8,512]{3,2,1,0:T(8,128)(2,1)} custom-call(s32[12]{0:T(128)S(1)} %copy-done.6, f32[12]{0:T(128)S(1)} %copy-done.5, f32[4,2,128]{2,1,0:T(2,128)S(1)} %get-tuple-element.11.halo_marks, f32[32]{0:T(128)S(1)} %copy-done.7, s32[8,512]{1,0:T(8,128)S(1)} %copy-done.4, s32[8,4]{1,0:T(8,128)S(1)} %copy.10.wet_tiles, ...), custom_call_target="tpu_custom_call" | custom-call | bytes 60000000 | tf_op jit(solution)/shard_map/add_step/pallas_call | solution.py:480
  (1 shorter events, 0.0 us)
Async XLA Ops:
  0.0 50.7 %copy-start.6 = (s32[12]{0:T(128)S(1)}, s32[12]{0:T(128)}, u32[]{:S(2)}) copy-start(s32[12]{0:T(128)} %quadrant.1) | copy-start | bytes 148
  0.0 50.7 %copy-start.5 = (f32[12]{0:T(128)S(1)}, f32[12]{0:T(128)}, u32[]{:S(2)}) copy-start(f32[12]{0:T(128)} %cross_gain.1) | copy-start | bytes 148
  0.0 50.7 %copy-start.7 = (f32[32]{0:T(128)S(1)}, f32[32]{0:T(128)}, u32[]{:S(2)}) copy-start(f32[32]{0:T(128)} %coef.1) | copy-start | bytes 388
  2.2 1.1 %copy-start = (f32[12,128,128]{2,1,0:T(8,128)S(1)}, f32[12,128,128]{2,1,0:T(8,128)}, u32[]{:S(2)}) copy-start(f32[12,128,128]{2,1,0:T(8,128)} %inverse.3) | copy-start | bytes 2359300
  3.4 0.9 %copy-start.2 = (f32[12,8,512]{2,1,0:T(8,128)S(1)}, f32[12,8,512]{2,1,0:T(8,128)}, u32[]{:S(2)}) copy-start(f32[12,8,512]{2,1,0:T(8,128)} %coupling.3) | copy-start | bytes 589828
  4.3 1.1 %copy-start.3 = (f32[12,32,512]{2,1,0:T(8,128)S(1)}, f32[12,32,512]{2,1,0:T(8,128)}, u32[]{:S(2)}) copy-start(f32[12,32,512]{2,1,0:T(8,128)} %param.10) | copy-start | bytes 2359300
  5.4 0.7 %copy-start.4 = (s32[8,512]{1,0:T(8,128)S(1)}, s32[8,512]{1,0:T(8,128)}, u32[]{:S(2)}) copy-start(s32[8,512]{1,0:T(8,128)} %sea_mask.3) | copy-start | bytes 49156
  6.2 44.5 %copy-start.1 = (f32[12,128,128]{2,1,0:T(8,128)S(1)}, f32[12,128,128]{2,1,0:T(8,128)}, u32[]{:S(2)}) copy-start(f32[12,128,128]{2,1,0:T(8,128)} %inverse.3) | copy-start | bytes 2359300
where the time goes:
time: 71 us; the launch traced here: 70.5 us
  Pallas kernels  64.3 us (91%)
  local copies, waits for them, and re-layouts  4.67 us (7%)
  other arithmetic  1.47 us (2%)
    pallas_call x1, Pallas kernels, scan_devices(): pl.pallas_call(functools.partial(scan_kernel, count, dir_count, chunks),...  44.5 us
    pallas_call x1, Pallas kernels, add_step(): pl.pallas_call(functools.partial(step_kernel, dirs), grid=(dirs + 2 * SHI...  19.8 us
    unnamed x17, local copies, waits for them, and re-layouts  4.67 us

commit v1 on v0

v1 whole, which is shorter than its diff:
```python
import functools

import jax
import jax.numpy as jnp
from jax import lax
from jax.experimental import pallas as pl
from jax.experimental.pallas import tpu as pltpu
from jax.sharding import PartitionSpec as P

SHIFT = 2
f32 = jnp.float32
bf16 = jnp.bfloat16
MESH = pl.DeviceIdType.MESH
SCAN_VMEM = 56 * 1024 * 1024
STEP_VMEM = 32 * 1024 * 1024
BLOCK = 128


def cost(microseconds):
    return pl.CostEstimate(
        flops=0, bytes_accessed=int(microseconds * 3_000_000), transcendentals=0
    )


def weights(coupling, sea):
    return coupling * sea, sea * (1.0 - coupling)


def visit_order(shape, backward):
    row = lax.broadcasted_iota(jnp.int32, shape, 0)
    return shape[0] - 1 - row if backward else row


def rolled(x, steps, backward):
    rows = x.shape[0]
    return pltpu.roll(x, (rows - steps if backward else steps) % rows, 0)


def row_weights(coupling, sea, backward):
    couple, weight = weights(coupling, sea)
    rows = couple.shape[0]
    order = visit_order(couple.shape, backward)
    after = jnp.where(order < rows - 1, rolled(couple, rows - 1, backward), 1.0)
    span = 1
    while span < rows - 1:
        after = after * jnp.where(order < rows - span, rolled(after, rows - span, backward), 1.0)
        span *= 2
    gain = jnp.sum(jnp.where(order == 0, couple * after, 0.0), axis=0, keepdims=True)
    return weight * after, gain


def scan_kernel(
    count, dir_count, chunks, quadrant, cross_gain, boundary_in, sea_in, previous_in, coupling_in,
    out, edges, halo_previous, halo_coupling, halo_marks,
    gain, state, shares, marks, boundary, sea_mask, previous, coupling,
    gains, got_core, half_total, got_pair, plane, chain_in, chain_out, pair_in, pair_out, core_out,
    load_sem, gain_send, gain_recv, core_send, core_recv, pair_send, pair_recv,
    chain_send, chain_recv, back_send, back_recv, last_send, last_recv, halo_send, halo_recv,
):
    me = lax.axis_index("rows")
    c, x, z = me % 2, (me // 2) % 2, me // 4
    depth = count // 4
    core_peer = me + 1 - 2 * c
    pair_peer = me + 2 - 4 * x
    cross_peer = core_peer + 2 - 4 * x
    dirs = gain.shape[0]
    size = dirs // chunks
    peers = (core_peer, pair_peer, cross_peer)

    def part(j):
        return pl.ds(j * size, size)

    barrier = pltpu.get_barrier_semaphore()
    for peer in peers:
        pl.semaphore_signal(barrier, inc=1, device_id={"rows": peer}, device_id_type=MESH)

    @pl.when(z > 0)
    def _():
        pl.semaphore_signal(barrier, inc=1, device_id={"rows": me - 4}, device_id_type=MESH)

    @pl.when(z < depth - 1)
    def _():
        pl.semaphore_signal(barrier, inc=1, device_id={"rows": me + 4}, device_id_type=MESH)

    mine = lax.axis_index("dirs")
    higher, lower = (mine + 1) % dir_count, (mine + dir_count - 1) % dir_count
    neighbours = (higher, lower) if dir_count > 2 else (higher,)
    for peer in neighbours:
        pl.semaphore_signal(barrier, inc=1, device_id={"dirs": peer}, device_id_type=MESH)

    order = [0] + list(range(chunks - 1, 0, -1))
    coupling_load = pltpu.make_async_copy(coupling_in, coupling, load_sem.at[0])
    sea_load = pltpu.make_async_copy(sea_in, sea_mask, load_sem.at[1])
    boundary_load = pltpu.make_async_copy(boundary_in, boundary, load_sem.at[2])
    previous_loads = [
        pltpu.make_async_copy(previous_in.at[part(j)], previous.at[part(j)], load_sem.at[3 + j])
        for j in range(chunks)
    ]
    sea_load.start()
    coupling_load.start()
    for j in order:
        previous_loads[j].start()
    boundary_load.start()
    for d in range(dirs):
        marks[d, 0:1] = jnp.full((1, marks.shape[2]), cross_gain[d], f32)
        marks[d, 1:2] = jnp.full((1, marks.shape[2]), quadrant[d].astype(f32), f32)
    pl.semaphore_wait(
        barrier, 3 + len(neighbours) + (z > 0).astype(jnp.int32) + (z < depth - 1).astype(jnp.int32)
    )

    def remote(src, dst, send, recv, peer):
        return pltpu.make_async_remote_copy(
            src_ref=src, dst_ref=dst, send_sem=send, recv_sem=recv,
            device_id={"rows": peer}, device_id_type=MESH,
        )

    gain_copies = [
        remote(gain, gains.at[i], gain_send.at[i], gain_recv.at[i], peer) for i, peer in enumerate(peers)
    ]
    core_copies = [
        remote(state.at[1 - c, :, part(j)], got_core.at[:, part(j)], core_send.at[j], core_recv.at[j], core_peer)
        for j in range(chunks)
    ]
    pair_copies = [
        remote(half_total.at[1 - x, part(j)], got_pair.at[part(j)], pair_send.at[j], pair_recv.at[j], pair_peer)
        for j in range(chunks)
    ]
    back_copies = [
        remote(pair_out.at[part(j)], pair_in.at[x, part(j)], back_send.at[j], back_recv.at[j], pair_peer)
        for j in range(chunks)
    ]
    last_copies = [
        remote(core_out.at[:, part(j)], out.at[c, :, part(j)], last_send.at[j], last_recv.at[j], core_peer)
        for j in range(chunks)
    ]

    halo_copies = []
    for way, (peer, start, to) in enumerate(((lower, 0, SHIFT), (higher, dirs - SHIFT, 0))):
        for i, (array, halo) in enumerate(
            ((previous_in, halo_previous), (coupling_in, halo_coupling), (marks, halo_marks))
        ):
            halo_copies.append(
                pltpu.make_async_remote_copy(
                    src_ref=array.at[pl.ds(start, SHIFT)], dst_ref=halo.at[pl.ds(to, SHIFT)],
                    send_sem=halo_send.at[way, i], recv_sem=halo_recv.at[way, i],
                    device_id={"dirs": peer}, device_id_type=MESH,
                )
            )
            halo_copies[-1].start()

    flags = marks[:, 1:2, :]
    flags = flags - 2.0 * jnp.floor(0.5 * flags)
    back = jnp.concatenate([flags] * (gain.shape[-1] // flags.shape[-1]), axis=2)
    sea_load.wait()
    coupling_load.wait()
    sea = sea_mask[...].astype(f32)
    for d in range(dirs):
        onward, onward_gain = row_weights(coupling[d], sea, False)
        against, _ = row_weights(coupling[d], sea, True)
        shares[d] = jnp.where(back[d] > 0.5, against, onward)
        gain[d] = onward_gain
    for copy in gain_copies:
        copy.start()

    def compose(h, d, _):
        share = shares[d]
        for q in range(2):
            values = previous[d, pl.ds((2 * h + q) * state.shape[3], state.shape[3])].astype(f32)
            state[h, q, d] = jnp.sum(values * share[None], axis=1)
        return 0

    for j in order:
        previous_loads[j].wait()
        lax.fori_loop(j * size, (j + 1) * size, functools.partial(compose, 1 - c), 0)
        core_copies[j].start()
    for j in order:
        lax.fori_loop(j * size, (j + 1) * size, functools.partial(compose, c), 0)
    boundary_load.wait()
    c_bit, x_bit = c.astype(f32), x.astype(f32)
    core_after = c_bit + back - 2.0 * c_bit * back
    pair_after = x_bit + back - 2.0 * x_bit * back
    for copy in gain_copies:
        copy.wait_recv()
    core_mine, core_theirs = gain[...], gains[0]
    pair_mine, pair_theirs = core_mine * core_theirs, gains[1] * gains[2]
    plane_gain = pair_mine * pair_theirs

    def total(after, mine, theirs):
        return after * mine + (1.0 - after), (1.0 - after) * theirs + after

    core_a, core_b = total(core_after, core_mine, core_theirs)
    pair_a, pair_b = total(pair_after, pair_mine, pair_theirs)

    def cut(v, j):
        return v[j * size : (j + 1) * size]

    for j in order:
        core_copies[j].wait_recv()
        half_total[:, part(j)] = (
            cut(core_a, j)[None] * got_core[:, part(j)] + cut(core_b, j)[None] * state[c, :, part(j)]
        )
        pair_copies[j].start()
    for j in order:
        pair_copies[j].wait_recv()
        plane[part(j)] = cut(pair_a, j) * got_pair[part(j)] + cut(pair_b, j) * half_total[x, part(j)]

    upper = (2 * z >= depth).astype(jnp.int32)
    mine_at = 2 * c + x

    def chain(j, way):
        step = 1 - 2 * way
        has_before = jnp.where(way == 0, z > 0, z < depth - 1)
        has_after = jnp.where(way == 0, z < depth - 1, z > 0)
        copy = remote(
            chain_out.at[way, part(j)], chain_in.at[way, part(j)],
            chain_send.at[way, j], chain_recv.at[way, j], me + 4 * step,
        )

        @pl.when(has_before)
        def _():
            copy.wait_recv()

        @pl.when(jnp.logical_not(has_before))
        def _():
            chain_in[way, part(j)] = boundary[part(j), mine_at]

        @pl.when(has_after)
        def _():
            chain_out[way, part(j)] = cut(plane_gain, j) * chain_in[way, part(j)] + plane[part(j)]
            copy.start()

    def split(after, mine, theirs):
        return after * theirs + (1.0 - after), (1.0 - after) * mine + after

    pair_p, pair_q = split(pair_after, pair_mine, pair_theirs)
    core_p, core_q = split(core_after, core_mine, core_theirs)
    for j in order:
        chain(j, upper)
    for j in order:
        chain(j, 1 - upper)
        entering = jnp.where(cut(back, j) > 0.5, chain_in[1, part(j)], chain_in[0, part(j)])
        pair_out[part(j)] = cut(pair_q, j) * entering + (1.0 - cut(pair_after, j)) * half_total[x, part(j)]
        back_copies[j].start()
        pair_in[x, part(j)] = cut(pair_p, j) * entering + cut(pair_after, j) * got_pair[part(j)]
    for j in order:
        back_copies[j].wait_recv()
        entering = pair_in[:, part(j)]
        core_out[:, part(j)] = (
            cut(core_q, j)[None] * entering + (1.0 - cut(core_after, j))[None] * state[c, :, part(j)]
        )
        last_copies[j].start()
        out[c, :, part(j)] = cut(core_p, j)[None] * entering + cut(core_after, j)[None] * got_core[:, part(j)]
    for j in order:
        last_copies[j].wait_recv()
    edges[0] = out[:, :, 0:SHIFT]
    edges[1] = out[:, :, dirs - SHIFT : dirs]
    for copy in halo_copies:
        copy.wait_recv()
    for copy in halo_copies + gain_copies + core_copies + pair_copies + back_copies + last_copies:
        copy.wait_send()

    def drain(j, way):
        copy = remote(
            chain_out.at[way, part(j)], chain_in.at[way, part(j)],
            chain_send.at[way, j], chain_recv.at[way, j], me + 4 * (1 - 2 * way),
        )

        @pl.when(z < depth - 1 if way == 0 else z > 0)
        def _():
            copy.wait_send()

    for j in range(chunks):
        drain(j, 0)
        drain(j, 1)


def scan_devices(count, dir_count, quadrant, cross_gain, boundary, sea_mask, previous, coupling):
    dirs, bands, rows, columns = previous.shape
    chunks = 4 if dirs % 4 == 0 else 3 if dirs % 3 == 0 else 1
    quarter = bands // 4
    boundary = boundary.reshape(dirs, 4, quarter, columns)
    vmem = pl.BlockSpec(memory_space=pltpu.VMEM)
    smem = pl.BlockSpec(memory_space=pltpu.SMEM)
    part = (dirs, quarter, columns)
    dma = pltpu.SemaphoreType.DMA
    anywhere = pl.BlockSpec(memory_space=pl.ANY)
    marks = (dirs, 2, 128)

    def halo(a):
        return jax.ShapeDtypeStruct((2 * SHIFT,) + a.shape[1:], a.dtype)

    out, edges, *halos = pl.pallas_call(
        functools.partial(scan_kernel, count, dir_count, chunks),
        in_specs=[smem, smem] + [anywhere] * 4,
        out_specs=[vmem, vmem] + [anywhere] * 3,
        out_shape=[
            jax.ShapeDtypeStruct((2, 2) + part, f32),
            jax.ShapeDtypeStruct((2, 2, 2, SHIFT, quarter, columns), f32),
            halo(previous),
            halo(coupling),
            jax.ShapeDtypeStruct((2 * SHIFT,) + marks[1:], f32),
        ],
        scratch_shapes=[
            pltpu.VMEM((dirs, 1, columns), f32),
            pltpu.VMEM((2, 2) + part, f32),
            pltpu.VMEM(coupling.shape, f32),
            pltpu.VMEM(marks, f32),
            pltpu.VMEM(boundary.shape, f32),
            pltpu.VMEM(sea_mask.shape, jnp.int32),
            pltpu.VMEM(previous.shape, bf16),
            pltpu.VMEM(coupling.shape, f32),
            pltpu.VMEM((3, dirs, 1, columns), f32),
            pltpu.VMEM((2,) + part, f32),
            pltpu.VMEM((2,) + part, f32),
            pltpu.VMEM(part, f32),
            pltpu.VMEM(part, f32),
            pltpu.VMEM((2,) + part, f32),
            pltpu.VMEM((2,) + part, f32),
            pltpu.VMEM((2,) + part, f32),
            pltpu.VMEM(part, f32),
            pltpu.VMEM((2,) + part, f32),
            dma((3 + chunks,)),
            dma((3,)), dma((3,)),
            dma((chunks,)), dma((chunks,)),
            dma((chunks,)), dma((chunks,)),
            dma((2, chunks)), dma((2, chunks)),
            dma((chunks,)), dma((chunks,)),
            dma((chunks,)), dma((chunks,)),
            dma((2, 3)), dma((2, 3)),
        ],
        compiler_params=pltpu.CompilerParams(
            collective_id=0, has_side_effects=True, vmem_limit_bytes=SCAN_VMEM
        ),
        cost_estimate=cost(30),
        name="scan_devices",
    )(quadrant, cross_gain, boundary, sea_mask, previous, coupling)
    return out.reshape(4, dirs, quarter, columns), edges, halos


def sweep(previous, coupling, inflow_of, swept, sea, backward):
    bands = previous.shape[0]
    quarter = bands // 4
    couple, weight = weights(coupling, sea)
    rows = couple.shape[0]
    order = visit_order(couple.shape, backward)
    first = jnp.where(order == 0, couple, 0.0)
    spans, reach, span = [], couple, 1
    while span < rows:
        spans.append((span, jnp.where(order >= span, reach, 0.0)))
        reach = jnp.where(order >= span, reach * rolled(reach, span, backward), reach)
        span *= 2

    def group(q, _):
        inflow = inflow_of(q)
        for r in range(quarter):
            value = weight * previous[q * quarter + r].astype(f32) + first * inflow[r : r + 1]
            for span, factor in spans:
                value = value + factor * rolled(value, span, backward)
            swept[q * quarter + r] = value
        return 0

    lax.fori_loop(0, 4, group, 0)


def columns_solve(gain, sea, swept, rounded, settled, sideways):
    bands, rows, columns = swept.shape
    block = BLOCK
    pieces = columns // block
    gains = jnp.full((1, block), gain, f32)
    slope, scale = jnp.log(gains / (1.0 + gains)), 1.0 / (1.0 + gains)
    row = lax.broadcasted_iota(jnp.int32, (block, block), 0)
    column = lax.broadcasted_iota(jnp.int32, (block, block), 1)
    offset = row - column if sideways else column - row
    matrix = jnp.where(offset >= 0, jnp.exp(offset.astype(f32) * slope) * scale, 0.0)
    carry = gains * (matrix[block - 1 :] if sideways else matrix[:1])
    high = matrix.astype(bf16)
    low = (matrix - high.astype(f32)).astype(bf16)
    whole = jnp.concatenate(
        [
            jnp.concatenate([high, low], axis=1),
            jnp.concatenate([high, jnp.zeros_like(low)], axis=1),
        ],
        axis=0,
    )
    before = None
    for k in range(pieces - 1, -1, -1) if sideways else range(pieces):
        here = slice(k * block, (k + 1) * block)
        x = swept[:, :, here].reshape(bands * rows, block)
        upper = x.astype(bf16)
        lower = (x - upper.astype(f32)).astype(bf16)
        both = jnp.dot(
            jnp.concatenate([upper, lower], axis=1), whole, preferred_element_type=f32
        )
        y = both[:, :block] + both[:, block:]
        if before is not None:
            y = y + (before[:, :1] if sideways else before[:, block - 1 :]) * carry
        before = y
        masked = y.reshape(bands, rows, block) * sea[:, here][None]
        rounded[:, :, here] = masked.astype(bf16)
        if settled is not None:
            settled[:, :, here] = masked


def settle(previous, coupling, inflow_of, corner, gain, sea, swept, rounded, settled):
    for flag in (0, 1):
        pl.when(corner % 2 == flag)(
            functools.partial(sweep, previous, coupling, inflow_of, swept, sea, flag == 1)
        )
    for flag in (0, 1):
        pl.when(corner // 2 == flag)(
            functools.partial(columns_solve, gain, sea, swept, rounded, settled, flag == 1)
        )


def own_kernel(
    quadrant, cross_gain, sea_mask, previous_in, coupling, entering, rounded, settled,
    previous, swept, sea, load_sem,
):
    dirs = previous.shape[0]
    loads = [
        pltpu.make_async_copy(previous_in.at[d], previous.at[d], load_sem.at[d]) for d in range(dirs)
    ]
    for load in loads:
        load.start()
    sea[...] = sea_mask[...].astype(f32)
    for load in loads:
        load.wait()

    def one(d, _):
        settle(
            previous.at[d], coupling[d], lambda q: entering[q, d], quadrant[d], cross_gain[d], sea[...],
            swept, rounded.at[d], settled.at[d],
        )
        return 0

    lax.fori_loop(0, dirs, one, 0)


def settle_own(quadrant, cross_gain, sea_mask, previous, coupling, entering):
    dirs, bands, rows, columns = previous.shape
    vmem = pl.BlockSpec(memory_space=pltpu.VMEM)
    smem = pl.BlockSpec(memory_space=pltpu.SMEM)
    anywhere = pl.BlockSpec(memory_space=pl.ANY)
    return pl.pallas_call(
        own_kernel,
        in_specs=[smem, smem, vmem, anywhere, vmem, vmem],
        out_specs=[vmem, vmem],
        out_shape=[
            jax.ShapeDtypeStruct(previous.shape, bf16),
            jax.ShapeDtypeStruct(previous.shape, f32),
        ],
        scratch_shapes=[
            pltpu.VMEM(previous.shape, bf16),
            pltpu.VMEM((bands, rows, columns), f32),
            pltpu.VMEM((rows, columns), f32),
            pltpu.SemaphoreType.DMA((dirs,)),
        ],
        compiler_params=pltpu.CompilerParams(vmem_limit_bytes=STEP_VMEM),
        cost_estimate=cost(12),
        name="settle_own",
    )(quadrant, cross_gain, sea_mask, previous, coupling, entering)


def source_kernel(
    halo_marks, coef, sea_mask, wet_tiles, halo_previous, halo_coupling, incoming, own, settled,
    out, halo, swept, sea, wet, result, store_sem,
):
    dirs, bands, rows, columns = settled.shape
    pieces = columns // BLOCK
    sea[...] = sea_mask[...].astype(f32)
    for k in range(pieces):
        flag = wet_tiles[:, k : k + 1].astype(f32)
        wet[:, k * BLOCK : (k + 1) * BLOCK] = jnp.broadcast_to(flag, (rows, BLOCK))
    stores = [pltpu.make_async_copy(result.at[d], out.at[d], store_sem.at[d]) for d in range(dirs)]

    def source(d):
        wet_cells = wet[...]
        onward_of = own.at[d + SHIFT] if d + SHIFT < dirs else halo.at[2 * SHIFT + d - dirs]
        against_of = own.at[d - SHIFT] if d >= SHIFT else halo.at[d]

        def one(f, onward, against):
            energy = own[d, f].astype(f32)
            value = coef[f] * (
                energy * energy * (onward + against) - 2.0 * energy * onward * against
            )
            result[d, f] = (settled[d, f] + wet_cells * value.astype(bf16).astype(f32)).astype(bf16)

        def above(f):
            return onward_of[f + 1].astype(f32)

        def below(f):
            return against_of[f - 1].astype(f32)

        nothing = jnp.zeros(wet.shape, f32)
        one(0, above(0), nothing)
        one(bands - 1, nothing, below(bands - 1))

        def body(f, _):
            one(f, above(f), below(f))
            return 0

        lax.fori_loop(1, bands - 1, body, 0, unroll=6 if (bands - 2) % 6 == 0 else 1)
        stores[d].start()

    inner = [d for d in range(dirs) if SHIFT <= d < dirs - SHIFT]
    for d in inner:
        source(d)

    def one_halo(t, _):
        way, at = 1 - t // SHIFT, t % SHIFT
        settle(
            halo_previous.at[t], halo_coupling[t], lambda q: incoming[way, q, at],
            halo_marks[t, 1, 0].astype(jnp.int32), halo_marks[t, 0, 0], sea[...],
            swept, halo.at[t], None,
        )
        return 0

    lax.fori_loop(0, 2 * SHIFT, one_halo, 0)
    for d in range(dirs):
        if d not in inner:
            source(d)
    for store in stores:
        store.wait()


def add_source(
    halo_marks, quad_coef, sea_mask, wet_tiles, halo_previous, halo_coupling, incoming, rounded, settled
):
    dirs, bands, rows, columns = settled.shape
    vmem = pl.BlockSpec(memory_space=pltpu.VMEM)
    smem = pl.BlockSpec(memory_space=pltpu.SMEM)
    return pl.pallas_call(
        source_kernel,
        in_specs=[smem, smem] + [vmem] * 7,
        out_specs=pl.BlockSpec(memory_space=pl.ANY),
        out_shape=jax.ShapeDtypeStruct(settled.shape, bf16),
        scratch_shapes=[
            pltpu.VMEM((2 * SHIFT, bands, rows, columns), bf16),
            pltpu.VMEM((bands, rows, columns), f32),
            pltpu.VMEM((rows, columns), f32),
            pltpu.VMEM((rows, columns), f32),
            pltpu.VMEM(settled.shape, bf16),
            pltpu.SemaphoreType.DMA((dirs,)),
        ],
        compiler_params=pltpu.CompilerParams(vmem_limit_bytes=STEP_VMEM),
        cost_estimate=cost(8),
        name="add_source",
    )(halo_marks, quad_coef, sea_mask, wet_tiles, halo_previous, halo_coupling, incoming, rounded, settled)


def exchange(edges, dir_count):
    if dir_count == 2:
        return lax.ppermute(edges, "dirs", [(0, 1), (1, 0)])
    down = [(i, (i - 1) % dir_count) for i in range(dir_count)]
    up = [(i, (i + 1) % dir_count) for i in range(dir_count)]
    return jnp.stack([lax.ppermute(edges[0], "dirs", down), lax.ppermute(edges[1], "dirs", up)])


def on_device(
    row_devices, dir_devices,
    previous, boundary, row_coupling, cross_gain, block_inverse, quadrant, sea_mask, wet_tiles, quad_coef,
):
    entering, edges, (halo_previous, halo_coupling, halo_marks) = scan_devices(
        row_devices, dir_devices, quadrant, cross_gain, boundary, sea_mask, previous, row_coupling
    )
    incoming = exchange(edges, dir_devices)
    incoming = incoming.reshape((2, 4) + incoming.shape[3:])
    rounded, settled = settle_own(quadrant, cross_gain, sea_mask, previous, row_coupling, entering)
    return add_source(
        halo_marks, quad_coef, sea_mask, wet_tiles, halo_previous, halo_coupling, incoming, rounded, settled
    )


def solution(mesh):
    in_specs = (
        P("dirs", None, "rows", None),
        P("dirs", None, None),
        P("dirs", "rows", None),
        P("dirs"),
        P("dirs", None, None),
        P("dirs"),
        P("rows", None),
        P("rows", None),
        P(),
    )
    out_specs = P("dirs", None, "rows", None)
    return jax.shard_map(
        functools.partial(on_device, mesh.shape["rows"], mesh.shape["dirs"]),
        mesh=mesh, in_specs=in_specs, out_specs=out_specs, check_vma=False,
    )
```

time: 71 us -> 55.7 us (0.78)
  Pallas kernels: 64.3 us -> 52.9 us
  local copies, waits for them, and re-layouts: 4.67 us -> 1.33 us
  other arithmetic: 1.47 us -> 0 us
  starting transfers between devices: 0 us -> 1.17 us
    pallas_call x1, Pallas kernels: 44.5 us -> 34.3 us  [scan_devices(): pl.pallas_call(functools.partial(scan_kernel, count, dir_count, chunks),...]
    unnamed x17 -> x23, local copies, waits for them, and re-layouts: 4.67 us -> 1.33 us
    ppermute x0 -> x1, starting transfers between devices: none -> 1.17 us  [exchange(): return lax.ppermute(edges, 'dirs', [(0, 1), (1, 0)])]
    pallas_call x1 -> x2, Pallas kernels: 19.8 us -> 18.7 us  [the longest x1 10.1 us: settle_own(): pl.pallas_call(own_kernel, in_specs=[smem, smem, vmem, anywhere, vmem, vm...]
    select_n x1 -> x0, other arithmetic: 0.74 us -> none  [on_device(): jnp.where(which == 0, cross_gain[:, None, None], quadrant.astype(f32)[:,...]
    convert_element_type x1 -> x0, other arithmetic: 0.72 us -> none  [on_device(): quadrant.astype(f32)[:, None, None]]
  transfers between devices with their start and end apart: 0 -> 1, of which waited for: 0 -> 0; matrix products, arithmetic and copies ran while one was open for 0% -> 0% of each run, Pallas kernels for 0% -> 18%
where the time goes in v1:
time: 55.7 us; the launch traced here: 55.6 us
  Pallas kernels  52.9 us (95%)
  local copies, waits for them, and re-layouts  1.33 us (2%)
  starting transfers between devices  1.17 us (2%)
    pallas_call x1, Pallas kernels, scan_devices(): pl.pallas_call(functools.partial(scan_kernel, count, dir_count, chunks),...  34.3 us
    pallas_call x1, Pallas kernels, settle_own(): pl.pallas_call(own_kernel, in_specs=[smem, smem, vmem, anywhere, vmem, vm...  10.1 us
    pallas_call x1, Pallas kernels, add_source(): pl.pallas_call(source_kernel, in_specs=[smem, smem] + [vmem] * 7, out_spe...  8.61 us
    unnamed x23, local copies, waits for them, and re-layouts  1.33 us
    ppermute x1, starting transfers between devices, exchange(): return lax.ppermute(edges, 'dirs', [(0, 1), (1, 0)])  1.17 us
  transfers between devices with their start and end apart: 1, of which 0 were waited for; matrix products, arithmetic and copies ran while one was open for 0% of the time, Pallas kernels for 18%

profile of v1, /device:TPU:0, one launch (start us, length us, event | category | flops | bytes accessed | tf_op | source)
XLA Modules:
  0.0 55.6 jit_solution(14936745964669184282)
XLA Ops:
  0.0 0.0 copy-start.4
  0.0 0.0 copy-start.7
  0.0 0.0 copy-start.8
  0.0 0.0 copy-start.2
  0.0 0.0 copy-start
  0.0 0.0 copy-start.10
  0.0 0.0 copy-start.9
  0.0 34.3 %scan_devices.1 = (f32[2,2,12,8,512]{4,3,2,1,0:T(8,128)}, f32[2,2,2,2,8,512]{5,4,3,2,1,0:T(8,128)}, bf16[4,32,8,512]{3,2,1,0:T(8,128)(2,1)}, f32[4,8,512]{2,1,0:T(8,128)}, f32[4,2,128]{2,1,0:T(2,128)}) custom-call(s32[12]{0:T(128)} %quadrant.3, f32[12]{0:T(128)} %cross_gain.3, f32[12,4,8,512]{3,2,1,0:T(8,128)} %bitcast.4, s32[8,512]{1,0:T(8,128)} %sea_mask.3, ...), custom_call_target="tpu_custom_call" | custom-call | bytes 90000000 | tf_op jit(solution)/shard_map/scan_devices/pallas_call | solution.py:292
  34.3 0.0 copy-start.6
  34.3 1.2 %collective-permute-start = (f32[2,2,2,2,8,512]{5,4,3,2,1,0:T(8,128)}, f32[2,2,2,2,8,512]{5,4,3,2,1,0:T(8,128)}, u32[]{:S(2)}, u32[]{:S(2)}) collective-permute-start(f32[2,2,2,2,8,512]{5,4,3,2,1,0:T(8,128)} %get-tuple-element.15), channel_id=1, source_target_pairs={{0,1},{1,0},{2,3},{3,2},{4,5},{5,4},{6,7},{7,6},{8,9},{9,8},{10,11... | collective-permute-start | bytes 786440 | tf_op jit(solution)/shard_map/ppermute | solution.py:553
  35.5 0.0 copy-done.10
  35.5 0.1 copy.9.wet_tiles
  35.6 0.0 copy-start.1
  35.6 0.0 copy-done.4
  35.6 0.0 copy-done.7
  35.6 0.0 copy-done.8
  35.6 0.0 copy-done.2
  35.6 0.0 copy-done
  35.6 0.0 copy-start.3
  35.6 1.2 %copy-done.3 = f32[2,2,12,8,512]{4,3,2,1,0:T(8,128)S(1)} copy-done((f32[2,2,12,8,512]{4,3,2,1,0:T(8,128)S(1)}, f32[2,2,12,8,512]{4,3,2,1,0:T(8,128)}, u32[]{:S(2)}) %copy-start.3) | copy-done | bytes 786456
  36.8 0.0 copy-start.5
  36.8 10.1 %settle_own.1 = (bf16[12,32,8,512]{3,2,1,0:T(8,128)(2,1)S(1)}, f32[12,32,8,512]{3,2,1,0:T(8,128)S(1)}) custom-call(s32[12]{0:T(128)S(1)} %copy-done.7, f32[12]{0:T(128)S(1)} %copy-done.8, s32[8,512]{1,0:T(8,128)S(1)} %copy-done.4, bf16[12,32,8,512]{3,2,1,0:T(8,128)(2,1)S(1)} %copy-done, f32[12,8,512]{2,1,0:T(8,128)S(1)} %copy-done.2, ...), custom_call_target="tpu_custom_call" | custom-call | bytes 36000000 | tf_op jit(solution)/shard_map/settle_own/pallas_call | solution.py:444
  46.9 0.0 collective-permute-done
  46.9 0.0 copy-done.9
  46.9 0.0 copy-done.6
  46.9 0.0 copy-done.1
  46.9 0.0 copy-done.5
  46.9 8.6 %add_source.1 = bf16[12,32,8,512]{3,2,1,0:T(8,128)(2,1)} custom-call(f32[4,2,128]{2,1,0:T(2,128)S(1)} %copy-done.6, f32[32]{0:T(128)S(1)} %copy-done.9, s32[8,512]{1,0:T(8,128)S(1)} %copy-done.4, s32[8,4]{1,0:T(8,128)S(1)} %copy.9.wet_tiles, bf16[4,32,8,512]{3,2,1,0:T(8,128)(2,1)S(1)} %copy-done.1, f32[4,8,512]{2,1,0:T(8,128)S(1)} %copy-done.5, ...), custom_call_target="tpu_custom_call" | custom-call | bytes 24000000 | tf_op jit(solution)/shard_map/add_source/pallas_call | solution.py:532
Async XLA Ops:
  0.0 35.6 %copy-start.4 = (s32[8,512]{1,0:T(8,128)S(1)}, s32[8,512]{1,0:T(8,128)}, u32[]{:S(2)}) copy-start(s32[8,512]{1,0:T(8,128)} %sea_mask.3) | copy-start | bytes 49156
  0.0 35.6 %copy-start.7 = (s32[12]{0:T(128)S(1)}, s32[12]{0:T(128)}, u32[]{:S(2)}) copy-start(s32[12]{0:T(128)} %quadrant.3) | copy-start | bytes 148
  0.0 35.6 %copy-start.8 = (f32[12]{0:T(128)S(1)}, f32[12]{0:T(128)}, u32[]{:S(2)}) copy-start(f32[12]{0:T(128)} %cross_gain.3) | copy-start | bytes 148
  0.0 35.6 %copy-start.2 = (f32[12,8,512]{2,1,0:T(8,128)S(1)}, f32[12,8,512]{2,1,0:T(8,128)}, u32[]{:S(2)}) copy-start(f32[12,8,512]{2,1,0:T(8,128)} %coupling.1) | copy-start | bytes 589828
  0.0 35.6 %copy-start = (bf16[12,32,8,512]{3,2,1,0:T(8,128)(2,1)S(1)}, bf16[12,32,8,512]{3,2,1,0:T(8,128)(2,1)}, u32[]{:S(2)}) copy-start(bf16[12,32,8,512]{3,2,1,0:T(8,128)(2,1)} %previous_in.3) | copy-start | bytes 9437188
  0.0 35.5 %copy-start.10 = (s32[8,4]{0,1:T(4,128)S(1)}, s32[8,4]{0,1:T(4,128)}, u32[]{:S(2)}) copy-start(s32[8,4]{0,1:T(4,128)} %param.15) | copy-start | bytes 388
  0.0 46.9 %copy-start.9 = (f32[32]{0:T(128)S(1)}, f32[32]{0:T(128)}, u32[]{:S(2)}) copy-start(f32[32]{0:T(128)} %coef.1) | copy-start | bytes 388
  34.3 12.6 %copy-start.6 = (f32[4,2,128]{2,1,0:T(2,128)S(1)}, f32[4,2,128]{2,1,0:T(2,128)}, u32[]{:S(2)}) copy-start(f32[4,2,128]{2,1,0:T(2,128)} %get-tuple-element.12.halo_marks) | copy-start | bytes 12292
  34.3 12.6 %collective-permute-start = (f32[2,2,2,2,8,512]{5,4,3,2,1,0:T(8,128)}, f32[2,2,2,2,8,512]{5,4,3,2,1,0:T(8,128)}, u32[]{:S(2)}, u32[]{:S(2)}) collective-permute-start(f32[2,2,2,2,8,512]{5,4,3,2,1,0:T(8,128)} %get-tuple-element.15), channel_id=1, source_target_pairs={{0,1},{1,0},{2,3},{3,2},{4,5},{5,4},{6,7},{7,6},{8,9},{9,8},{10,11... | collective-permute-start | bytes 786440 | tf_op jit(solution)/shard_map/ppermute | solution.py:553
  35.6 11.4 %copy-start.1 = (bf16[4,32,8,512]{3,2,1,0:T(8,128)(2,1)S(1)}, bf16[4,32,8,512]{3,2,1,0:T(8,128)(2,1)}, u32[]{:S(2)}) copy-start(bf16[4,32,8,512]{3,2,1,0:T(8,128)(2,1)} %get-tuple-element.13.halo_previous) | copy-start | bytes 3145732
  35.6 1.2 %copy-start.3 = (f32[2,2,12,8,512]{4,3,2,1,0:T(8,128)S(1)}, f32[2,2,12,8,512]{4,3,2,1,0:T(8,128)}, u32[]{:S(2)}) copy-start(f32[2,2,12,8,512]{4,3,2,1,0:T(8,128)} %get-tuple-element.16) | copy-start | bytes 2359300
  36.8 10.1 %copy-start.5 = (f32[4,8,512]{2,1,0:T(8,128)S(1)}, f32[4,8,512]{2,1,0:T(8,128)}, u32[]{:S(2)}) copy-start(f32[4,8,512]{2,1,0:T(8,128)} %get-tuple-element.14.halo_coupling) | copy-start | bytes 196612

commit v2 on v1

--- a/solution.py
+++ b/solution.py
@@ -12,7 +12,7 @@
 bf16 = jnp.bfloat16
 MESH = pl.DeviceIdType.MESH
 SCAN_VMEM = 56 * 1024 * 1024
-STEP_VMEM = 32 * 1024 * 1024
+STEP_VMEM = 16 * 1024 * 1024
 BLOCK = 128
 
 
@@ -51,21 +51,23 @@
 
 def scan_kernel(
     count, dir_count, chunks, quadrant, cross_gain, boundary_in, sea_in, previous_in, coupling_in,
-    out, edges, halo_previous, halo_coupling, halo_marks,
+    entering_out, edges, halo_previous, halo_marks,
+    out,
     gain, state, shares, marks, boundary, sea_mask, previous, coupling,
     gains, got_core, half_total, got_pair, plane, chain_in, chain_out, pair_in, pair_out, core_out,
-    load_sem, gain_send, gain_recv, core_send, core_recv, pair_send, pair_recv,
+    load_sem, store_sem, gain_send, gain_recv, core_send, core_recv, pair_send, pair_recv,
     chain_send, chain_recv, back_send, back_recv, last_send, last_recv, halo_send, halo_recv,
 ):
     me = lax.axis_index("rows")
     c, x, z = me % 2, (me // 2) % 2, me // 4
     depth = count // 4
+    half = (c + x + z) % 2
     core_peer = me + 1 - 2 * c
-    pair_peer = me + 2 - 4 * x
-    cross_peer = core_peer + 2 - 4 * x
+    side_peer = me + 2 - 4 * x
+    pair_peer = core_peer + 2 - 4 * x
     dirs = gain.shape[0]
     size = dirs // chunks
-    peers = (core_peer, pair_peer, cross_peer)
+    peers = (core_peer, side_peer, pair_peer)
 
     def part(j):
         return pl.ds(j * size, size)
@@ -76,11 +78,11 @@
 
     @pl.when(z > 0)
     def _():
-        pl.semaphore_signal(barrier, inc=1, device_id={"rows": me - 4}, device_id_type=MESH)
+        pl.semaphore_signal(barrier, inc=1, device_id={"rows": core_peer - 4}, device_id_type=MESH)
 
     @pl.when(z < depth - 1)
     def _():
-        pl.semaphore_signal(barrier, inc=1, device_id={"rows": me + 4}, device_id_type=MESH)
+        pl.semaphore_signal(barrier, inc=1, device_id={"rows": core_peer + 4}, device_id_type=MESH)
 
     mine = lax.axis_index("dirs")
     higher, lower = (mine + 1) % dir_count, (mine + dir_count - 1) % dir_count
@@ -104,10 +106,6 @@
     for d in range(dirs):
         marks[d, 0:1] = jnp.full((1, marks.shape[2]), cross_gain[d], f32)
         marks[d, 1:2] = jnp.full((1, marks.shape[2]), quadrant[d].astype(f32), f32)
-    pl.semaphore_wait(
-        barrier, 3 + len(neighbours) + (z > 0).astype(jnp.int32) + (z < depth - 1).astype(jnp.int32)
-    )
-
     def remote(src, dst, send, recv, peer):
         return pltpu.make_async_remote_copy(
             src_ref=src, dst_ref=dst, send_sem=send, recv_sem=recv,
@@ -118,7 +116,7 @@
         remote(gain, gains.at[i], gain_send.at[i], gain_recv.at[i], peer) for i, peer in enumerate(peers)
     ]
     core_copies = [
-        remote(state.at[1 - c, :, part(j)], got_core.at[:, part(j)], core_send.at[j], core_recv.at[j], core_peer)
+        remote(state.at[1 - half, :, part(j)], got_core.at[:, part(j)], core_send.at[j], core_recv.at[j], core_peer)
         for j in range(chunks)
     ]
     pair_copies = [
@@ -130,23 +128,9 @@
         for j in range(chunks)
     ]
     last_copies = [
-        remote(core_out.at[:, part(j)], out.at[c, :, part(j)], last_send.at[j], last_recv.at[j], core_peer)
+        remote(core_out.at[:, part(j)], out.at[half, :, part(j)], last_send.at[j], last_recv.at[j], core_peer)
         for j in range(chunks)
     ]
-
-    halo_copies = []
-    for way, (peer, start, to) in enumerate(((lower, 0, SHIFT), (higher, dirs - SHIFT, 0))):
-        for i, (array, halo) in enumerate(
-            ((previous_in, halo_previous), (coupling_in, halo_coupling), (marks, halo_marks))
-        ):
-            halo_copies.append(
-                pltpu.make_async_remote_copy(
-                    src_ref=array.at[pl.ds(start, SHIFT)], dst_ref=halo.at[pl.ds(to, SHIFT)],
-                    send_sem=halo_send.at[way, i], recv_sem=halo_recv.at[way, i],
-                    device_id={"dirs": peer}, device_id_type=MESH,
-                )
-            )
-            halo_copies[-1].start()
 
     flags = marks[:, 1:2, :]
     flags = flags - 2.0 * jnp.floor(0.5 * flags)
@@ -159,8 +143,38 @@
         against, _ = row_weights(coupling[d], sea, True)
         shares[d] = jnp.where(back[d] > 0.5, against, onward)
         gain[d] = onward_gain
+    pl.semaphore_wait(
+        barrier, 3 + len(neighbours) + (z > 0).astype(jnp.int32) + (z < depth - 1).astype(jnp.int32)
+    )
+
+    stores = []
+
+    def keep(src, dst):
+        stores.append(pltpu.make_async_copy(src, dst, store_sem.at[len(stores)]))
+        stores[-1].start()
+
+    halo_copies = []
+    for way, (peer, start, to) in enumerate(((lower, 0, SHIFT), (higher, dirs - SHIFT, 0))):
+        bands = pl.ds(1 - way, previous.shape[1] - 1)
+        for i, (src, dst) in enumerate(
+            (
+                (previous_in.at[pl.ds(start, SHIFT), bands], halo_previous.at[pl.ds(to, SHIFT), bands]),
+                (marks.at[pl.ds(start, SHIFT)], halo_marks.at[pl.ds(to, SHIFT)]),
+            )
+        ):
+            halo_copies.append(
+                pltpu.make_async_remote_copy(
+                    src_ref=src, dst_ref=dst,
+                    send_sem=halo_send.at[way, i], recv_sem=halo_recv.at[way, i],
+                    device_id={"dirs": peer}, device_id_type=MESH,
+                )
+            )
+            halo_copies[-1].start()
+
     for copy in gain_copies:
         copy.start()
+    for way, start in enumerate((0, dirs - SHIFT)):
+        keep(coupling.at[pl.ds(start, SHIFT)], edges.at[way, 4])
 
     def compose(h, d, _):
         share = shares[d]
@@ -171,10 +185,10 @@
 
     for j in order:
         previous_loads[j].wait()
-        lax.fori_loop(j * size, (j + 1) * size, functools.partial(compose, 1 - c), 0)
+        lax.fori_loop(j * size, (j + 1) * size, functools.partial(compose, 1 - half), 0)
         core_copies[j].start()
     for j in order:
-        lax.fori_loop(j * size, (j + 1) * size, functools.partial(compose, c), 0)
+        lax.fori_loop(j * size, (j + 1) * size, functools.partial(compose, half), 0)
     boundary_load.wait()
     c_bit, x_bit = c.astype(f32), x.astype(f32)
     core_after = c_bit + back - 2.0 * c_bit * back
@@ -197,15 +211,11 @@
     for j in order:
         core_copies[j].wait_recv()
         half_total[:, part(j)] = (
-            cut(core_a, j)[None] * got_core[:, part(j)] + cut(core_b, j)[None] * state[c, :, part(j)]
+            cut(core_a, j)[None] * got_core[:, part(j)] + cut(core_b, j)[None] * state[half, :, part(j)]
         )
         pair_copies[j].start()
-    for j in order:
-        pair_copies[j].wait_recv()
-        plane[part(j)] = cut(pair_a, j) * got_pair[part(j)] + cut(pair_b, j) * half_total[x, part(j)]
-
     upper = (2 * z >= depth).astype(jnp.int32)
-    mine_at = 2 * c + x
+    mine_at = 2 * half + x
 
     def chain(j, way):
         step = 1 - 2 * way
@@ -213,7 +223,7 @@
         has_after = jnp.where(way == 0, z < depth - 1, z > 0)
         copy = remote(
             chain_out.at[way, part(j)], chain_in.at[way, part(j)],
-            chain_send.at[way, j], chain_recv.at[way, j], me + 4 * step,
+            chain_send.at[way, j], chain_recv.at[way, j], core_peer + 4 * step,
         )
 
         @pl.when(has_before)
@@ -234,35 +244,51 @@
 
     pair_p, pair_q = split(pair_after, pair_mine, pair_theirs)
     core_p, core_q = split(core_after, core_mine, core_theirs)
-    for j in order:
-        chain(j, upper)
-    for j in order:
-        chain(j, 1 - upper)
+
+    def leave(j):
         entering = jnp.where(cut(back, j) > 0.5, chain_in[1, part(j)], chain_in[0, part(j)])
         pair_out[part(j)] = cut(pair_q, j) * entering + (1.0 - cut(pair_after, j)) * half_total[x, part(j)]
         back_copies[j].start()
         pair_in[x, part(j)] = cut(pair_p, j) * entering + cut(pair_after, j) * got_pair[part(j)]
-    for j in order:
+
+    def finish(j):
         back_copies[j].wait_recv()
         entering = pair_in[:, part(j)]
         core_out[:, part(j)] = (
-            cut(core_q, j)[None] * entering + (1.0 - cut(core_after, j))[None] * state[c, :, part(j)]
+            cut(core_q, j)[None] * entering + (1.0 - cut(core_after, j))[None] * state[half, :, part(j)]
         )
         last_copies[j].start()
-        out[c, :, part(j)] = cut(core_p, j)[None] * entering + cut(core_after, j)[None] * got_core[:, part(j)]
+        out[half, :, part(j)] = cut(core_p, j)[None] * entering + cut(core_after, j)[None] * got_core[:, part(j)]
+
+    for i in range(2 * chunks + 1):
+        if i < chunks:
+            j = order[i]
+            pair_copies[j].wait_recv()
+            plane[part(j)] = cut(pair_a, j) * got_pair[part(j)] + cut(pair_b, j) * half_total[x, part(j)]
+            chain(j, upper)
+        if chunks <= i < 2 * chunks:
+            chain(order[i - chunks], 1 - upper)
+            leave(order[i - chunks])
+        if chunks < i:
+            finish(order[i - chunks - 1])
     for j in order:
         last_copies[j].wait_recv()
-    edges[0] = out[:, :, 0:SHIFT]
-    edges[1] = out[:, :, dirs - SHIFT : dirs]
+        keep(out.at[:, :, part(j)], entering_out.at[:, :, part(j)])
+        for way, (at, start) in enumerate(((0, 0), (chunks - 1, dirs - SHIFT))):
+            if j == at:
+                for h in range(2):
+                    keep(out.at[h, :, pl.ds(start, SHIFT)], edges.at[way, pl.ds(2 * h, 2)])
     for copy in halo_copies:
         copy.wait_recv()
+    for store in stores:
+        store.wait()
     for copy in halo_copies + gain_copies + core_copies + pair_copies + back_copies + last_copies:
         copy.wait_send()
 
     def drain(j, way):
         copy = remote(
             chain_out.at[way, part(j)], chain_in.at[way, part(j)],
-            chain_send.at[way, j], chain_recv.at[way, j], me + 4 * (1 - 2 * way),
+            chain_send.at[way, j], chain_recv.at[way, j], core_peer + 4 * (1 - 2 * way),
         )
 
         @pl.when(z < depth - 1 if way == 0 else z > 0)
@@ -292,15 +318,15 @@
     out, edges, *halos = pl.pallas_call(
         functools.partial(scan_kernel, count, dir_count, chunks),
         in_specs=[smem, smem] + [anywhere] * 4,
-        out_specs=[vmem, vmem] + [anywhere] * 3,
+        out_specs=[anywhere] * 4,
         out_shape=[
             jax.ShapeDtypeStruct((2, 2) + part, f32),
-            jax.ShapeDtypeStruct((2, 2, 2, SHIFT, quarter, columns), f32),
+            jax.ShapeDtypeStruct((2, 5, SHIFT, quarter, columns), f32),
             halo(previous),
-            halo(coupling),
             jax.ShapeDtypeStruct((2 * SHIFT,) + marks[1:], f32),
         ],
         scratch_shapes=[
+            pltpu.VMEM((2, 2) + part, f32),
             pltpu.VMEM((dirs, 1, columns), f32),
             pltpu.VMEM((2, 2) + part, f32),
             pltpu.VMEM(coupling.shape, f32),
@@ -320,13 +346,14 @@
             pltpu.VMEM(part, f32),
             pltpu.VMEM((2,) + part, f32),
             dma((3 + chunks,)),
+            dma((6 + chunks,)),
             dma((3,)), dma((3,)),
             dma((chunks,)), dma((chunks,)),
             dma((chunks,)), dma((chunks,)),
             dma((2, chunks)), dma((2, chunks)),
             dma((chunks,)), dma((chunks,)),
             dma((chunks,)), dma((chunks,)),
-            dma((2, 3)), dma((2, 3)),
+            dma((2, 2)), dma((2, 2)),
         ],
         compiler_params=pltpu.CompilerParams(
             collective_id=0, has_side_effects=True, vmem_limit_bytes=SCAN_VMEM
@@ -359,7 +386,8 @@
             swept[q * quarter + r] = value
         return 0
 
-    lax.fori_loop(0, 4, group, 0)
+    for q in range(4):
+        group(q, 0)
 
 
 def columns_solve(gain, sea, swept, rounded, settled, sideways):
@@ -373,6 +401,7 @@
     offset = row - column if sideways else column - row
     matrix = jnp.where(offset >= 0, jnp.exp(offset.astype(f32) * slope) * scale, 0.0)
     carry = gains * (matrix[block - 1 :] if sideways else matrix[:1])
+    carry_last = carry[:, :1] if sideways else carry[:, block - 1 :]
     high = matrix.astype(bf16)
     low = (matrix - high.astype(f32)).astype(bf16)
     whole = jnp.concatenate(
@@ -392,9 +421,11 @@
             jnp.concatenate([upper, lower], axis=1), whole, preferred_element_type=f32
         )
         y = both[:, :block] + both[:, block:]
+        last = jnp.broadcast_to(y[:, :1] if sideways else y[:, block - 1 :], y.shape)
         if before is not None:
-            y = y + (before[:, :1] if sideways else before[:, block - 1 :]) * carry
-        before = y
+            y = y + before * carry
+            last = last + before * carry_last
+        before = last
         masked = y.reshape(bands, rows, block) * sea[:, here][None]
         rounded[:, :, here] = masked.astype(bf16)
         if settled is not None:
@@ -413,18 +444,9 @@
 
 
 def own_kernel(
-    quadrant, cross_gain, sea_mask, previous_in, coupling, entering, rounded, settled,
-    previous, swept, sea, load_sem,
+    quadrant, cross_gain, sea_mask, previous, coupling, entering, rounded, settled, swept, sea,
 ):
-    dirs = previous.shape[0]
-    loads = [
-        pltpu.make_async_copy(previous_in.at[d], previous.at[d], load_sem.at[d]) for d in range(dirs)
-    ]
-    for load in loads:
-        load.start()
     sea[...] = sea_mask[...].astype(f32)
-    for load in loads:
-        load.wait()
 
     def one(d, _):
         settle(
@@ -433,27 +455,24 @@
         )
         return 0
 
-    lax.fori_loop(0, dirs, one, 0)
+    lax.fori_loop(0, previous.shape[0], one, 0)
 
 
 def settle_own(quadrant, cross_gain, sea_mask, previous, coupling, entering):
     dirs, bands, rows, columns = previous.shape
     vmem = pl.BlockSpec(memory_space=pltpu.VMEM)
     smem = pl.BlockSpec(memory_space=pltpu.SMEM)
-    anywhere = pl.BlockSpec(memory_space=pl.ANY)
     return pl.pallas_call(
         own_kernel,
-        in_specs=[smem, smem, vmem, anywhere, vmem, vmem],
+        in_specs=[smem, smem] + [vmem] * 4,
         out_specs=[vmem, vmem],
         out_shape=[
             jax.ShapeDtypeStruct(previous.shape, bf16),
             jax.ShapeDtypeStruct(previous.shape, f32),
         ],
         scratch_shapes=[
-            pltpu.VMEM(previous.shape, bf16),
             pltpu.VMEM((bands, rows, columns), f32),
             pltpu.VMEM((rows, columns), f32),
-            pltpu.SemaphoreType.DMA((dirs,)),
         ],
         compiler_params=pltpu.CompilerParams(vmem_limit_bytes=STEP_VMEM),
         cost_estimate=cost(12),
@@ -462,11 +481,13 @@
 
 
 def source_kernel(
-    halo_marks, coef, sea_mask, wet_tiles, halo_previous, halo_coupling, incoming, own, settled,
-    out, halo, swept, sea, wet, result, store_sem,
+    halo_marks, coef, sea_mask, wet_tiles, halo_previous, incoming_in, own, settled,
+    out, halo, incoming, swept, sea, wet, result, load_sem, store_sem,
 ):
     dirs, bands, rows, columns = settled.shape
     pieces = columns // BLOCK
+    load = pltpu.make_async_copy(incoming_in, incoming, load_sem.at[0])
+    load.start()
     sea[...] = sea_mask[...].astype(f32)
     for k in range(pieces):
         flag = wet_tiles[:, k : k + 1].astype(f32)
@@ -499,7 +520,7 @@
             one(f, above(f), below(f))
             return 0
 
-        lax.fori_loop(1, bands - 1, body, 0, unroll=6 if (bands - 2) % 6 == 0 else 1)
+        lax.fori_loop(1, bands - 1, body, 0, unroll=True)
         stores[d].start()
 
     inner = [d for d in range(dirs) if SHIFT <= d < dirs - SHIFT]
@@ -509,12 +530,13 @@
     def one_halo(t, _):
         way, at = 1 - t // SHIFT, t % SHIFT
         settle(
-            halo_previous.at[t], halo_coupling[t], lambda q: incoming[way, q, at],
+            halo_previous.at[t], incoming[way, 4, at], lambda q: incoming[way, q, at],
             halo_marks[t, 1, 0].astype(jnp.int32), halo_marks[t, 0, 0], sea[...],
             swept, halo.at[t], None,
         )
         return 0
 
+    load.wait()
     lax.fori_loop(0, 2 * SHIFT, one_halo, 0)
     for d in range(dirs):
         if d not in inner:
@@ -524,28 +546,30 @@
 
 
 def add_source(
-    halo_marks, quad_coef, sea_mask, wet_tiles, halo_previous, halo_coupling, incoming, rounded, settled
+    halo_marks, quad_coef, sea_mask, wet_tiles, halo_previous, incoming, rounded, settled
 ):
     dirs, bands, rows, columns = settled.shape
     vmem = pl.BlockSpec(memory_space=pltpu.VMEM)
     smem = pl.BlockSpec(memory_space=pltpu.SMEM)
     return pl.pallas_call(
         source_kernel,
-        in_specs=[smem, smem] + [vmem] * 7,
+        in_specs=[smem, smem, vmem, vmem, vmem, pl.BlockSpec(memory_space=pl.ANY), vmem, vmem],
         out_specs=pl.BlockSpec(memory_space=pl.ANY),
         out_shape=jax.ShapeDtypeStruct(settled.shape, bf16),
         scratch_shapes=[
             pltpu.VMEM((2 * SHIFT, bands, rows, columns), bf16),
+            pltpu.VMEM(incoming.shape, f32),
             pltpu.VMEM((bands, rows, columns), f32),
             pltpu.VMEM((rows, columns), f32),
             pltpu.VMEM((rows, columns), f32),
             pltpu.VMEM(settled.shape, bf16),
+            pltpu.SemaphoreType.DMA((1,)),
             pltpu.SemaphoreType.DMA((dirs,)),
         ],
         compiler_params=pltpu.CompilerParams(vmem_limit_bytes=STEP_VMEM),
         cost_estimate=cost(8),
         name="add_source",
-    )(halo_marks, quad_coef, sea_mask, wet_tiles, halo_previous, halo_coupling, incoming, rounded, settled)
+    )(halo_marks, quad_coef, sea_mask, wet_tiles, halo_previous, incoming, rounded, settled)
 
 
 def exchange(edges, dir_count):
@@ -560,14 +584,13 @@
     row_devices, dir_devices,
     previous, boundary, row_coupling, cross_gain, block_inverse, quadrant, sea_mask, wet_tiles, quad_coef,
 ):
-    entering, edges, (halo_previous, halo_coupling, halo_marks) = scan_devices(
+    entering, edges, (halo_previous, halo_marks) = scan_devices(
         row_devices, dir_devices, quadrant, cross_gain, boundary, sea_mask, previous, row_coupling
     )
     incoming = exchange(edges, dir_devices)
-    incoming = incoming.reshape((2, 4) + incoming.shape[3:])
     rounded, settled = settle_own(quadrant, cross_gain, sea_mask, previous, row_coupling, entering)
     return add_source(
-        halo_marks, quad_coef, sea_mask, wet_tiles, halo_previous, halo_coupling, incoming, rounded, settled
+        halo_marks, quad_coef, sea_mask, wet_tiles, halo_previous, incoming, rounded, settled
     )
 
 

time: 55.7 us -> 51.1 us (0.917)
  Pallas kernels: 52.9 us -> 47.6 us
  starting transfers between devices: 1.17 us -> 1.81 us
    pallas_call x1, Pallas kernels: 34.3 us -> 31 us  [scan_devices(): pl.pallas_call(functools.partial(scan_kernel, count, dir_count, chunks),...]
    pallas_call x2, Pallas kernels: 18.7 us -> 16.7 us  [the longest x1 8.69 us: settle_own(): pl.pallas_call(own_kernel, in_specs=[smem, smem] + [vmem] * 4, out_specs=...]
    ppermute x1, starting transfers between devices: 1.17 us -> 1.81 us  [exchange(): return lax.ppermute(edges, 'dirs', [(0, 1), (1, 0)])]
    unnamed x23 -> x21, local copies, waits for them, and re-layouts: 1.33 us -> 1.32 us
  transfers between devices with their start and end apart: 1 -> 1, of which waited for: 0 -> 0; matrix products, arithmetic and copies ran while one was open for 0% -> 0% of each run, Pallas kernels for 18% -> 17%
where the time goes in v2:
time: 51.1 us; the launch traced here: 50.9 us
  Pallas kernels  47.6 us (93%)
  starting transfers between devices  1.81 us (4%)
  local copies, waits for them, and re-layouts  1.32 us (3%)
    pallas_call x1, Pallas kernels, scan_devices(): pl.pallas_call(functools.partial(scan_kernel, count, dir_count, chunks),...  31 us
    pallas_call x1, Pallas kernels, settle_own(): pl.pallas_call(own_kernel, in_specs=[smem, smem] + [vmem] * 4, out_specs=...  8.69 us
    pallas_call x1, Pallas kernels, add_source(): pl.pallas_call(source_kernel, in_specs=[smem, smem, vmem, vmem, vmem, pl....  7.97 us
    ppermute x1, starting transfers between devices, exchange(): return lax.ppermute(edges, 'dirs', [(0, 1), (1, 0)])  1.81 us
    unnamed x21, local copies, waits for them, and re-layouts  1.32 us
  transfers between devices with their start and end apart: 1, of which 0 were waited for; matrix products, arithmetic and copies ran while one was open for 0% of the time, Pallas kernels for 17%

profile of v2, /device:TPU:0, one launch (start us, length us, event | category | flops | bytes accessed | tf_op | source)
XLA Modules:
  0.0 50.9 jit_solution(615871598792663071)
XLA Ops:
  0.0 0.0 copy-start.4
  0.0 0.0 copy-start.6
  0.0 0.0 copy-start.7
  0.0 0.0 copy-start.2
  0.0 0.0 copy-start
  0.0 0.0 copy-start.9
  0.0 0.0 copy-start.8
  0.0 31.0 %scan_devices.1 = (f32[2,2,12,8,512]{4,3,2,1,0:T(8,128)}, f32[2,5,2,8,512]{4,3,2,1,0:T(8,128)}, bf16[4,32,8,512]{3,2,1,0:T(8,128)(2,1)}, f32[4,2,128]{2,1,0:T(2,128)}) custom-call(s32[12]{0:T(128)} %quadrant.3, f32[12]{0:T(128)} %cross_gain.3, f32[12,4,8,512]{3,2,1,0:T(8,128)} %bitcast.3, s32[8,512]{1,0:T(8,128)} %sea_mask.3, ...), custom_call_target="tpu_custom_call" | custom-call | bytes 90000000 | tf_op jit(solution)/shard_map/scan_devices/pallas_call | solution.py:318
  31.0 0.0 copy-start.5
  31.0 1.8 %collective-permute-start = (f32[2,5,2,8,512]{4,3,2,1,0:T(8,128)}, f32[2,5,2,8,512]{4,3,2,1,0:T(8,128)}, u32[]{:S(2)}, u32[]{:S(2)}) collective-permute-start(f32[2,5,2,8,512]{4,3,2,1,0:T(8,128)} %get-tuple-element.13), channel_id=1, source_target_pairs={{0,1},{1,0},{2,3},{3,2},{4,5},{5,4},{6,7},{7,6},{8,9},{9,8},{10,11... | collective-permute-start | bytes 983048 | tf_op jit(solution)/shard_map/ppermute | solution.py:577
  32.8 0.0 copy-done.9
  32.8 0.1 copy.9.wet_tiles
  32.9 0.0 copy-start.1
  32.9 0.0 copy-done.4
  32.9 0.0 copy-done.6
  32.9 0.0 copy-done.7
  32.9 0.0 copy-done.2
  32.9 0.0 copy-done
  32.9 0.0 copy-start.3
  32.9 1.2 %copy-done.3 = f32[2,2,12,8,512]{4,3,2,1,0:T(8,128)S(1)} copy-done((f32[2,2,12,8,512]{4,3,2,1,0:T(8,128)S(1)}, f32[2,2,12,8,512]{4,3,2,1,0:T(8,128)}, u32[]{:S(2)}) %copy-start.3) | copy-done | bytes 786456
  34.1 8.7 %settle_own.1 = (bf16[12,32,8,512]{3,2,1,0:T(8,128)(2,1)S(1)}, f32[12,32,8,512]{3,2,1,0:T(8,128)S(1)}) custom-call(s32[12]{0:T(128)S(1)} %copy-done.6, f32[12]{0:T(128)S(1)} %copy-done.7, s32[8,512]{1,0:T(8,128)S(1)} %copy-done.4, bf16[12,32,8,512]{3,2,1,0:T(8,128)(2,1)S(1)} %copy-done, f32[12,8,512]{2,1,0:T(8,128)S(1)} %copy-done.2, ...), custom_call_target="tpu_custom_call" | custom-call | bytes 36000000 | tf_op jit(solution)/shard_map/settle_own/pallas_call | solution.py:465
  42.8 0.0 collective-permute-done.incoming_in
  42.9 0.0 copy-done.8
  42.9 0.0 copy-done.5
  42.9 0.0 copy-done.1
  42.9 8.0 %add_source.1 = bf16[12,32,8,512]{3,2,1,0:T(8,128)(2,1)} custom-call(f32[4,2,128]{2,1,0:T(2,128)S(1)} %copy-done.5, f32[32]{0:T(128)S(1)} %copy-done.8, s32[8,512]{1,0:T(8,128)S(1)} %copy-done.4, s32[8,4]{1,0:T(8,128)S(1)} %copy.9.wet_tiles, bf16[4,32,8,512]{3,2,1,0:T(8,128)(2,1)S(1)} %copy-done.1, f32[2,5,2,8,512]{4,3,2,1,0:T(8,128)} %collective-permute-done.incoming_in, ...), custom_call_target="tpu_custom_call" | custom-call | bytes 24000000 | tf_op jit(solution)/shard_map/add_source/pallas_call | solution.py:554
Async XLA Ops:
  0.0 32.9 %copy-start.4 = (s32[8,512]{1,0:T(8,128)S(1)}, s32[8,512]{1,0:T(8,128)}, u32[]{:S(2)}) copy-start(s32[8,512]{1,0:T(8,128)} %sea_mask.3) | copy-start | bytes 49156
  0.0 32.9 %copy-start.6 = (s32[12]{0:T(128)S(1)}, s32[12]{0:T(128)}, u32[]{:S(2)}) copy-start(s32[12]{0:T(128)} %quadrant.3) | copy-start | bytes 148
  0.0 32.9 %copy-start.7 = (f32[12]{0:T(128)S(1)}, f32[12]{0:T(128)}, u32[]{:S(2)}) copy-start(f32[12]{0:T(128)} %cross_gain.3) | copy-start | bytes 148
  0.0 32.9 %copy-start.2 = (f32[12,8,512]{2,1,0:T(8,128)S(1)}, f32[12,8,512]{2,1,0:T(8,128)}, u32[]{:S(2)}) copy-start(f32[12,8,512]{2,1,0:T(8,128)} %coupling.1) | copy-start | bytes 589828
  0.0 32.9 %copy-start = (bf16[12,32,8,512]{3,2,1,0:T(8,128)(2,1)S(1)}, bf16[12,32,8,512]{3,2,1,0:T(8,128)(2,1)}, u32[]{:S(2)}) copy-start(bf16[12,32,8,512]{3,2,1,0:T(8,128)(2,1)} %previous.1) | copy-start | bytes 9437188
  0.0 32.8 %copy-start.9 = (s32[8,4]{0,1:T(4,128)S(1)}, s32[8,4]{0,1:T(4,128)}, u32[]{:S(2)}) copy-start(s32[8,4]{0,1:T(4,128)} %param.15) | copy-start | bytes 388
  0.0 42.8 %copy-start.8 = (f32[32]{0:T(128)S(1)}, f32[32]{0:T(128)}, u32[]{:S(2)}) copy-start(f32[32]{0:T(128)} %coef.1) | copy-start | bytes 388
  31.0 11.9 %copy-start.5 = (f32[4,2,128]{2,1,0:T(2,128)S(1)}, f32[4,2,128]{2,1,0:T(2,128)}, u32[]{:S(2)}) copy-start(f32[4,2,128]{2,1,0:T(2,128)} %get-tuple-element.11.halo_marks) | copy-start | bytes 12292
  31.0 11.8 %collective-permute-start = (f32[2,5,2,8,512]{4,3,2,1,0:T(8,128)}, f32[2,5,2,8,512]{4,3,2,1,0:T(8,128)}, u32[]{:S(2)}, u32[]{:S(2)}) collective-permute-start(f32[2,5,2,8,512]{4,3,2,1,0:T(8,128)} %get-tuple-element.13), channel_id=1, source_target_pairs={{0,1},{1,0},{2,3},{3,2},{4,5},{5,4},{6,7},{7,6},{8,9},{9,8},{10,11... | collective-permute-start | bytes 983048 | tf_op jit(solution)/shard_map/ppermute | solution.py:577
  32.9 10.0 %copy-start.1 = (bf16[4,32,8,512]{3,2,1,0:T(8,128)(2,1)S(1)}, bf16[4,32,8,512]{3,2,1,0:T(8,128)(2,1)}, u32[]{:S(2)}) copy-start(bf16[4,32,8,512]{3,2,1,0:T(8,128)(2,1)} %get-tuple-element.12.halo_previous) | copy-start | bytes 3145732
  32.9 1.2 %copy-start.3 = (f32[2,2,12,8,512]{4,3,2,1,0:T(8,128)S(1)}, f32[2,2,12,8,512]{4,3,2,1,0:T(8,128)}, u32[]{:S(2)}) copy-start(f32[2,2,12,8,512]{4,3,2,1,0:T(8,128)} %get-tuple-element.14) | copy-start | bytes 2359300

commit v3 on v2

--- a/solution.py
+++ b/solution.py
@@ -364,35 +364,10 @@
     return out.reshape(4, dirs, quarter, columns), edges, halos
 
 
-def sweep(previous, coupling, inflow_of, swept, sea, backward):
-    bands = previous.shape[0]
+def settle_one(previous, coupling, inflow_of, gain, sea, rounded, settled, backward, sideways):
+    bands, rows, columns = previous.shape
+    block = BLOCK
     quarter = bands // 4
-    couple, weight = weights(coupling, sea)
-    rows = couple.shape[0]
-    order = visit_order(couple.shape, backward)
-    first = jnp.where(order == 0, couple, 0.0)
-    spans, reach, span = [], couple, 1
-    while span < rows:
-        spans.append((span, jnp.where(order >= span, reach, 0.0)))
-        reach = jnp.where(order >= span, reach * rolled(reach, span, backward), reach)
-        span *= 2
-
-    def group(q, _):
-        inflow = inflow_of(q)
-        for r in range(quarter):
-            value = weight * previous[q * quarter + r].astype(f32) + first * inflow[r : r + 1]
-            for span, factor in spans:
-                value = value + factor * rolled(value, span, backward)
-            swept[q * quarter + r] = value
-        return 0
-
-    for q in range(4):
-        group(q, 0)
-
-
-def columns_solve(gain, sea, swept, rounded, settled, sideways):
-    bands, rows, columns = swept.shape
-    block = BLOCK
     pieces = columns // block
     gains = jnp.full((1, block), gain, f32)
     slope, scale = jnp.log(gains / (1.0 + gains)), 1.0 / (1.0 + gains)
@@ -411,10 +386,26 @@
         ],
         axis=0,
     )
+    order = visit_order((rows, block), backward)
     before = None
     for k in range(pieces - 1, -1, -1) if sideways else range(pieces):
         here = slice(k * block, (k + 1) * block)
-        x = swept[:, :, here].reshape(bands * rows, block)
+        couple, weight = weights(coupling[:, here], sea[:, here])
+        first = jnp.where(order == 0, couple, 0.0)
+        spans, reach, span = [], couple, 1
+        while span < rows:
+            spans.append((span, jnp.where(order >= span, reach, 0.0)))
+            reach = jnp.where(order >= span, reach * rolled(reach, span, backward), reach)
+            span *= 2
+        values = []
+        for f in range(bands):
+            value = weight * previous[f, :, here].astype(f32) + first * inflow_of(
+                f // quarter, f % quarter, here
+            )
+            for span, factor in spans:
+                value = value + factor * rolled(value, span, backward)
+            values.append(value)
+        x = jnp.concatenate(values, axis=0)
         upper = x.astype(bf16)
         lower = (x - upper.astype(f32)).astype(bf16)
         both = jnp.dot(
@@ -432,144 +423,167 @@
             settled[:, :, here] = masked
 
 
-def settle(previous, coupling, inflow_of, corner, gain, sea, swept, rounded, settled):
-    for flag in (0, 1):
-        pl.when(corner % 2 == flag)(
-            functools.partial(sweep, previous, coupling, inflow_of, swept, sea, flag == 1)
-        )
-    for flag in (0, 1):
-        pl.when(corner // 2 == flag)(
-            functools.partial(columns_solve, gain, sea, swept, rounded, settled, flag == 1)
-        )
+def settle(previous, coupling, inflow_of, corner, gain, sea, rounded, settled):
+    for flag in range(4):
+        pl.when(corner == flag)(
+            functools.partial(
+                settle_one, previous, coupling, inflow_of, gain, sea, rounded, settled,
+                flag % 2 == 1, flag // 2 == 1,
+            )
+        )
+
+
+def wet_field(wet_tiles, wet):
+    rows, columns = wet.shape
+    for k in range(columns // BLOCK):
+        flag = wet_tiles[:, k : k + 1].astype(f32)
+        wet[:, k * BLOCK : (k + 1) * BLOCK] = jnp.broadcast_to(flag, (rows, BLOCK))
+
+
+def source(coef, own, onward_of, against_of, settled, wet, result):
+    bands = own.shape[0]
+    wet_cells = wet[...]
+
+    def one(f, onward, against):
+        energy = own[f].astype(f32)
+        value = coef[f] * (
+            energy * energy * (onward + against) - 2.0 * energy * onward * against
+        )
+        result[f] = (settled[f] + wet_cells * value.astype(bf16).astype(f32)).astype(bf16)
+
+    def above(f):
+        return onward_of[f + 1].astype(f32)
+
+    def below(f):
+        return against_of[f - 1].astype(f32)
+
+    nothing = jnp.zeros(wet.shape, f32)
+    one(0, above(0), nothing)
+    one(bands - 1, nothing, below(bands - 1))
+
+    def body(f, _):
+        one(f, above(f), below(f))
+        return 0
+
+    lax.fori_loop(1, bands - 1, body, 0, unroll=True)
 
 
 def own_kernel(
-    quadrant, cross_gain, sea_mask, previous, coupling, entering, rounded, settled, swept, sea,
+    quadrant, cross_gain, coef, sea_mask, wet_tiles, previous, coupling, entering, rounded, settled, *refs
 ):
+    dirs = previous.shape[0]
+    *inner, sea, wet = refs
     sea[...] = sea_mask[...].astype(f32)
+    wet_field(wet_tiles, wet)
 
     def one(d, _):
         settle(
-            previous.at[d], coupling[d], lambda q: entering[q, d], quadrant[d], cross_gain[d], sea[...],
-            swept, rounded.at[d], settled.at[d],
+            previous.at[d], coupling.at[d], lambda q, r, here: entering[q, d, r : r + 1, here],
+            quadrant[d], cross_gain[d], sea, rounded.at[d], settled.at[d],
         )
         return 0
 
-    lax.fori_loop(0, previous.shape[0], one, 0)
-
-
-def settle_own(quadrant, cross_gain, sea_mask, previous, coupling, entering):
+    def inner_source(d, _):
+        source(
+            coef, rounded.at[d], rounded.at[d + SHIFT], rounded.at[d - SHIFT], settled.at[d], wet,
+            inner[0].at[d - SHIFT],
+        )
+        return 0
+
+    lax.fori_loop(0, dirs, one, 0)
+    if inner:
+        lax.fori_loop(SHIFT, dirs - SHIFT, inner_source, 0)
+
+
+def settle_own(quadrant, cross_gain, quad_coef, sea_mask, wet_tiles, previous, coupling, entering):
     dirs, bands, rows, columns = previous.shape
     vmem = pl.BlockSpec(memory_space=pltpu.VMEM)
     smem = pl.BlockSpec(memory_space=pltpu.SMEM)
+    out_shape = [
+        jax.ShapeDtypeStruct(previous.shape, bf16),
+        jax.ShapeDtypeStruct(previous.shape, f32),
+    ]
+    if dirs > 2 * SHIFT:
+        out_shape.append(jax.ShapeDtypeStruct((dirs - 2 * SHIFT,) + previous.shape[1:], bf16))
     return pl.pallas_call(
         own_kernel,
-        in_specs=[smem, smem] + [vmem] * 4,
-        out_specs=[vmem, vmem],
-        out_shape=[
-            jax.ShapeDtypeStruct(previous.shape, bf16),
-            jax.ShapeDtypeStruct(previous.shape, f32),
-        ],
+        in_specs=[smem, smem, smem] + [vmem] * 5,
+        out_specs=[vmem] * len(out_shape),
+        out_shape=out_shape,
         scratch_shapes=[
-            pltpu.VMEM((bands, rows, columns), f32),
+            pltpu.VMEM((rows, columns), f32),
             pltpu.VMEM((rows, columns), f32),
         ],
         compiler_params=pltpu.CompilerParams(vmem_limit_bytes=STEP_VMEM),
         cost_estimate=cost(12),
         name="settle_own",
-    )(quadrant, cross_gain, sea_mask, previous, coupling, entering)
-
-
-def source_kernel(
-    halo_marks, coef, sea_mask, wet_tiles, halo_previous, incoming_in, own, settled,
-    out, halo, incoming, swept, sea, wet, result, load_sem, store_sem,
-):
+    )(quadrant, cross_gain, quad_coef, sea_mask, wet_tiles, previous, coupling, entering)
+
+
+def source_kernel(halo_marks, coef, sea_mask, wet_tiles, halo_previous, incoming_in, own, settled, *refs):
+    *inner, out, halo, incoming, sea, wet, result, load_sem, store_sem = refs
     dirs, bands, rows, columns = settled.shape
-    pieces = columns // BLOCK
     load = pltpu.make_async_copy(incoming_in, incoming, load_sem.at[0])
     load.start()
+    edge = [d for d in range(dirs) if d < SHIFT or d >= dirs - SHIFT]
+    stores = [pltpu.make_async_copy(result.at[i], out.at[d], store_sem.at[i]) for i, d in enumerate(edge)]
+    if inner:
+        copy = pltpu.make_async_copy(
+            inner[0], out.at[pl.ds(SHIFT, dirs - 2 * SHIFT)], store_sem.at[len(edge)]
+        )
+        copy.start()
     sea[...] = sea_mask[...].astype(f32)
-    for k in range(pieces):
-        flag = wet_tiles[:, k : k + 1].astype(f32)
-        wet[:, k * BLOCK : (k + 1) * BLOCK] = jnp.broadcast_to(flag, (rows, BLOCK))
-    stores = [pltpu.make_async_copy(result.at[d], out.at[d], store_sem.at[d]) for d in range(dirs)]
-
-    def source(d):
-        wet_cells = wet[...]
-        onward_of = own.at[d + SHIFT] if d + SHIFT < dirs else halo.at[2 * SHIFT + d - dirs]
-        against_of = own.at[d - SHIFT] if d >= SHIFT else halo.at[d]
-
-        def one(f, onward, against):
-            energy = own[d, f].astype(f32)
-            value = coef[f] * (
-                energy * energy * (onward + against) - 2.0 * energy * onward * against
-            )
-            result[d, f] = (settled[d, f] + wet_cells * value.astype(bf16).astype(f32)).astype(bf16)
-
-        def above(f):
-            return onward_of[f + 1].astype(f32)
-
-        def below(f):
-            return against_of[f - 1].astype(f32)
-
-        nothing = jnp.zeros(wet.shape, f32)
-        one(0, above(0), nothing)
-        one(bands - 1, nothing, below(bands - 1))
-
-        def body(f, _):
-            one(f, above(f), below(f))
-            return 0
-
-        lax.fori_loop(1, bands - 1, body, 0, unroll=True)
-        stores[d].start()
-
-    inner = [d for d in range(dirs) if SHIFT <= d < dirs - SHIFT]
-    for d in inner:
-        source(d)
+    wet_field(wet_tiles, wet)
+    load.wait()
 
     def one_halo(t, _):
         way, at = 1 - t // SHIFT, t % SHIFT
         settle(
-            halo_previous.at[t], incoming[way, 4, at], lambda q: incoming[way, q, at],
-            halo_marks[t, 1, 0].astype(jnp.int32), halo_marks[t, 0, 0], sea[...],
-            swept, halo.at[t], None,
+            halo_previous.at[t], incoming.at[way, 4, at],
+            lambda q, r, here: incoming[way, q, at, r : r + 1, here],
+            halo_marks[t, 1, 0].astype(jnp.int32), halo_marks[t, 0, 0], sea, halo.at[t], None,
         )
         return 0
 
-    load.wait()
     lax.fori_loop(0, 2 * SHIFT, one_halo, 0)
-    for d in range(dirs):
-        if d not in inner:
-            source(d)
+    for i, d in enumerate(edge):
+        source(
+            coef, own.at[d],
+            own.at[d + SHIFT] if d + SHIFT < dirs else halo.at[2 * SHIFT + d - dirs],
+            own.at[d - SHIFT] if d >= SHIFT else halo.at[d],
+            settled.at[d], wet, result.at[i],
+        )
+        stores[i].start()
     for store in stores:
         store.wait()
-
-
-def add_source(
-    halo_marks, quad_coef, sea_mask, wet_tiles, halo_previous, incoming, rounded, settled
-):
+    if inner:
+        copy.wait()
+
+
+def add_source(halo_marks, quad_coef, sea_mask, wet_tiles, halo_previous, incoming, rounded, settled, *inner):
     dirs, bands, rows, columns = settled.shape
     vmem = pl.BlockSpec(memory_space=pltpu.VMEM)
     smem = pl.BlockSpec(memory_space=pltpu.SMEM)
+    anywhere = pl.BlockSpec(memory_space=pl.ANY)
+    edges = min(dirs, 2 * SHIFT)
     return pl.pallas_call(
         source_kernel,
-        in_specs=[smem, smem, vmem, vmem, vmem, pl.BlockSpec(memory_space=pl.ANY), vmem, vmem],
-        out_specs=pl.BlockSpec(memory_space=pl.ANY),
+        in_specs=[smem, smem, vmem, vmem, vmem, anywhere, vmem, vmem] + [anywhere] * len(inner),
+        out_specs=anywhere,
         out_shape=jax.ShapeDtypeStruct(settled.shape, bf16),
         scratch_shapes=[
             pltpu.VMEM((2 * SHIFT, bands, rows, columns), bf16),
             pltpu.VMEM(incoming.shape, f32),
-            pltpu.VMEM((bands, rows, columns), f32),
             pltpu.VMEM((rows, columns), f32),
             pltpu.VMEM((rows, columns), f32),
-            pltpu.VMEM(settled.shape, bf16),
+            pltpu.VMEM((edges, bands, rows, columns), bf16),
             pltpu.SemaphoreType.DMA((1,)),
-            pltpu.SemaphoreType.DMA((dirs,)),
+            pltpu.SemaphoreType.DMA((edges + 1,)),
         ],
         compiler_params=pltpu.CompilerParams(vmem_limit_bytes=STEP_VMEM),
         cost_estimate=cost(8),
         name="add_source",
-    )(halo_marks, quad_coef, sea_mask, wet_tiles, halo_previous, incoming, rounded, settled)
+    )(halo_marks, quad_coef, sea_mask, wet_tiles, halo_previous, incoming, rounded, settled, *inner)
 
 
 def exchange(edges, dir_count):
@@ -588,9 +602,11 @@
         row_devices, dir_devices, quadrant, cross_gain, boundary, sea_mask, previous, row_coupling
     )
     incoming = exchange(edges, dir_devices)
-    rounded, settled = settle_own(quadrant, cross_gain, sea_mask, previous, row_coupling, entering)
+    rounded, settled, *inner = settle_own(
+        quadrant, cross_gain, quad_coef, sea_mask, wet_tiles, previous, row_coupling, entering
+    )
     return add_source(
-        halo_marks, quad_coef, sea_mask, wet_tiles, halo_previous, incoming, rounded, settled
+        halo_marks, quad_coef, sea_mask, wet_tiles, halo_previous, incoming, rounded, settled, *inner
     )
 
 

time: 51.1 us -> 49 us (0.959)
  Pallas kernels: 47.6 us -> 45.5 us
    pallas_call x2, Pallas kernels: 16.7 us -> 14.5 us  [the longest x1 8.89 us: settle_own(): pl.pallas_call(own_kernel, in_specs=[smem, smem, smem] + [vmem] * 5, out_...]
  transfers between devices with their start and end apart: 1 -> 1, of which waited for: 0 -> 0; matrix products, arithmetic and copies ran while one was open for 0% -> 0% of each run, Pallas kernels for 17% -> 18%
where the time goes in v3:
time: 49 us; the launch traced here: 48.7 us
  Pallas kernels  45.5 us (93%)
  starting transfers between devices  1.81 us (4%)
  local copies, waits for them, and re-layouts  1.32 us (3%)
    pallas_call x1, Pallas kernels, scan_devices(): pl.pallas_call(functools.partial(scan_kernel, count, dir_count, chunks),...  31 us
    pallas_call x1, Pallas kernels, settle_own(): pl.pallas_call(own_kernel, in_specs=[smem, smem, smem] + [vmem] * 5, out_...  8.89 us
    pallas_call x1, Pallas kernels, add_source(): pl.pallas_call(source_kernel, in_specs=[smem, smem, vmem, vmem, vmem, any...  5.65 us
    ppermute x1, starting transfers between devices, exchange(): return lax.ppermute(edges, 'dirs', [(0, 1), (1, 0)])  1.81 us
    unnamed x21, local copies, waits for them, and re-layouts  1.32 us
  transfers between devices with their start and end apart: 1, of which 0 were waited for; matrix products, arithmetic and copies ran while one was open for 0% of the time, Pallas kernels for 18%

profile of v3, /device:TPU:0, one launch (start us, length us, event | category | flops | bytes accessed | tf_op | source)
XLA Modules:
  0.0 48.7 jit_solution(2354748899500079045)
XLA Ops:
  0.0 0.0 copy-start.4
  0.0 0.0 copy-start.7
  0.0 0.0 copy-start.8
  0.0 0.0 copy-start.2
  0.0 0.0 copy-start
  0.0 0.0 copy-start.9
  0.0 0.0 copy-start.6
  0.0 31.0 %scan_devices.1 = (f32[2,2,12,8,512]{4,3,2,1,0:T(8,128)}, f32[2,5,2,8,512]{4,3,2,1,0:T(8,128)}, bf16[4,32,8,512]{3,2,1,0:T(8,128)(2,1)}, f32[4,2,128]{2,1,0:T(2,128)}) custom-call(s32[12]{0:T(128)} %quadrant.3, f32[12]{0:T(128)} %cross_gain.3, f32[12,4,8,512]{3,2,1,0:T(8,128)} %bitcast.3, s32[8,512]{1,0:T(8,128)} %sea_mask.3, ...), custom_call_target="tpu_custom_call" | custom-call | bytes 90000000 | tf_op jit(solution)/shard_map/scan_devices/pallas_call | solution.py:318
  31.0 0.0 copy-start.5
  31.0 1.8 %collective-permute-start = (f32[2,5,2,8,512]{4,3,2,1,0:T(8,128)}, f32[2,5,2,8,512]{4,3,2,1,0:T(8,128)}, u32[]{:S(2)}, u32[]{:S(2)}) collective-permute-start(f32[2,5,2,8,512]{4,3,2,1,0:T(8,128)} %get-tuple-element.14), channel_id=1, source_target_pairs={{0,1},{1,0},{2,3},{3,2},{4,5},{5,4},{6,7},{7,6},{8,9},{9,8},{10,11... | collective-permute-start | bytes 983048 | tf_op jit(solution)/shard_map/ppermute | solution.py:591
  32.8 0.0 copy-done.9
  32.8 0.1 copy.10.wet_tiles
  32.9 0.0 copy-start.1
  32.9 0.0 copy-done.4
  32.9 0.0 copy-done.7
  32.9 0.0 copy-done.8
  32.9 0.0 copy-done.2
  32.9 0.0 copy-done
  32.9 0.0 copy-done.6
  32.9 0.0 copy-start.3
  33.0 1.2 %copy-done.3 = f32[2,2,12,8,512]{4,3,2,1,0:T(8,128)S(1)} copy-done((f32[2,2,12,8,512]{4,3,2,1,0:T(8,128)S(1)}, f32[2,2,12,8,512]{4,3,2,1,0:T(8,128)}, u32[]{:S(2)}) %copy-start.3) | copy-done | bytes 786456
  34.2 8.9 %settle_own.1 = (bf16[12,32,8,512]{3,2,1,0:T(8,128)(2,1)S(1)}, f32[12,32,8,512]{3,2,1,0:T(8,128)S(1)}, bf16[8,32,8,512]{3,2,1,0:T(8,128)(2,1)S(1)}) custom-call(s32[12]{0:T(128)S(1)} %copy-done.7, f32[12]{0:T(128)S(1)} %copy-done.8, f32[32]{0:T(128)S(1)} %copy-done.6, s32[8,512]{1,0:T(8,128)S(1)} %copy-done.4, s32[8,4]{1,0:T(8,128)S(1)} %copy.10.wet_tiles, ...), custom_call_target="tpu_custom_call" | custom-call | bytes 36000000 | tf_op jit(solution)/shard_map/settle_own/pallas_call | solution.py:508
  43.1 0.0 collective-permute-done.incoming_in
  43.1 0.0 copy-done.5
  43.1 0.0 copy-done.1
  43.1 5.6 %add_source.1 = bf16[12,32,8,512]{3,2,1,0:T(8,128)(2,1)} custom-call(f32[4,2,128]{2,1,0:T(2,128)S(1)} %copy-done.5, f32[32]{0:T(128)S(1)} %copy-done.6, s32[8,512]{1,0:T(8,128)S(1)} %copy-done.4, s32[8,4]{1,0:T(8,128)S(1)} %copy.10.wet_tiles, bf16[4,32,8,512]{3,2,1,0:T(8,128)(2,1)S(1)} %copy-done.1, f32[2,5,2,8,512]{4,3,2,1,0:T(8,128)} %collective-permute-done.incoming_in, ...), custom_call_target="tpu_custom_call" | custom-call | bytes 24000000 | tf_op jit(solution)/shard_map/add_source/pallas_call | solution.py:569
Async XLA Ops:
  0.0 32.9 %copy-start.4 = (s32[8,512]{1,0:T(8,128)S(1)}, s32[8,512]{1,0:T(8,128)}, u32[]{:S(2)}) copy-start(s32[8,512]{1,0:T(8,128)} %sea_mask.3) | copy-start | bytes 49156
  0.0 32.9 %copy-start.7 = (s32[12]{0:T(128)S(1)}, s32[12]{0:T(128)}, u32[]{:S(2)}) copy-start(s32[12]{0:T(128)} %quadrant.3) | copy-start | bytes 148
  0.0 32.9 %copy-start.8 = (f32[12]{0:T(128)S(1)}, f32[12]{0:T(128)}, u32[]{:S(2)}) copy-start(f32[12]{0:T(128)} %cross_gain.3) | copy-start | bytes 148
  0.0 32.9 %copy-start.2 = (f32[12,8,512]{2,1,0:T(8,128)S(1)}, f32[12,8,512]{2,1,0:T(8,128)}, u32[]{:S(2)}) copy-start(f32[12,8,512]{2,1,0:T(8,128)} %coupling.1) | copy-start | bytes 589828
  0.0 32.9 %copy-start = (bf16[12,32,8,512]{3,2,1,0:T(8,128)(2,1)S(1)}, bf16[12,32,8,512]{3,2,1,0:T(8,128)(2,1)}, u32[]{:S(2)}) copy-start(bf16[12,32,8,512]{3,2,1,0:T(8,128)(2,1)} %previous.1) | copy-start | bytes 9437188
  0.0 32.8 %copy-start.9 = (s32[8,4]{0,1:T(4,128)S(1)}, s32[8,4]{0,1:T(4,128)}, u32[]{:S(2)}) copy-start(s32[8,4]{0,1:T(4,128)} %param.15) | copy-start | bytes 388
  0.0 32.9 %copy-start.6 = (f32[32]{0:T(128)S(1)}, f32[32]{0:T(128)}, u32[]{:S(2)}) copy-start(f32[32]{0:T(128)} %coef.3) | copy-start | bytes 388
  31.0 12.1 %copy-start.5 = (f32[4,2,128]{2,1,0:T(2,128)S(1)}, f32[4,2,128]{2,1,0:T(2,128)}, u32[]{:S(2)}) copy-start(f32[4,2,128]{2,1,0:T(2,128)} %get-tuple-element.12.halo_marks) | copy-start | bytes 12292
  31.0 12.0 %collective-permute-start = (f32[2,5,2,8,512]{4,3,2,1,0:T(8,128)}, f32[2,5,2,8,512]{4,3,2,1,0:T(8,128)}, u32[]{:S(2)}, u32[]{:S(2)}) collective-permute-start(f32[2,5,2,8,512]{4,3,2,1,0:T(8,128)} %get-tuple-element.14), channel_id=1, source_target_pairs={{0,1},{1,0},{2,3},{3,2},{4,5},{5,4},{6,7},{7,6},{8,9},{9,8},{10,11... | collective-permute-start | bytes 983048 | tf_op jit(solution)/shard_map/ppermute | solution.py:591
  32.9 10.2 %copy-start.1 = (bf16[4,32,8,512]{3,2,1,0:T(8,128)(2,1)S(1)}, bf16[4,32,8,512]{3,2,1,0:T(8,128)(2,1)}, u32[]{:S(2)}) copy-start(bf16[4,32,8,512]{3,2,1,0:T(8,128)(2,1)} %get-tuple-element.13.halo_previous) | copy-start | bytes 3145732
  32.9 1.2 %copy-start.3 = (f32[2,2,12,8,512]{4,3,2,1,0:T(8,128)S(1)}, f32[2,2,12,8,512]{4,3,2,1,0:T(8,128)}, u32[]{:S(2)}) copy-start(f32[2,2,12,8,512]{4,3,2,1,0:T(8,128)} %get-tuple-element.15) | copy-start | bytes 2359300

commit v4 on v3

--- a/solution.py
+++ b/solution.py
@@ -12,7 +12,7 @@
 bf16 = jnp.bfloat16
 MESH = pl.DeviceIdType.MESH
 SCAN_VMEM = 56 * 1024 * 1024
-STEP_VMEM = 16 * 1024 * 1024
+STEP_VMEM = 56 * 1024 * 1024
 BLOCK = 128
 
 
@@ -50,13 +50,14 @@
 
 
 def scan_kernel(
-    count, dir_count, chunks, quadrant, cross_gain, boundary_in, sea_in, previous_in, coupling_in,
-    entering_out, edges, halo_previous, halo_marks,
-    out,
+    count, dir_count, chunks, quadrant, cross_gain, coef, boundary_in, sea_in, previous_in, coupling_in, wet_in,
+    own_out, settled_out, inner_out, halo_previous, halo_entering, halo_coupling, halo_marks,
+    out, back_rows, cumulated, settled, rounded, result, wet_tiles, wet, sea_field,
     gain, state, shares, marks, boundary, sea_mask, previous, coupling,
     gains, got_core, half_total, got_pair, plane, chain_in, chain_out, pair_in, pair_out, core_out,
-    load_sem, store_sem, gain_send, gain_recv, core_send, core_recv, pair_send, pair_recv,
+    load_sem, gain_send, gain_recv, core_send, core_recv, pair_send, pair_recv,
     chain_send, chain_recv, back_send, back_recv, last_send, last_recv, halo_send, halo_recv,
+    edge_send, edge_recv, own_sem, settled_sem, inner_sem,
 ):
     me = lax.axis_index("rows")
     c, x, z = me % 2, (me // 2) % 2, me // 4
@@ -91,6 +92,7 @@
         pl.semaphore_signal(barrier, inc=1, device_id={"dirs": peer}, device_id_type=MESH)
 
     order = [0] + list(range(chunks - 1, 0, -1))
+    wet_load = pltpu.make_async_copy(wet_in, wet_tiles, load_sem.at[3 + chunks])
     coupling_load = pltpu.make_async_copy(coupling_in, coupling, load_sem.at[0])
     sea_load = pltpu.make_async_copy(sea_in, sea_mask, load_sem.at[1])
     boundary_load = pltpu.make_async_copy(boundary_in, boundary, load_sem.at[2])
@@ -103,6 +105,7 @@
     for j in order:
         previous_loads[j].start()
     boundary_load.start()
+    wet_load.start()
     for d in range(dirs):
         marks[d, 0:1] = jnp.full((1, marks.shape[2]), cross_gain[d], f32)
         marks[d, 1:2] = jnp.full((1, marks.shape[2]), quadrant[d].astype(f32), f32)
@@ -138,6 +141,8 @@
     sea_load.wait()
     coupling_load.wait()
     sea = sea_mask[...].astype(f32)
+    sea_field[...] = sea
+    back_rows[...] = back
     for d in range(dirs):
         onward, onward_gain = row_weights(coupling[d], sea, False)
         against, _ = row_weights(coupling[d], sea, True)
@@ -147,11 +152,21 @@
         barrier, 3 + len(neighbours) + (z > 0).astype(jnp.int32) + (z < depth - 1).astype(jnp.int32)
     )
 
-    stores = []
-
-    def keep(src, dst):
-        stores.append(pltpu.make_async_copy(src, dst, store_sem.at[len(stores)]))
-        stores[-1].start()
+    edge_copies = []
+    for way, (peer, start) in enumerate(((lower, 0), (higher, dirs - SHIFT))):
+        for i, (src, dst) in enumerate(
+            (
+                (coupling.at[pl.ds(start, SHIFT)], halo_coupling.at[way]),
+                (out.at[:, :, pl.ds(start, SHIFT)], halo_entering.at[way]),
+            )
+        ):
+            edge_copies.append(
+                pltpu.make_async_remote_copy(
+                    src_ref=src, dst_ref=dst,
+                    send_sem=edge_send.at[way, i], recv_sem=edge_recv.at[way, i],
+                    device_id={"dirs": peer}, device_id_type=MESH,
+                )
+            )
 
     halo_copies = []
     for way, (peer, start, to) in enumerate(((lower, 0, SHIFT), (higher, dirs - SHIFT, 0))):
@@ -173,8 +188,6 @@
 
     for copy in gain_copies:
         copy.start()
-    for way, start in enumerate((0, dirs - SHIFT)):
-        keep(coupling.at[pl.ds(start, SHIFT)], edges.at[way, 4])
 
     def compose(h, d, _):
         share = shares[d]
@@ -190,6 +203,8 @@
     for j in order:
         lax.fori_loop(j * size, (j + 1) * size, functools.partial(compose, half), 0)
     boundary_load.wait()
+    wet_load.wait()
+    wet_field(wet_tiles, wet)
     c_bit, x_bit = c.astype(f32), x.astype(f32)
     core_after = c_bit + back - 2.0 * c_bit * back
     pair_after = x_bit + back - 2.0 * x_bit * back
@@ -214,6 +229,14 @@
             cut(core_a, j)[None] * got_core[:, part(j)] + cut(core_b, j)[None] * state[half, :, part(j)]
         )
         pair_copies[j].start()
+    def local(d, _):
+        local_sweep(previous.at[d], coupling.at[d], back_rows.at[d], sea_field, cumulated.at[d], settled.at[d])
+        return 0
+
+    early = min(dirs, 4)
+    at_end = (z == 0) | (z == depth - 1)
+    middle = jnp.where(at_end, dirs, early)
+    lax.fori_loop(0, early, local, 0)
     upper = (2 * z >= depth).astype(jnp.int32)
     mine_at = 2 * half + x
 
@@ -260,7 +283,9 @@
         last_copies[j].start()
         out[half, :, part(j)] = cut(core_p, j)[None] * entering + cut(core_after, j)[None] * got_core[:, part(j)]
 
-    for i in range(2 * chunks + 1):
+    for i in range(2 * chunks + 2):
+        if i == chunks:
+            lax.fori_loop(early, middle, local, 0)
         if i < chunks:
             j = order[i]
             pair_copies[j].wait_recv()
@@ -269,20 +294,69 @@
         if chunks <= i < 2 * chunks:
             chain(order[i - chunks], 1 - upper)
             leave(order[i - chunks])
-        if chunks < i:
-            finish(order[i - chunks - 1])
-    for j in order:
-        last_copies[j].wait_recv()
-        keep(out.at[:, :, part(j)], entering_out.at[:, :, part(j)])
-        for way, (at, start) in enumerate(((0, 0), (chunks - 1, dirs - SHIFT))):
-            if j == at:
-                for h in range(2):
-                    keep(out.at[h, :, pl.ds(start, SHIFT)], edges.at[way, pl.ds(2 * h, 2)])
-    for copy in halo_copies:
+        if chunks + 2 <= i:
+            finish(order[i - chunks - 2])
+    lax.fori_loop(middle, dirs, local, 0)
+    def own_copy(d):
+        return pltpu.make_async_copy(rounded.at[d], own_out.at[d], own_sem.at[d])
+
+    def settled_copy(d):
+        return pltpu.make_async_copy(settled.at[d], settled_out.at[d], settled_sem.at[d])
+
+    def inner_copy(d):
+        return pltpu.make_async_copy(result.at[d], inner_out.at[d], inner_sem.at[d])
+
+    def own(d, _):
+        solve_free(
+            out.at[:, :, d], cumulated.at[d], marks.at[d], sea_field, rounded.at[d], settled.at[d]
+        )
+        own_copy(d).start()
+        settled_copy(d).start()
+        return 0
+
+    def inner(d, _):
+        source(
+            coef, rounded.at[d], rounded.at[d + SHIFT], rounded.at[d - SHIFT], settled.at[d], wet, result.at[d]
+        )
+        inner_copy(d).start()
+        return 0
+
+    def leave_own(d, _):
+        own_copy(d).wait()
+        settled_copy(d).wait()
+        return 0
+
+    def leave_inner(d, _):
+        inner_copy(d).wait()
+        return 0
+
+    def chunk(i, _):
+        j = (chunks - i) % chunks
+        remote(
+            core_out.at[:, part(j)], out.at[half, :, part(j)], last_send.at[j], last_recv.at[j], core_peer
+        ).wait_recv()
+
+        @pl.when(j == 0)
+        def _():
+            for copy in edge_copies[:2]:
+                copy.start()
+
+        @pl.when(j == chunks - 1)
+        def _():
+            for copy in edge_copies[2:]:
+                copy.start()
+
+        lax.fori_loop(j * size, (j + 1) * size, own, 0)
+        return 0
+
+    lax.fori_loop(0, chunks, chunk, 0)
+    if dirs > 2 * SHIFT:
+        lax.fori_loop(SHIFT, dirs - SHIFT, inner, 0)
+        lax.fori_loop(SHIFT, dirs - SHIFT, leave_inner, 0)
+    lax.fori_loop(0, dirs, leave_own, 0)
+    for copy in halo_copies + edge_copies:
         copy.wait_recv()
-    for store in stores:
-        store.wait()
-    for copy in halo_copies + gain_copies + core_copies + pair_copies + back_copies + last_copies:
+    for copy in halo_copies + edge_copies + gain_copies + core_copies + pair_copies + back_copies + last_copies:
         copy.wait_send()
 
     def drain(j, way):
@@ -300,7 +374,9 @@
         drain(j, 1)
 
 
-def scan_devices(count, dir_count, quadrant, cross_gain, boundary, sea_mask, previous, coupling):
+def scan_devices(
+    count, dir_count, quadrant, cross_gain, quad_coef, boundary, sea_mask, previous, coupling, wet_tiles
+):
     dirs, bands, rows, columns = previous.shape
     chunks = 4 if dirs % 4 == 0 else 3 if dirs % 3 == 0 else 1
     quarter = bands // 4
@@ -310,23 +386,35 @@
     part = (dirs, quarter, columns)
     dma = pltpu.SemaphoreType.DMA
     anywhere = pl.BlockSpec(memory_space=pl.ANY)
+    hbm = pl.BlockSpec(memory_space=pltpu.HBM)
     marks = (dirs, 2, 128)
 
     def halo(a):
         return jax.ShapeDtypeStruct((2 * SHIFT,) + a.shape[1:], a.dtype)
 
-    out, edges, *halos = pl.pallas_call(
+    return pl.pallas_call(
         functools.partial(scan_kernel, count, dir_count, chunks),
-        in_specs=[smem, smem] + [anywhere] * 4,
-        out_specs=[anywhere] * 4,
+        in_specs=[smem, smem, smem] + [hbm] * 5,
+        out_specs=[anywhere] * 7,
         out_shape=[
-            jax.ShapeDtypeStruct((2, 2) + part, f32),
-            jax.ShapeDtypeStruct((2, 5, SHIFT, quarter, columns), f32),
+            jax.ShapeDtypeStruct(previous.shape, bf16),
+            jax.ShapeDtypeStruct(previous.shape, f32),
+            jax.ShapeDtypeStruct(previous.shape, bf16),
             halo(previous),
+            jax.ShapeDtypeStruct((2, 2, 2, SHIFT, quarter, columns), f32),
+            jax.ShapeDtypeStruct((2, SHIFT, rows, columns), f32),
             jax.ShapeDtypeStruct((2 * SHIFT,) + marks[1:], f32),
         ],
         scratch_shapes=[
             pltpu.VMEM((2, 2) + part, f32),
+            pltpu.VMEM((dirs, 1, columns), f32),
+            pltpu.VMEM(coupling.shape, f32),
+            pltpu.VMEM(previous.shape, f32),
+            pltpu.VMEM(previous.shape, bf16),
+            pltpu.VMEM(previous.shape, bf16),
+            pltpu.VMEM(wet_tiles.shape, jnp.int32),
+            pltpu.VMEM(sea_mask.shape, f32),
+            pltpu.VMEM(sea_mask.shape, f32),
             pltpu.VMEM((dirs, 1, columns), f32),
             pltpu.VMEM((2, 2) + part, f32),
             pltpu.VMEM(coupling.shape, f32),
@@ -345,8 +433,7 @@
             pltpu.VMEM((2,) + part, f32),
             pltpu.VMEM(part, f32),
             pltpu.VMEM((2,) + part, f32),
-            dma((3 + chunks,)),
-            dma((6 + chunks,)),
+            dma((4 + chunks,)),
             dma((3,)), dma((3,)),
             dma((chunks,)), dma((chunks,)),
             dma((chunks,)), dma((chunks,)),
@@ -354,14 +441,116 @@
             dma((chunks,)), dma((chunks,)),
             dma((chunks,)), dma((chunks,)),
             dma((2, 2)), dma((2, 2)),
+            dma((2, 2)), dma((2, 2)),
+            dma((dirs,)), dma((dirs,)), dma((dirs,)),
         ],
         compiler_params=pltpu.CompilerParams(
             collective_id=0, has_side_effects=True, vmem_limit_bytes=SCAN_VMEM
         ),
         cost_estimate=cost(30),
         name="scan_devices",
-    )(quadrant, cross_gain, boundary, sea_mask, previous, coupling)
-    return out.reshape(4, dirs, quarter, columns), edges, halos
+    )(quadrant, cross_gain, quad_coef, boundary, sea_mask, previous, coupling, wet_tiles)
+
+
+def spans_of(couple, backward):
+    rows = couple.shape[0]
+    order = visit_order(couple.shape, backward)
+    spans, reach, span = [], couple, 1
+    while span < rows:
+        spans.append((span, jnp.where(order >= span, reach, 0.0)))
+        reach = jnp.where(order >= span, reach * rolled(reach, span, backward), reach)
+        span *= 2
+    return spans, reach
+
+
+def local_sweep(previous, coupling, back, sea, cumulated, local):
+    bands, rows, columns = previous.shape
+    for k in range(columns // BLOCK):
+        here = slice(k * BLOCK, (k + 1) * BLOCK)
+        couple, weight = weights(coupling[:, here], sea[:, here])
+        flag = jnp.broadcast_to(back[:, here], couple.shape) > 0.5
+        ways = [spans_of(couple, backward) for backward in (False, True)]
+        cumulated[:, here] = jnp.where(flag, ways[1][1], ways[0][1])
+        for f in range(bands):
+            start = weight * previous[f, :, here].astype(f32)
+            values = []
+            for backward in (False, True):
+                value = start
+                for span, factor in ways[backward][0]:
+                    value = value + factor * rolled(value, span, backward)
+                values.append(value)
+            local[f, :, here] = jnp.where(flag, values[1], values[0])
+
+
+def solve_free(entering, cumulated, marks, sea, rounded, settled):
+    bands, rows, columns = settled.shape
+    block = BLOCK
+    quarter = bands // 4
+    pieces = columns // block
+    gains, corner = marks[0:1], marks[1:2]
+    side = corner > 1.5
+    slope, scale = jnp.log(gains / (1.0 + gains)), 1.0 / (1.0 + gains)
+    row = lax.broadcasted_iota(jnp.int32, (block, block), 0)
+    column = lax.broadcasted_iota(jnp.int32, (block, block), 1)
+    sides = jnp.broadcast_to(side, (block, block))
+    offset = jnp.where(sides, row - column, column - row)
+    matrix = jnp.where(offset >= 0, jnp.exp(offset.astype(f32) * slope) * scale, 0.0)
+    lane = lax.broadcasted_iota(jnp.int32, (1, block), 1)
+    reach = jnp.where(side, block - 1 - lane, lane).astype(f32)
+    carry = gains * scale * jnp.exp(reach * slope)
+    carry_last = gains * scale * jnp.exp((block - 1) * slope)
+    high = matrix.astype(bf16)
+    low = (matrix - high.astype(f32)).astype(bf16)
+    whole = jnp.concatenate(
+        [
+            jnp.concatenate([high, low], axis=1),
+            jnp.concatenate([high, jnp.zeros_like(low)], axis=1),
+        ],
+        axis=0,
+    )
+    solved, ends = [], []
+    for k in range(pieces):
+        here = slice(k * block, (k + 1) * block)
+        growth = cumulated[:, here]
+        x = jnp.concatenate(
+            [
+                settled[f, :, here]
+                + growth * entering[f // quarter // 2, f // quarter % 2, f % quarter : f % quarter + 1, here]
+                for f in range(bands)
+            ],
+            axis=0,
+        )
+        upper = x.astype(bf16)
+        lower = (x - upper.astype(f32)).astype(bf16)
+        both = jnp.dot(
+            jnp.concatenate([upper, lower], axis=1), whole, preferred_element_type=f32
+        )
+        y = both[:, :block] + both[:, block:]
+        solved.append(y)
+        ends.append(
+            jnp.where(
+                jnp.broadcast_to(side, y.shape),
+                jnp.broadcast_to(y[:, :1], y.shape),
+                jnp.broadcast_to(y[:, block - 1 :], y.shape),
+            )
+        )
+    onward, against = [None] * pieces, [None] * pieces
+    for k in range(1, pieces):
+        onward[k] = ends[k - 1] if k == 1 else ends[k - 1] + carry_last * onward[k - 1]
+    for k in range(pieces - 2, -1, -1):
+        against[k] = ends[k + 1] if k == pieces - 2 else ends[k + 1] + carry_last * against[k + 1]
+    onward_carry = jnp.where(side, 0.0, carry)
+    against_carry = jnp.where(side, carry, 0.0)
+    for k in range(pieces):
+        here = slice(k * block, (k + 1) * block)
+        y = solved[k]
+        if k > 0:
+            y = y + onward[k] * onward_carry
+        if k < pieces - 1:
+            y = y + against[k] * against_carry
+        masked = y.reshape(bands, rows, block) * sea[:, here][None]
+        rounded[:, :, here] = masked.astype(bf16)
+        settled[:, :, here] = masked
 
 
 def settle_one(previous, coupling, inflow_of, gain, sea, rounded, settled, backward, sideways):
@@ -433,10 +622,13 @@
         )
 
 
-def wet_field(wet_tiles, wet):
+def wet_field(wet_columns, wet):
     rows, columns = wet.shape
+    row = lax.broadcasted_iota(jnp.int32, (rows, rows), 0)
+    column = lax.broadcasted_iota(jnp.int32, (rows, rows), 1)
     for k in range(columns // BLOCK):
-        flag = wet_tiles[:, k : k + 1].astype(f32)
+        flags = jnp.broadcast_to(wet_columns[k : k + 1].astype(f32), (rows, rows))
+        flag = jnp.sum(jnp.where(row == column, flags, 0.0), axis=1, keepdims=True)
         wet[:, k * BLOCK : (k + 1) * BLOCK] = jnp.broadcast_to(flag, (rows, BLOCK))
 
 
@@ -468,145 +660,111 @@
     lax.fori_loop(1, bands - 1, body, 0, unroll=True)
 
 
-def own_kernel(
-    quadrant, cross_gain, coef, sea_mask, wet_tiles, previous, coupling, entering, rounded, settled, *refs
+def source_kernel(
+    halo_marks, coef, sea_in, wet_in, previous_in, entering_in, coupling_in, own_in, settled_in, inner_in,
+    out, previous, entering, coupling, own, settled, halo, sea_mask, wet_tiles, sea, wet, result, bounce,
+    load_sem, own_sem, settled_sem, store_sem,
 ):
-    dirs = previous.shape[0]
-    *inner, sea, wet = refs
+    dirs, bands, rows, columns = own.shape
+    edge = [d for d in range(dirs) if d < SHIFT or d >= dirs - SHIFT]
+    near = [d for d in range(dirs) if d < 2 * SHIFT or d >= dirs - 2 * SHIFT]
+    small = [
+        pltpu.make_async_copy(src, dst, load_sem.at[i])
+        for i, (src, dst) in enumerate(
+            ((sea_in, sea_mask), (wet_in, wet_tiles), (coupling_in, coupling), (entering_in, entering), (previous_in, previous))
+        )
+    ]
+    own_loads = {d: pltpu.make_async_copy(own_in.at[d], own.at[d], own_sem.at[d]) for d in near}
+    settled_loads = [
+        pltpu.make_async_copy(settled_in.at[d], settled.at[i], settled_sem.at[i]) for i, d in enumerate(edge)
+    ]
+    stores = [pltpu.make_async_copy(result.at[i], out.at[d], store_sem.at[i]) for i, d in enumerate(edge)]
+    inner = []
+    if dirs > 2 * SHIFT:
+        middle = pl.ds(SHIFT, dirs - 2 * SHIFT)
+        inner.append(pltpu.make_async_copy(inner_in.at[middle], bounce, load_sem.at[5]))
+        stores.append(pltpu.make_async_copy(bounce, out.at[middle], store_sem.at[len(edge)]))
+    for load in small + list(own_loads.values()) + settled_loads + inner:
+        load.start()
+    for load in small[:2]:
+        load.wait()
     sea[...] = sea_mask[...].astype(f32)
     wet_field(wet_tiles, wet)
-
-    def one(d, _):
-        settle(
-            previous.at[d], coupling.at[d], lambda q, r, here: entering[q, d, r : r + 1, here],
-            quadrant[d], cross_gain[d], sea, rounded.at[d], settled.at[d],
-        )
-        return 0
-
-    def inner_source(d, _):
-        source(
-            coef, rounded.at[d], rounded.at[d + SHIFT], rounded.at[d - SHIFT], settled.at[d], wet,
-            inner[0].at[d - SHIFT],
-        )
-        return 0
-
-    lax.fori_loop(0, dirs, one, 0)
-    if inner:
-        lax.fori_loop(SHIFT, dirs - SHIFT, inner_source, 0)
-
-
-def settle_own(quadrant, cross_gain, quad_coef, sea_mask, wet_tiles, previous, coupling, entering):
-    dirs, bands, rows, columns = previous.shape
-    vmem = pl.BlockSpec(memory_space=pltpu.VMEM)
-    smem = pl.BlockSpec(memory_space=pltpu.SMEM)
-    out_shape = [
-        jax.ShapeDtypeStruct(previous.shape, bf16),
-        jax.ShapeDtypeStruct(previous.shape, f32),
-    ]
-    if dirs > 2 * SHIFT:
-        out_shape.append(jax.ShapeDtypeStruct((dirs - 2 * SHIFT,) + previous.shape[1:], bf16))
-    return pl.pallas_call(
-        own_kernel,
-        in_specs=[smem, smem, smem] + [vmem] * 5,
-        out_specs=[vmem] * len(out_shape),
-        out_shape=out_shape,
-        scratch_shapes=[
-            pltpu.VMEM((rows, columns), f32),
-            pltpu.VMEM((rows, columns), f32),
-        ],
-        compiler_params=pltpu.CompilerParams(vmem_limit_bytes=STEP_VMEM),
-        cost_estimate=cost(12),
-        name="settle_own",
-    )(quadrant, cross_gain, quad_coef, sea_mask, wet_tiles, previous, coupling, entering)
-
-
-def source_kernel(halo_marks, coef, sea_mask, wet_tiles, halo_previous, incoming_in, own, settled, *refs):
-    *inner, out, halo, incoming, sea, wet, result, load_sem, store_sem = refs
-    dirs, bands, rows, columns = settled.shape
-    load = pltpu.make_async_copy(incoming_in, incoming, load_sem.at[0])
-    load.start()
-    edge = [d for d in range(dirs) if d < SHIFT or d >= dirs - SHIFT]
-    stores = [pltpu.make_async_copy(result.at[i], out.at[d], store_sem.at[i]) for i, d in enumerate(edge)]
-    if inner:
-        copy = pltpu.make_async_copy(
-            inner[0], out.at[pl.ds(SHIFT, dirs - 2 * SHIFT)], store_sem.at[len(edge)]
-        )
-        copy.start()
-    sea[...] = sea_mask[...].astype(f32)
-    wet_field(wet_tiles, wet)
-    load.wait()
+    for load in small[2:]:
+        load.wait()
 
     def one_halo(t, _):
         way, at = 1 - t // SHIFT, t % SHIFT
         settle(
-            halo_previous.at[t], incoming.at[way, 4, at],
-            lambda q, r, here: incoming[way, q, at, r : r + 1, here],
+            previous.at[t], coupling.at[way, at],
+            lambda q, r, here: entering[way, q // 2, q % 2, at, r : r + 1, here],
             halo_marks[t, 1, 0].astype(jnp.int32), halo_marks[t, 0, 0], sea, halo.at[t], None,
         )
         return 0
 
     lax.fori_loop(0, 2 * SHIFT, one_halo, 0)
+    for load in inner:
+        load.wait()
+        stores[-1].start()
+    for load in list(own_loads.values()) + settled_loads:
+        load.wait()
     for i, d in enumerate(edge):
         source(
             coef, own.at[d],
             own.at[d + SHIFT] if d + SHIFT < dirs else halo.at[2 * SHIFT + d - dirs],
             own.at[d - SHIFT] if d >= SHIFT else halo.at[d],
-            settled.at[d], wet, result.at[i],
+            settled.at[i], wet, result.at[i],
         )
         stores[i].start()
     for store in stores:
         store.wait()
-    if inner:
-        copy.wait()
-
-
-def add_source(halo_marks, quad_coef, sea_mask, wet_tiles, halo_previous, incoming, rounded, settled, *inner):
+
+
+def add_source(
+    halo_marks, quad_coef, sea_mask, wet_tiles, halo_previous, halo_entering, halo_coupling, own, settled, inner
+):
     dirs, bands, rows, columns = settled.shape
-    vmem = pl.BlockSpec(memory_space=pltpu.VMEM)
     smem = pl.BlockSpec(memory_space=pltpu.SMEM)
     anywhere = pl.BlockSpec(memory_space=pl.ANY)
     edges = min(dirs, 2 * SHIFT)
+    dma = pltpu.SemaphoreType.DMA
     return pl.pallas_call(
         source_kernel,
-        in_specs=[smem, smem, vmem, vmem, vmem, anywhere, vmem, vmem] + [anywhere] * len(inner),
+        in_specs=[smem, smem] + [anywhere] * 8,
         out_specs=anywhere,
         out_shape=jax.ShapeDtypeStruct(settled.shape, bf16),
         scratch_shapes=[
-            pltpu.VMEM((2 * SHIFT, bands, rows, columns), bf16),
-            pltpu.VMEM(incoming.shape, f32),
+            pltpu.VMEM(halo_previous.shape, bf16),
+            pltpu.VMEM(halo_entering.shape, f32),
+            pltpu.VMEM(halo_coupling.shape, f32),
+            pltpu.VMEM(own.shape, bf16),
+            pltpu.VMEM((edges, bands, rows, columns), f32),
+            pltpu.VMEM(halo_previous.shape, bf16),
+            pltpu.VMEM(sea_mask.shape, jnp.int32),
+            pltpu.VMEM(wet_tiles.shape, jnp.int32),
             pltpu.VMEM((rows, columns), f32),
             pltpu.VMEM((rows, columns), f32),
             pltpu.VMEM((edges, bands, rows, columns), bf16),
-            pltpu.SemaphoreType.DMA((1,)),
-            pltpu.SemaphoreType.DMA((edges + 1,)),
+            pltpu.VMEM((max(dirs - 2 * SHIFT, 1), bands, rows, columns), bf16),
+            dma((6,)), dma((dirs,)), dma((edges,)), dma((edges + 1,)),
         ],
         compiler_params=pltpu.CompilerParams(vmem_limit_bytes=STEP_VMEM),
-        cost_estimate=cost(8),
+        cost_estimate=cost(6),
         name="add_source",
-    )(halo_marks, quad_coef, sea_mask, wet_tiles, halo_previous, incoming, rounded, settled, *inner)
-
-
-def exchange(edges, dir_count):
-    if dir_count == 2:
-        return lax.ppermute(edges, "dirs", [(0, 1), (1, 0)])
-    down = [(i, (i - 1) % dir_count) for i in range(dir_count)]
-    up = [(i, (i + 1) % dir_count) for i in range(dir_count)]
-    return jnp.stack([lax.ppermute(edges[0], "dirs", down), lax.ppermute(edges[1], "dirs", up)])
+    )(halo_marks, quad_coef, sea_mask, wet_tiles, halo_previous, halo_entering, halo_coupling, own, settled, inner)
 
 
 def on_device(
     row_devices, dir_devices,
     previous, boundary, row_coupling, cross_gain, block_inverse, quadrant, sea_mask, wet_tiles, quad_coef,
 ):
-    entering, edges, (halo_previous, halo_marks) = scan_devices(
-        row_devices, dir_devices, quadrant, cross_gain, boundary, sea_mask, previous, row_coupling
-    )
-    incoming = exchange(edges, dir_devices)
-    rounded, settled, *inner = settle_own(
-        quadrant, cross_gain, quad_coef, sea_mask, wet_tiles, previous, row_coupling, entering
+    wet_tiles = wet_tiles.T
+    own, settled, inner, halo_previous, halo_entering, halo_coupling, halo_marks = scan_devices(
+        row_devices, dir_devices, quadrant, cross_gain, quad_coef, boundary, sea_mask, previous, row_coupling,
+        wet_tiles,
     )
     return add_source(
-        halo_marks, quad_coef, sea_mask, wet_tiles, halo_previous, incoming, rounded, settled, *inner
+        halo_marks, quad_coef, sea_mask, wet_tiles, halo_previous, halo_entering, halo_coupling, own, settled, inner
     )
 
 

time: 49 us -> 46.9 us (0.957)
  starting transfers between devices: 1.81 us -> 0 us
  local copies, waits for them, and re-layouts: 1.32 us -> 0 us
  Pallas kernels: 45.5 us -> 46.6 us
    pallas_call x1, Pallas kernels: 31 us -> 39.6 us  [scan_devices(): pl.pallas_call(functools.partial(scan_kernel, count, dir_count, chunks),...]
    pallas_call x2 -> x1, Pallas kernels: 14.5 us -> 6.95 us  [add_source(): pl.pallas_call(source_kernel, in_specs=[smem, smem] + [anywhere] * 8, out...]
    ppermute x1 -> x0, starting transfers between devices: 1.81 us -> none  [exchange(): return lax.ppermute(edges, 'dirs', [(0, 1), (1, 0)])]
    unnamed x21 -> x0, local copies, waits for them, and re-layouts: 1.32 us -> none
  transfers between devices with their start and end apart: 1 -> 0, of which waited for: 0 -> 0; matrix products, arithmetic and copies ran while one was open for 0% -> 0% of each run, Pallas kernels for 18% -> 0%
where the time goes in v4:
time: 46.9 us; the launch traced here: 46.6 us
  Pallas kernels  46.6 us (99%)
    pallas_call x1, Pallas kernels, scan_devices(): pl.pallas_call(functools.partial(scan_kernel, count, dir_count, chunks),...  39.6 us
    pallas_call x1, Pallas kernels, add_source(): pl.pallas_call(source_kernel, in_specs=[smem, smem] + [anywhere] * 8, out...  6.95 us

profile of v4, /device:TPU:0, one launch (start us, length us, event | category | flops | bytes accessed | tf_op | source)
XLA Modules:
  0.0 46.6 jit_solution(8877243196487459529)
XLA Ops:
  0.0 39.6 %scan_devices.1 = (bf16[12,32,8,512]{3,2,1,0:T(8,128)(2,1)}, f32[12,32,8,512]{3,2,1,0:T(8,128)}, bf16[12,32,8,512]{3,2,1,0:T(8,128)(2,1)}, bf16[4,32,8,512]{3,2,...) custom-call(s32[12]{0:T(128)} %quadrant.1, f32[12]{0:T(128)} %cross_gain.1, ...), custom_call_target="tpu_custom_call" | custom-call | bytes 90000000 | tf_op jit(solution)/shard_map/scan_devices/pallas_call | solution.py:395
  39.6 7.0 %add_source.1 = bf16[12,32,8,512]{3,2,1,0:T(8,128)(2,1)} custom-call(f32[4,2,128]{2,1,0:T(2,128)} %get-tuple-element.12.halo_marks, f32[32]{0:T(128)} %coef.3, s32[8,512]{1,0:T(8,128)} %sea_in.3, s32[4,8]{1,0:T(4,128)} %bitcast.4, bf16[4,32,8,512]{3,2,1,0:T(8,128)(2,1)} %get-tuple-element.13.previous_in, ...), custom_call_target="tpu_custom_call" | custom-call | bytes 18000000 | tf_op jit(solution)/shard_map/add_source/pallas_call | solution.py:731

commit v5 on v4

--- a/solution.py
+++ b/solution.py
@@ -51,13 +51,13 @@
 
 def scan_kernel(
     count, dir_count, chunks, quadrant, cross_gain, coef, boundary_in, sea_in, previous_in, coupling_in, wet_in,
-    own_out, settled_out, inner_out, halo_previous, halo_entering, halo_coupling, halo_marks,
-    out, back_rows, cumulated, settled, rounded, result, wet_tiles, wet, sea_field,
+    own_out, rest_out, inner_out, halo_previous, halo_entering, halo_coupling, halo_marks,
+    out, rest, inflow, edge_state, back_rows, cumulated, settled, rounded, result, wet_tiles, wet, sea_field,
     gain, state, shares, marks, boundary, sea_mask, previous, coupling,
     gains, got_core, half_total, got_pair, plane, chain_in, chain_out, pair_in, pair_out, core_out,
     load_sem, gain_send, gain_recv, core_send, core_recv, pair_send, pair_recv,
     chain_send, chain_recv, back_send, back_recv, last_send, last_recv, halo_send, halo_recv,
-    edge_send, edge_recv, own_sem, settled_sem, inner_sem,
+    edge_send, edge_recv, own_sem, rest_sem, inner_sem,
 ):
     me = lax.axis_index("rows")
     c, x, z = me % 2, (me // 2) % 2, me // 4
@@ -154,19 +154,13 @@
 
     edge_copies = []
     for way, (peer, start) in enumerate(((lower, 0), (higher, dirs - SHIFT))):
-        for i, (src, dst) in enumerate(
-            (
-                (coupling.at[pl.ds(start, SHIFT)], halo_coupling.at[way]),
-                (out.at[:, :, pl.ds(start, SHIFT)], halo_entering.at[way]),
+        edge_copies.append(
+            pltpu.make_async_remote_copy(
+                src_ref=edge_state.at[way], dst_ref=halo_entering.at[way],
+                send_sem=edge_send.at[way], recv_sem=edge_recv.at[way],
+                device_id={"dirs": peer}, device_id_type=MESH,
             )
-        ):
-            edge_copies.append(
-                pltpu.make_async_remote_copy(
-                    src_ref=src, dst_ref=dst,
-                    send_sem=edge_send.at[way, i], recv_sem=edge_recv.at[way, i],
-                    device_id={"dirs": peer}, device_id_type=MESH,
-                )
-            )
+        )
 
     halo_copies = []
     for way, (peer, start, to) in enumerate(((lower, 0, SHIFT), (higher, dirs - SHIFT, 0))):
@@ -175,6 +169,7 @@
             (
                 (previous_in.at[pl.ds(start, SHIFT), bands], halo_previous.at[pl.ds(to, SHIFT), bands]),
                 (marks.at[pl.ds(start, SHIFT)], halo_marks.at[pl.ds(to, SHIFT)]),
+                (coupling_in.at[pl.ds(start, SHIFT)], halo_coupling.at[way]),
             )
         ):
             halo_copies.append(
@@ -230,7 +225,10 @@
         )
         pair_copies[j].start()
     def local(d, _):
-        local_sweep(previous.at[d], coupling.at[d], back_rows.at[d], sea_field, cumulated.at[d], settled.at[d])
+        side = jnp.where(marks[d, 1:2] > 1.5, 1.0, 0.0)
+        local_sweep(
+            previous.at[d], coupling.at[d], back_rows.at[d], side, sea_field, cumulated.at[d], settled.at[d]
+        )
         return 0
 
     early = min(dirs, 4)
@@ -297,37 +295,44 @@
         if chunks + 2 <= i:
             finish(order[i - chunks - 2])
     lax.fori_loop(middle, dirs, local, 0)
-    def own_copy(d):
-        return pltpu.make_async_copy(rounded.at[d], own_out.at[d], own_sem.at[d])
-
-    def settled_copy(d):
-        return pltpu.make_async_copy(settled.at[d], settled_out.at[d], settled_sem.at[d])
-
-    def inner_copy(d):
-        return pltpu.make_async_copy(result.at[d], inner_out.at[d], inner_sem.at[d])
+    def own_copy(j):
+        return pltpu.make_async_copy(rounded.at[part(j)], own_out.at[part(j)], own_sem.at[j])
+
+    rest_copy = pltpu.make_async_copy(rest, rest_out, rest_sem.at[0])
+
+    count = dirs - 2 * SHIFT
+    step = 2 if count % 2 == 0 else 1
+
+    def inner_copy(i):
+        piece = pl.ds(SHIFT + i * step, step)
+        return pltpu.make_async_copy(result.at[piece], inner_out.at[piece], inner_sem.at[i])
 
     def own(d, _):
         solve_free(
-            out.at[:, :, d], cumulated.at[d], marks.at[d], sea_field, rounded.at[d], settled.at[d]
-        )
-        own_copy(d).start()
-        settled_copy(d).start()
+            out.at[:, :, d], inflow, cumulated.at[d], marks.at[d], sea_field, rounded.at[d], settled.at[d]
+        )
         return 0
 
     def inner(d, _):
         source(
-            coef, rounded.at[d], rounded.at[d + SHIFT], rounded.at[d - SHIFT], settled.at[d], wet, result.at[d]
-        )
-        inner_copy(d).start()
+            coef, rounded.at[d], rounded.at[d + SHIFT], rounded.at[d - SHIFT], settled.at[d], None, wet,
+            result.at[d],
+        )
         return 0
 
-    def leave_own(d, _):
-        own_copy(d).wait()
-        settled_copy(d).wait()
+    def inner_piece(i, _):
+        lax.fori_loop(SHIFT + i * step, SHIFT + (i + 1) * step, inner, 0)
+        inner_copy(i).start()
         return 0
 
-    def leave_inner(d, _):
-        inner_copy(d).wait()
+    def edge_rest(i, _):
+        d = jnp.where(i < SHIFT, i, i + dirs - edges)
+
+        def band(f, _):
+            rest[i, f] = (settled[d, f] - rounded[d, f].astype(f32)).astype(bf16)
+            return 0
+
+        lax.fori_loop(0, bands, band, 0, unroll=8)
         return 0
 
     def chunk(i, _):
@@ -336,24 +341,28 @@
             core_out.at[:, part(j)], out.at[half, :, part(j)], last_send.at[j], last_recv.at[j], core_peer
         ).wait_recv()
 
-        @pl.when(j == 0)
-        def _():
-            for copy in edge_copies[:2]:
-                copy.start()
-
-        @pl.when(j == chunks - 1)
-        def _():
-            for copy in edge_copies[2:]:
-                copy.start()
+        for way, (at, start) in enumerate(((0, 0), (chunks - 1, dirs - SHIFT))):
+
+            @pl.when(j == at if size >= SHIFT else i == chunks - 1)
+            def _(way=way, start=start):
+                edge_state[way] = out[:, :, start : start + SHIFT].astype(bf16)
+                edge_copies[way].start()
 
         lax.fori_loop(j * size, (j + 1) * size, own, 0)
+        own_copy(j).start()
         return 0
 
     lax.fori_loop(0, chunks, chunk, 0)
-    if dirs > 2 * SHIFT:
-        lax.fori_loop(SHIFT, dirs - SHIFT, inner, 0)
-        lax.fori_loop(SHIFT, dirs - SHIFT, leave_inner, 0)
-    lax.fori_loop(0, dirs, leave_own, 0)
+    bands, edges = previous.shape[1], rest.shape[0]
+    lax.fori_loop(0, edges, edge_rest, 0)
+    rest_copy.start()
+    if count > 0:
+        lax.fori_loop(0, count // step, inner_piece, 0)
+        for i in range(count // step):
+            inner_copy(i).wait()
+    for j in range(chunks):
+        own_copy(j).wait()
+    rest_copy.wait()
     for copy in halo_copies + edge_copies:
         copy.wait_recv()
     for copy in halo_copies + edge_copies + gain_copies + core_copies + pair_copies + back_copies + last_copies:
@@ -398,15 +407,18 @@
         out_specs=[anywhere] * 7,
         out_shape=[
             jax.ShapeDtypeStruct(previous.shape, bf16),
-            jax.ShapeDtypeStruct(previous.shape, f32),
+            jax.ShapeDtypeStruct((min(dirs, 2 * SHIFT),) + previous.shape[1:], bf16),
             jax.ShapeDtypeStruct(previous.shape, bf16),
             halo(previous),
-            jax.ShapeDtypeStruct((2, 2, 2, SHIFT, quarter, columns), f32),
+            jax.ShapeDtypeStruct((2, 2, 2, SHIFT, quarter, columns), bf16),
             jax.ShapeDtypeStruct((2, SHIFT, rows, columns), f32),
             jax.ShapeDtypeStruct((2 * SHIFT,) + marks[1:], f32),
         ],
         scratch_shapes=[
             pltpu.VMEM((2, 2) + part, f32),
+            pltpu.VMEM((min(dirs, 2 * SHIFT),) + previous.shape[1:], bf16),
+            pltpu.VMEM((4, quarter, columns), f32),
+            pltpu.VMEM((2, 2, 2, SHIFT, quarter, columns), bf16),
             pltpu.VMEM((dirs, 1, columns), f32),
             pltpu.VMEM(coupling.shape, f32),
             pltpu.VMEM(previous.shape, f32),
@@ -440,8 +452,8 @@
             dma((2, chunks)), dma((2, chunks)),
             dma((chunks,)), dma((chunks,)),
             dma((chunks,)), dma((chunks,)),
-            dma((2, 2)), dma((2, 2)),
-            dma((2, 2)), dma((2, 2)),
+            dma((2, 3)), dma((2, 3)),
+            dma((2,)), dma((2,)),
             dma((dirs,)), dma((dirs,)), dma((dirs,)),
         ],
         compiler_params=pltpu.CompilerParams(
@@ -463,26 +475,39 @@
     return spans, reach
 
 
-def local_sweep(previous, coupling, back, sea, cumulated, local):
+def local_sweep(previous, coupling, back, side, sea, cumulated, local):
     bands, rows, columns = previous.shape
-    for k in range(columns // BLOCK):
-        here = slice(k * BLOCK, (k + 1) * BLOCK)
-        couple, weight = weights(coupling[:, here], sea[:, here])
-        flag = jnp.broadcast_to(back[:, here], couple.shape) > 0.5
-        ways = [spans_of(couple, backward) for backward in (False, True)]
-        cumulated[:, here] = jnp.where(flag, ways[1][1], ways[0][1])
+    pieces = columns // BLOCK
+
+    def blocks(f, here, weight, ways, flag):
+        start = weight * previous[f, :, here].astype(f32)
+        values = []
+        for backward in (False, True):
+            value = start
+            for span, factor in ways[backward][0]:
+                value = value + factor * rolled(value, span, backward)
+            values.append(value)
+        return jnp.where(flag, values[1], values[0])
+
+    shape = (rows, BLOCK)
+    flag = jnp.broadcast_to(back[:, :BLOCK], shape) > 0.5
+    sides = jnp.broadcast_to(side, shape) > 0.5
+    for k in range(pieces // 2):
+        pair = [slice(at * BLOCK, (at + 1) * BLOCK) for at in (k, pieces - 1 - k)]
+        held = []
+        for here in pair:
+            couple, weight = weights(coupling[:, here], sea[:, here])
+            ways = [spans_of(couple, backward) for backward in (False, True)]
+            held.append((weight, ways, jnp.where(flag, ways[1][1], ways[0][1])))
+        for at, here in enumerate(pair):
+            cumulated[:, here] = jnp.where(sides, held[1 - at][2], held[at][2])
         for f in range(bands):
-            start = weight * previous[f, :, here].astype(f32)
-            values = []
-            for backward in (False, True):
-                value = start
-                for span, factor in ways[backward][0]:
-                    value = value + factor * rolled(value, span, backward)
-                values.append(value)
-            local[f, :, here] = jnp.where(flag, values[1], values[0])
-
-
-def solve_free(entering, cumulated, marks, sea, rounded, settled):
+            values = [blocks(f, here, *held[at][:2], flag) for at, here in enumerate(pair)]
+            for at, here in enumerate(pair):
+                local[f, :, here] = jnp.where(sides, values[1 - at], values[at])
+
+
+def solve_free(entering, inflow, cumulated, marks, sea, rounded, settled):
     bands, rows, columns = settled.shape
     block = BLOCK
     quarter = bands // 4
@@ -508,14 +533,22 @@
         ],
         axis=0,
     )
-    solved, ends = [], []
+    pairs = [
+        [slice(at * block, (at + 1) * block) for at in (k, pieces - 1 - k)] for k in range(pieces // 2)
+    ]
+    flip = jnp.broadcast_to(side, (quarter, block))
+    for q in range(4):
+        for pair in pairs:
+            values = [entering[q // 2, q % 2, :, here] for here in pair]
+            for at, here in enumerate(pair):
+                inflow[q, :, here] = jnp.where(flip, values[1 - at], values[at])
+    before = None
     for k in range(pieces):
         here = slice(k * block, (k + 1) * block)
         growth = cumulated[:, here]
         x = jnp.concatenate(
             [
-                settled[f, :, here]
-                + growth * entering[f // quarter // 2, f // quarter % 2, f % quarter : f % quarter + 1, here]
+                settled[f, :, here] + growth * inflow[f // quarter, f % quarter : f % quarter + 1, here]
                 for f in range(bands)
             ],
             axis=0,
@@ -526,31 +559,26 @@
             jnp.concatenate([upper, lower], axis=1), whole, preferred_element_type=f32
         )
         y = both[:, :block] + both[:, block:]
-        solved.append(y)
-        ends.append(
-            jnp.where(
+        if k < pieces - 1:
+            last = jnp.where(
                 jnp.broadcast_to(side, y.shape),
                 jnp.broadcast_to(y[:, :1], y.shape),
                 jnp.broadcast_to(y[:, block - 1 :], y.shape),
             )
-        )
-    onward, against = [None] * pieces, [None] * pieces
-    for k in range(1, pieces):
-        onward[k] = ends[k - 1] if k == 1 else ends[k - 1] + carry_last * onward[k - 1]
-    for k in range(pieces - 2, -1, -1):
-        against[k] = ends[k + 1] if k == pieces - 2 else ends[k + 1] + carry_last * against[k + 1]
-    onward_carry = jnp.where(side, 0.0, carry)
-    against_carry = jnp.where(side, carry, 0.0)
-    for k in range(pieces):
-        here = slice(k * block, (k + 1) * block)
-        y = solved[k]
-        if k > 0:
-            y = y + onward[k] * onward_carry
-        if k < pieces - 1:
-            y = y + against[k] * against_carry
-        masked = y.reshape(bands, rows, block) * sea[:, here][None]
-        rounded[:, :, here] = masked.astype(bf16)
-        settled[:, :, here] = masked
+        if before is not None:
+            y = y + before * carry
+            last = last + before * carry_last
+        before = last
+        settled[:, :, here] = y.reshape(bands, rows, block)
+    flip = jnp.broadcast_to(side, (rows, block))
+    for pair in pairs:
+        field = [sea[:, here] for here in pair]
+        for f in range(bands):
+            values = [settled[f, :, here] for here in pair]
+            for at, here in enumerate(pair):
+                masked = jnp.where(flip, values[1 - at], values[at]) * field[at]
+                settled[f, :, here] = masked
+                rounded[f, :, here] = masked.astype(bf16)
 
 
 def settle_one(previous, coupling, inflow_of, gain, sea, rounded, settled, backward, sideways):
@@ -632,7 +660,7 @@
         wet[:, k * BLOCK : (k + 1) * BLOCK] = jnp.broadcast_to(flag, (rows, BLOCK))
 
 
-def source(coef, own, onward_of, against_of, settled, wet, result):
+def source(coef, own, onward_of, against_of, settled, rest, wet, result):
     bands = own.shape[0]
     wet_cells = wet[...]
 
@@ -641,7 +669,8 @@
         value = coef[f] * (
             energy * energy * (onward + against) - 2.0 * energy * onward * against
         )
-        result[f] = (settled[f] + wet_cells * value.astype(bf16).astype(f32)).astype(bf16)
+        base = settled[f] if rest is None else energy + rest[f].astype(f32)
+        result[f] = (base + wet_cells * value.astype(bf16).astype(f32)).astype(bf16)
 
     def above(f):
         return onward_of[f + 1].astype(f32)
@@ -661,37 +690,44 @@
 
 
 def source_kernel(
-    halo_marks, coef, sea_in, wet_in, previous_in, entering_in, coupling_in, own_in, settled_in, inner_in,
-    out, previous, entering, coupling, own, settled, halo, sea_mask, wet_tiles, sea, wet, result, bounce,
-    load_sem, own_sem, settled_sem, store_sem,
+    halo_marks, coef, sea_in, wet_in, previous_in, entering_in, coupling_in, own_in, rest_in, inner_in,
+    out, previous, incoming, entering, coupling, own, rest, halo, sea_mask, wet_tiles, sea, wet, result, bounce,
+    load_sem, store_sem,
 ):
     dirs, bands, rows, columns = own.shape
     edge = [d for d in range(dirs) if d < SHIFT or d >= dirs - SHIFT]
-    near = [d for d in range(dirs) if d < 2 * SHIFT or d >= dirs - 2 * SHIFT]
     small = [
         pltpu.make_async_copy(src, dst, load_sem.at[i])
         for i, (src, dst) in enumerate(
-            ((sea_in, sea_mask), (wet_in, wet_tiles), (coupling_in, coupling), (entering_in, entering), (previous_in, previous))
-        )
-    ]
-    own_loads = {d: pltpu.make_async_copy(own_in.at[d], own.at[d], own_sem.at[d]) for d in near}
-    settled_loads = [
-        pltpu.make_async_copy(settled_in.at[d], settled.at[i], settled_sem.at[i]) for i, d in enumerate(edge)
-    ]
-    stores = [pltpu.make_async_copy(result.at[i], out.at[d], store_sem.at[i]) for i, d in enumerate(edge)]
+            ((sea_in, sea_mask), (wet_in, wet_tiles), (coupling_in, coupling), (entering_in, incoming))
+        )
+    ]
+    previous_load = pltpu.make_async_copy(previous_in, previous, load_sem.at[4])
+    late = [
+        pltpu.make_async_copy(own_in, own, load_sem.at[5]),
+        pltpu.make_async_copy(rest_in, rest, load_sem.at[6]),
+    ]
+    runs = [(0, 0, len(edge))] if dirs <= 2 * SHIFT else [(0, 0, SHIFT), (SHIFT, dirs - SHIFT, SHIFT)]
+    stores = [
+        pltpu.make_async_copy(result.at[pl.ds(at, n)], out.at[pl.ds(d, n)], store_sem.at[k])
+        for k, (at, d, n) in enumerate(runs)
+    ]
     inner = []
     if dirs > 2 * SHIFT:
         middle = pl.ds(SHIFT, dirs - 2 * SHIFT)
-        inner.append(pltpu.make_async_copy(inner_in.at[middle], bounce, load_sem.at[5]))
-        stores.append(pltpu.make_async_copy(bounce, out.at[middle], store_sem.at[len(edge)]))
-    for load in small + list(own_loads.values()) + settled_loads + inner:
+        inner = [
+            pltpu.make_async_copy(inner_in.at[middle], bounce, load_sem.at[7]),
+            pltpu.make_async_copy(bounce, out.at[middle], store_sem.at[2]),
+        ]
+    for load in small:
         load.start()
-    for load in small[:2]:
+    for load in [previous_load] + late + inner[:1]:
+        load.start()
+    for load in small:
         load.wait()
     sea[...] = sea_mask[...].astype(f32)
     wet_field(wet_tiles, wet)
-    for load in small[2:]:
-        load.wait()
+    entering[...] = incoming[...].astype(f32)
 
     def one_halo(t, _):
         way, at = 1 - t // SHIFT, t % SHIFT
@@ -702,28 +738,31 @@
         )
         return 0
 
+    previous_load.wait()
     lax.fori_loop(0, 2 * SHIFT, one_halo, 0)
-    for load in inner:
-        load.wait()
-        stores[-1].start()
-    for load in list(own_loads.values()) + settled_loads:
+    if inner:
+        inner[0].wait()
+        inner[1].start()
+    for load in late:
         load.wait()
     for i, d in enumerate(edge):
         source(
             coef, own.at[d],
             own.at[d + SHIFT] if d + SHIFT < dirs else halo.at[2 * SHIFT + d - dirs],
             own.at[d - SHIFT] if d >= SHIFT else halo.at[d],
-            settled.at[i], wet, result.at[i],
-        )
-        stores[i].start()
-    for store in stores:
+            None, rest.at[i], wet, result.at[i],
+        )
+        for store, run in zip(stores, runs):
+            if i == run[0] + run[2] - 1:
+                store.start()
+    for store in stores + inner[1:]:
         store.wait()
 
 
 def add_source(
-    halo_marks, quad_coef, sea_mask, wet_tiles, halo_previous, halo_entering, halo_coupling, own, settled, inner
+    halo_marks, quad_coef, sea_mask, wet_tiles, halo_previous, halo_entering, halo_coupling, own, rest, inner
 ):
-    dirs, bands, rows, columns = settled.shape
+    dirs, bands, rows, columns = own.shape
     smem = pl.BlockSpec(memory_space=pltpu.SMEM)
     anywhere = pl.BlockSpec(memory_space=pl.ANY)
     edges = min(dirs, 2 * SHIFT)
@@ -732,13 +771,14 @@
         source_kernel,
         in_specs=[smem, smem] + [anywhere] * 8,
         out_specs=anywhere,
-        out_shape=jax.ShapeDtypeStruct(settled.shape, bf16),
+        out_shape=jax.ShapeDtypeStruct(own.shape, bf16),
         scratch_shapes=[
             pltpu.VMEM(halo_previous.shape, bf16),
+            pltpu.VMEM(halo_entering.shape, bf16),
             pltpu.VMEM(halo_entering.shape, f32),
             pltpu.VMEM(halo_coupling.shape, f32),
             pltpu.VMEM(own.shape, bf16),
-            pltpu.VMEM((edges, bands, rows, columns), f32),
+            pltpu.VMEM((edges, bands, rows, columns), bf16),
             pltpu.VMEM(halo_previous.shape, bf16),
             pltpu.VMEM(sea_mask.shape, jnp.int32),
             pltpu.VMEM(wet_tiles.shape, jnp.int32),
@@ -746,12 +786,12 @@
             pltpu.VMEM((rows, columns), f32),
             pltpu.VMEM((edges, bands, rows, columns), bf16),
             pltpu.VMEM((max(dirs - 2 * SHIFT, 1), bands, rows, columns), bf16),
-            dma((6,)), dma((dirs,)), dma((edges,)), dma((edges + 1,)),
+            dma((8,)), dma((3,)),
         ],
         compiler_params=pltpu.CompilerParams(vmem_limit_bytes=STEP_VMEM),
         cost_estimate=cost(6),
         name="add_source",
-    )(halo_marks, quad_coef, sea_mask, wet_tiles, halo_previous, halo_entering, halo_coupling, own, settled, inner)
+    )(halo_marks, quad_coef, sea_mask, wet_tiles, halo_previous, halo_entering, halo_coupling, own, rest, inner)
 
 
 def on_device(
@@ -759,12 +799,12 @@
     previous, boundary, row_coupling, cross_gain, block_inverse, quadrant, sea_mask, wet_tiles, quad_coef,
 ):
     wet_tiles = wet_tiles.T
-    own, settled, inner, halo_previous, halo_entering, halo_coupling, halo_marks = scan_devices(
+    own, rest, inner, halo_previous, halo_entering, halo_coupling, halo_marks = scan_devices(
         row_devices, dir_devices, quadrant, cross_gain, quad_coef, boundary, sea_mask, previous, row_coupling,
         wet_tiles,
     )
     return add_source(
-        halo_marks, quad_coef, sea_mask, wet_tiles, halo_previous, halo_entering, halo_coupling, own, settled, inner
+        halo_marks, quad_coef, sea_mask, wet_tiles, halo_previous, halo_entering, halo_coupling, own, rest, inner
     )
 
 

time: 46.9 us -> 45.8 us (0.977)
  Pallas kernels: 46.6 us -> 45.4 us
    pallas_call x1, Pallas kernels: 6.95 us -> 6.22 us  [add_source(): pl.pallas_call(source_kernel, in_specs=[smem, smem] + [anywhere] * 8, out...]
    pallas_call x1, Pallas kernels: 39.6 us -> 39.2 us  [scan_devices(): pl.pallas_call(functools.partial(scan_kernel, count, dir_count, chunks),...]
where the time goes in v5:
time: 45.8 us; the launch traced here: 45.4 us
  Pallas kernels  45.4 us (99%)
    pallas_call x1, Pallas kernels, scan_devices(): pl.pallas_call(functools.partial(scan_kernel, count, dir_count, chunks),...  39.2 us
    pallas_call x1, Pallas kernels, add_source(): pl.pallas_call(source_kernel, in_specs=[smem, smem] + [anywhere] * 8, out...  6.22 us

profile of v5, /device:TPU:0, one launch (start us, length us, event | category | flops | bytes accessed | tf_op | source)
XLA Modules:
  0.0 45.4 jit_solution(6927058905037712056)
XLA Ops:
  0.0 39.2 %scan_devices.1 = (bf16[12,32,8,512]{3,2,1,0:T(8,128)(2,1)}, bf16[4,32,8,512]{3,2,1,0:T(8,128)(2,1)}, bf16[12,32,8,512]{3,2,1,0:T(8,128)(2,1)}, bf16[4,32,8,512]...) custom-call(s32[12]{0:T(128)} %quadrant.1, ...), custom_call_target="tpu_custom_call" | custom-call | bytes 90000000 | tf_op jit(solution)/shard_map/scan_devices/pallas_call | solution.py:404
  39.2 6.2 %add_source.1 = bf16[12,32,8,512]{3,2,1,0:T(8,128)(2,1)} custom-call(f32[4,2,128]{2,1,0:T(2,128)} %get-tuple-element.12.halo_marks, f32[32]{0:T(128)} %coef.3, s32[8,512]{1,0:T(8,128)} %sea_in.3, s32[4,8]{1,0:T(4,128)} %bitcast.4, bf16[4,32,8,512]{3,2,1,0:T(8,128)(2,1)} %get-tuple-element.13.previous_in, ...), custom_call_target="tpu_custom_call" | custom-call | bytes 18000000 | tf_op jit(solution)/shard_map/add_source/pallas_call | solution.py:770

commit v6 on v5

--- a/solution.py
+++ b/solution.py
@@ -50,14 +50,14 @@
 
 
 def scan_kernel(
-    count, dir_count, chunks, quadrant, cross_gain, coef, boundary_in, sea_in, previous_in, coupling_in, wet_in,
-    own_out, rest_out, inner_out, halo_previous, halo_entering, halo_coupling, halo_marks,
-    out, rest, inflow, edge_state, back_rows, cumulated, settled, rounded, result, wet_tiles, wet, sea_field,
+    count, dir_count, chunks, quadrant, cross_gain, boundary_in, sea_in, previous_in, coupling_in,
+    own_out, rest_out, halo_previous, halo_entering, halo_coupling, halo_marks,
+    out, rest, inflow, edge_state, back_rows, cumulated, settled, rounded, sea_field,
     gain, state, shares, marks, boundary, sea_mask, previous, coupling,
     gains, got_core, half_total, got_pair, plane, chain_in, chain_out, pair_in, pair_out, core_out,
     load_sem, gain_send, gain_recv, core_send, core_recv, pair_send, pair_recv,
     chain_send, chain_recv, back_send, back_recv, last_send, last_recv, halo_send, halo_recv,
-    edge_send, edge_recv, own_sem, rest_sem, inner_sem,
+    edge_send, edge_recv, own_sem, rest_sem,
 ):
     me = lax.axis_index("rows")
     c, x, z = me % 2, (me // 2) % 2, me // 4
@@ -92,7 +92,6 @@
         pl.semaphore_signal(barrier, inc=1, device_id={"dirs": peer}, device_id_type=MESH)
 
     order = [0] + list(range(chunks - 1, 0, -1))
-    wet_load = pltpu.make_async_copy(wet_in, wet_tiles, load_sem.at[3 + chunks])
     coupling_load = pltpu.make_async_copy(coupling_in, coupling, load_sem.at[0])
     sea_load = pltpu.make_async_copy(sea_in, sea_mask, load_sem.at[1])
     boundary_load = pltpu.make_async_copy(boundary_in, boundary, load_sem.at[2])
@@ -105,7 +104,6 @@
     for j in order:
         previous_loads[j].start()
     boundary_load.start()
-    wet_load.start()
     for d in range(dirs):
         marks[d, 0:1] = jnp.full((1, marks.shape[2]), cross_gain[d], f32)
         marks[d, 1:2] = jnp.full((1, marks.shape[2]), quadrant[d].astype(f32), f32)
@@ -198,8 +196,6 @@
     for j in order:
         lax.fori_loop(j * size, (j + 1) * size, functools.partial(compose, half), 0)
     boundary_load.wait()
-    wet_load.wait()
-    wet_field(wet_tiles, wet)
     c_bit, x_bit = c.astype(f32), x.astype(f32)
     core_after = c_bit + back - 2.0 * c_bit * back
     pair_after = x_bit + back - 2.0 * x_bit * back
@@ -231,7 +227,7 @@
         )
         return 0
 
-    early = min(dirs, 4)
+    early = min(dirs, 7)
     at_end = (z == 0) | (z == depth - 1)
     middle = jnp.where(at_end, dirs, early)
     lax.fori_loop(0, early, local, 0)
@@ -298,41 +294,13 @@
     def own_copy(j):
         return pltpu.make_async_copy(rounded.at[part(j)], own_out.at[part(j)], own_sem.at[j])
 
-    rest_copy = pltpu.make_async_copy(rest, rest_out, rest_sem.at[0])
-
-    count = dirs - 2 * SHIFT
-    step = 2 if count % 2 == 0 else 1
-
-    def inner_copy(i):
-        piece = pl.ds(SHIFT + i * step, step)
-        return pltpu.make_async_copy(result.at[piece], inner_out.at[piece], inner_sem.at[i])
+    def rest_copy(j):
+        return pltpu.make_async_copy(rest.at[part(j)], rest_out.at[part(j)], rest_sem.at[j])
 
     def own(d, _):
         solve_free(
-            out.at[:, :, d], inflow, cumulated.at[d], marks.at[d], sea_field, rounded.at[d], settled.at[d]
-        )
-        return 0
-
-    def inner(d, _):
-        source(
-            coef, rounded.at[d], rounded.at[d + SHIFT], rounded.at[d - SHIFT], settled.at[d], None, wet,
-            result.at[d],
-        )
-        return 0
-
-    def inner_piece(i, _):
-        lax.fori_loop(SHIFT + i * step, SHIFT + (i + 1) * step, inner, 0)
-        inner_copy(i).start()
-        return 0
-
-    def edge_rest(i, _):
-        d = jnp.where(i < SHIFT, i, i + dirs - edges)
-
-        def band(f, _):
-            rest[i, f] = (settled[d, f] - rounded[d, f].astype(f32)).astype(bf16)
-            return 0
-
-        lax.fori_loop(0, bands, band, 0, unroll=8)
+            out.at[:, :, d], inflow, cumulated.at[d], marks.at[d], sea_field, settled.at[d], rounded.at[d], rest.at[d]
+        )
         return 0
 
     def chunk(i, _):
@@ -350,19 +318,13 @@
 
         lax.fori_loop(j * size, (j + 1) * size, own, 0)
         own_copy(j).start()
+        rest_copy(j).start()
         return 0
 
     lax.fori_loop(0, chunks, chunk, 0)
-    bands, edges = previous.shape[1], rest.shape[0]
-    lax.fori_loop(0, edges, edge_rest, 0)
-    rest_copy.start()
-    if count > 0:
-        lax.fori_loop(0, count // step, inner_piece, 0)
-        for i in range(count // step):
-            inner_copy(i).wait()
     for j in range(chunks):
         own_copy(j).wait()
-    rest_copy.wait()
+        rest_copy(j).wait()
     for copy in halo_copies + edge_copies:
         copy.wait_recv()
     for copy in halo_copies + edge_copies + gain_copies + core_copies + pair_copies + back_copies + last_copies:
@@ -384,7 +346,7 @@
 
 
 def scan_devices(
-    count, dir_count, quadrant, cross_gain, quad_coef, boundary, sea_mask, previous, coupling, wet_tiles
+    count, dir_count, quadrant, cross_gain, boundary, sea_mask, previous, coupling
 ):
     dirs, bands, rows, columns = previous.shape
     chunks = 4 if dirs % 4 == 0 else 3 if dirs % 3 == 0 else 1
@@ -403,11 +365,10 @@
 
     return pl.pallas_call(
         functools.partial(scan_kernel, count, dir_count, chunks),
-        in_specs=[smem, smem, smem] + [hbm] * 5,
-        out_specs=[anywhere] * 7,
+        in_specs=[smem, smem] + [hbm] * 4,
+        out_specs=[anywhere] * 6,
         out_shape=[
             jax.ShapeDtypeStruct(previous.shape, bf16),
-            jax.ShapeDtypeStruct((min(dirs, 2 * SHIFT),) + previous.shape[1:], bf16),
             jax.ShapeDtypeStruct(previous.shape, bf16),
             halo(previous),
             jax.ShapeDtypeStruct((2, 2, 2, SHIFT, quarter, columns), bf16),
@@ -416,16 +377,13 @@
         ],
         scratch_shapes=[
             pltpu.VMEM((2, 2) + part, f32),
-            pltpu.VMEM((min(dirs, 2 * SHIFT),) + previous.shape[1:], bf16),
+            pltpu.VMEM(previous.shape, bf16),
             pltpu.VMEM((4, quarter, columns), f32),
             pltpu.VMEM((2, 2, 2, SHIFT, quarter, columns), bf16),
             pltpu.VMEM((dirs, 1, columns), f32),
             pltpu.VMEM(coupling.shape, f32),
             pltpu.VMEM(previous.shape, f32),
             pltpu.VMEM(previous.shape, bf16),
-            pltpu.VMEM(previous.shape, bf16),
-            pltpu.VMEM(wet_tiles.shape, jnp.int32),
-            pltpu.VMEM(sea_mask.shape, f32),
             pltpu.VMEM(sea_mask.shape, f32),
             pltpu.VMEM((dirs, 1, columns), f32),
             pltpu.VMEM((2, 2) + part, f32),
@@ -445,7 +403,7 @@
             pltpu.VMEM((2,) + part, f32),
             pltpu.VMEM(part, f32),
             pltpu.VMEM((2,) + part, f32),
-            dma((4 + chunks,)),
+            dma((3 + chunks,)),
             dma((3,)), dma((3,)),
             dma((chunks,)), dma((chunks,)),
             dma((chunks,)), dma((chunks,)),
@@ -454,14 +412,14 @@
             dma((chunks,)), dma((chunks,)),
             dma((2, 3)), dma((2, 3)),
             dma((2,)), dma((2,)),
-            dma((dirs,)), dma((dirs,)), dma((dirs,)),
+            dma((chunks,)), dma((chunks,)),
         ],
         compiler_params=pltpu.CompilerParams(
             collective_id=0, has_side_effects=True, vmem_limit_bytes=SCAN_VMEM
         ),
         cost_estimate=cost(30),
         name="scan_devices",
-    )(quadrant, cross_gain, quad_coef, boundary, sea_mask, previous, coupling, wet_tiles)
+    )(quadrant, cross_gain, boundary, sea_mask, previous, coupling)
 
 
 def spans_of(couple, backward):
@@ -507,7 +465,7 @@
                 local[f, :, here] = jnp.where(sides, values[1 - at], values[at])
 
 
-def solve_free(entering, inflow, cumulated, marks, sea, rounded, settled):
+def solve_free(entering, inflow, cumulated, marks, sea, settled, rounded, rest):
     bands, rows, columns = settled.shape
     block = BLOCK
     quarter = bands // 4
@@ -577,8 +535,9 @@
             values = [settled[f, :, here] for here in pair]
             for at, here in enumerate(pair):
                 masked = jnp.where(flip, values[1 - at], values[at]) * field[at]
-                settled[f, :, here] = masked
-                rounded[f, :, here] = masked.astype(bf16)
+                near = masked.astype(bf16)
+                rounded[f, :, here] = near
+                rest[f, :, here] = (masked - near.astype(f32)).astype(bf16)
 
 
 def settle_one(previous, coupling, inflow_of, gain, sea, rounded, settled, backward, sideways):
@@ -660,7 +619,7 @@
         wet[:, k * BLOCK : (k + 1) * BLOCK] = jnp.broadcast_to(flag, (rows, BLOCK))
 
 
-def source(coef, own, onward_of, against_of, settled, rest, wet, result):
+def source(coef, own, onward_of, against_of, rest, wet, result):
     bands = own.shape[0]
     wet_cells = wet[...]
 
@@ -669,7 +628,7 @@
         value = coef[f] * (
             energy * energy * (onward + against) - 2.0 * energy * onward * against
         )
-        base = settled[f] if rest is None else energy + rest[f].astype(f32)
+        base = energy + rest[f].astype(f32)
         result[f] = (base + wet_cells * value.astype(bf16).astype(f32)).astype(bf16)
 
     def above(f):
@@ -690,12 +649,15 @@
 
 
 def source_kernel(
-    halo_marks, coef, sea_in, wet_in, previous_in, entering_in, coupling_in, own_in, rest_in, inner_in,
-    out, previous, incoming, entering, coupling, own, rest, halo, sea_mask, wet_tiles, sea, wet, result, bounce,
-    load_sem, store_sem,
+    marks_in, coef_in, sea_in, wet_in, previous_in, entering_in, coupling_in, own_in, rest_in,
+    out, halo_marks, coef, previous, incoming, entering, coupling, own, rest, halo, sea_mask, wet_tiles, sea, wet, result,
+    load_sem, scalar_sem, store_sem,
 ):
     dirs, bands, rows, columns = own.shape
-    edge = [d for d in range(dirs) if d < SHIFT or d >= dirs - SHIFT]
+    scalars = [
+        pltpu.make_async_copy(marks_in, halo_marks, scalar_sem.at[0]),
+        pltpu.make_async_copy(coef_in, coef, scalar_sem.at[1]),
+    ]
     small = [
         pltpu.make_async_copy(src, dst, load_sem.at[i])
         for i, (src, dst) in enumerate(
@@ -703,27 +665,31 @@
         )
     ]
     previous_load = pltpu.make_async_copy(previous_in, previous, load_sem.at[4])
+    cut = dirs // 2 if dirs > 2 * SHIFT else dirs
     late = [
-        pltpu.make_async_copy(own_in, own, load_sem.at[5]),
-        pltpu.make_async_copy(rest_in, rest, load_sem.at[6]),
-    ]
-    runs = [(0, 0, len(edge))] if dirs <= 2 * SHIFT else [(0, 0, SHIFT), (SHIFT, dirs - SHIFT, SHIFT)]
+        pltpu.make_async_copy(whole.at[pl.ds(0, to)], held.at[pl.ds(0, to)], load_sem.at[i])
+        for i, (whole, held, to) in enumerate(((own_in, own, min(cut + SHIFT, dirs)), (rest_in, rest, cut)), 5)
+    ]
+    latest = [
+        pltpu.make_async_copy(whole.at[pl.ds(at, dirs - at)], held.at[pl.ds(at, dirs - at)], load_sem.at[i])
+        for i, (whole, held, at) in enumerate(((own_in, own, cut + SHIFT), (rest_in, rest, cut)), 7)
+        if at < dirs
+    ]
+    if dirs > 2 * SHIFT:
+        bounds = [0, SHIFT, dirs // 2, dirs - SHIFT, dirs - 1, dirs]
+    else:
+        bounds = list(range(dirs + 1))
     stores = [
-        pltpu.make_async_copy(result.at[pl.ds(at, n)], out.at[pl.ds(d, n)], store_sem.at[k])
-        for k, (at, d, n) in enumerate(runs)
-    ]
-    inner = []
-    if dirs > 2 * SHIFT:
-        middle = pl.ds(SHIFT, dirs - 2 * SHIFT)
-        inner = [
-            pltpu.make_async_copy(inner_in.at[middle], bounce, load_sem.at[7]),
-            pltpu.make_async_copy(bounce, out.at[middle], store_sem.at[2]),
-        ]
-    for load in small:
+        pltpu.make_async_copy(
+            result.at[pl.ds(at, to - at)], out.at[pl.ds(at, to - at)], store_sem.at[k]
+        )
+        for k, (at, to) in enumerate(zip(bounds, bounds[1:]))
+    ]
+    for load in small + scalars:
         load.start()
-    for load in [previous_load] + late + inner[:1]:
+    for load in [previous_load] + late + latest:
         load.start()
-    for load in small:
+    for load in small + scalars:
         load.wait()
     sea[...] = sea_mask[...].astype(f32)
     wet_field(wet_tiles, wet)
@@ -740,58 +706,66 @@
 
     previous_load.wait()
     lax.fori_loop(0, 2 * SHIFT, one_halo, 0)
-    if inner:
-        inner[0].wait()
-        inner[1].start()
     for load in late:
         load.wait()
-    for i, d in enumerate(edge):
+
+    def inner(d, _):
         source(
-            coef, own.at[d],
-            own.at[d + SHIFT] if d + SHIFT < dirs else halo.at[2 * SHIFT + d - dirs],
-            own.at[d - SHIFT] if d >= SHIFT else halo.at[d],
-            None, rest.at[i], wet, result.at[i],
-        )
-        for store, run in zip(stores, runs):
-            if i == run[0] + run[2] - 1:
-                store.start()
-    for store in stores + inner[1:]:
+            coef, own.at[d], own.at[d + SHIFT], own.at[d - SHIFT], rest.at[d], wet, result.at[d]
+        )
+        return 0
+
+    for store, at, to in zip(stores, bounds, bounds[1:]):
+        if at == cut:
+            for load in latest:
+                load.wait()
+        if at >= SHIFT and to <= dirs - SHIFT:
+            lax.fori_loop(at, to, inner, 0)
+        else:
+            for d in range(at, to):
+                source(
+                    coef, own.at[d],
+                    own.at[d + SHIFT] if d + SHIFT < dirs else halo.at[2 * SHIFT + d - dirs],
+                    own.at[d - SHIFT] if d >= SHIFT else halo.at[d],
+                    rest.at[d], wet, result.at[d],
+                )
+        store.start()
+    for store in stores:
         store.wait()
 
 
 def add_source(
-    halo_marks, quad_coef, sea_mask, wet_tiles, halo_previous, halo_entering, halo_coupling, own, rest, inner
+    halo_marks, quad_coef, sea_mask, wet_tiles, halo_previous, halo_entering, halo_coupling, own, rest
 ):
     dirs, bands, rows, columns = own.shape
-    smem = pl.BlockSpec(memory_space=pltpu.SMEM)
     anywhere = pl.BlockSpec(memory_space=pl.ANY)
-    edges = min(dirs, 2 * SHIFT)
     dma = pltpu.SemaphoreType.DMA
     return pl.pallas_call(
         source_kernel,
-        in_specs=[smem, smem] + [anywhere] * 8,
+        in_specs=[anywhere] * 9,
         out_specs=anywhere,
         out_shape=jax.ShapeDtypeStruct(own.shape, bf16),
         scratch_shapes=[
+            pltpu.SMEM(halo_marks.shape, f32),
+            pltpu.SMEM(quad_coef.shape, f32),
             pltpu.VMEM(halo_previous.shape, bf16),
             pltpu.VMEM(halo_entering.shape, bf16),
             pltpu.VMEM(halo_entering.shape, f32),
             pltpu.VMEM(halo_coupling.shape, f32),
             pltpu.VMEM(own.shape, bf16),
-            pltpu.VMEM((edges, bands, rows, columns), bf16),
+            pltpu.VMEM(own.shape, bf16),
             pltpu.VMEM(halo_previous.shape, bf16),
             pltpu.VMEM(sea_mask.shape, jnp.int32),
             pltpu.VMEM(wet_tiles.shape, jnp.int32),
             pltpu.VMEM((rows, columns), f32),
             pltpu.VMEM((rows, columns), f32),
-            pltpu.VMEM((edges, bands, rows, columns), bf16),
-            pltpu.VMEM((max(dirs - 2 * SHIFT, 1), bands, rows, columns), bf16),
-            dma((8,)), dma((3,)),
+            pltpu.VMEM(own.shape, bf16),
+            dma((9,)), dma((2,)), dma((max(dirs, 5),)),
         ],
         compiler_params=pltpu.CompilerParams(vmem_limit_bytes=STEP_VMEM),
         cost_estimate=cost(6),
         name="add_source",
-    )(halo_marks, quad_coef, sea_mask, wet_tiles, halo_previous, halo_entering, halo_coupling, own, rest, inner)
+    )(halo_marks, quad_coef, sea_mask, wet_tiles, halo_previous, halo_entering, halo_coupling, own, rest)
 
 
 def on_device(
@@ -799,12 +773,11 @@
     previous, boundary, row_coupling, cross_gain, block_inverse, quadrant, sea_mask, wet_tiles, quad_coef,
 ):
     wet_tiles = wet_tiles.T
-    own, rest, inner, halo_previous, halo_entering, halo_coupling, halo_marks = scan_devices(
-        row_devices, dir_devices, quadrant, cross_gain, quad_coef, boundary, sea_mask, previous, row_coupling,
-        wet_tiles,
+    own, rest, halo_previous, halo_entering, halo_coupling, halo_marks = scan_devices(
+        row_devices, dir_devices, quadrant, cross_gain, boundary, sea_mask, previous, row_coupling
     )
     return add_source(
-        halo_marks, quad_coef, sea_mask, wet_tiles, halo_previous, halo_entering, halo_coupling, own, rest, inner
+        halo_marks, quad_coef, sea_mask, wet_tiles, halo_previous, halo_entering, halo_coupling, own, rest
     )
 
 

time: 45.8 us -> 45.2 us (0.987)
  Pallas kernels: 45.4 us -> 44.8 us
    pallas_call x1, Pallas kernels: 39.2 us -> 36.8 us  [scan_devices(): pl.pallas_call(functools.partial(scan_kernel, count, dir_count, chunks),...]
    pallas_call x1, Pallas kernels: 6.22 us -> 7.95 us  [add_source(): pl.pallas_call(source_kernel, in_specs=[anywhere] * 9, out_specs=anywhere...]
where the time goes in v6:
time: 45.2 us; the launch traced here: 44.8 us
  Pallas kernels  44.8 us (99%)
    pallas_call x1, Pallas kernels, scan_devices(): pl.pallas_call(functools.partial(scan_kernel, count, dir_count, chunks),...  36.8 us
    pallas_call x1, Pallas kernels, add_source(): pl.pallas_call(source_kernel, in_specs=[anywhere] * 9, out_specs=anywhere...  7.95 us

profile of v6, /device:TPU:0, one launch (start us, length us, event | category | flops | bytes accessed | tf_op | source)
XLA Modules:
  0.0 44.8 jit_solution(14114505347534524219)
XLA Ops:
  0.0 36.8 %scan_devices.1 = (bf16[12,32,8,512]{3,2,1,0:T(8,128)(2,1)}, bf16[12,32,8,512]{3,2,1,0:T(8,128)(2,1)}, bf16[4,32,8,512]{3,2,1,0:T(8,128)(2,1)}, bf16[2,2,2,2,8,5...) custom-call(s32[12]{0:T(128)} %quadrant.1, f32[12]{0:T(128)} %cross_gain.1, ...), custom_call_target="tpu_custom_call" | custom-call | bytes 90000000 | tf_op jit(solution)/shard_map/scan_devices/pallas_call | solution.py:366
  36.8 7.9 %add_source.1 = bf16[12,32,8,512]{3,2,1,0:T(8,128)(2,1)} custom-call(f32[4,2,128]{2,1,0:T(2,128)} %get-tuple-element.11.marks_in, f32[32]{0:T(128)} %coef_in.1, s32[8,512]{1,0:T(8,128)} %sea_in.3, s32[4,8]{1,0:T(4,128)} %bitcast.3, bf16[4,32,8,512]{3,2,1,0:T(8,128)(2,1)} %get-tuple-element.12.previous_in, ...), custom_call_target="tpu_custom_call" | custom-call | bytes 18000000 | tf_op jit(solution)/shard_map/add_source/pallas_call | solution.py:743

commit v7 on v6

--- a/solution.py
+++ b/solution.py
@@ -50,9 +50,9 @@
 
 
 def scan_kernel(
-    count, dir_count, chunks, quadrant, cross_gain, boundary_in, sea_in, previous_in, coupling_in,
+    count, dir_count, chunks, quadrant_in, cross_gain_in, boundary_in, sea_in, previous_in, coupling_in,
     own_out, rest_out, halo_previous, halo_entering, halo_coupling, halo_marks,
-    out, rest, inflow, edge_state, back_rows, cumulated, settled, rounded, sea_field,
+    quadrant, cross_gain, out, rest, inflow, edge_state, back_rows, cumulated, settled, rounded, sea_field,
     gain, state, shares, marks, boundary, sea_mask, previous, coupling,
     gains, got_core, half_total, got_pair, plane, chain_in, chain_out, pair_in, pair_out, core_out,
     load_sem, gain_send, gain_recv, core_send, core_recv, pair_send, pair_recv,
@@ -99,11 +99,19 @@
         pltpu.make_async_copy(previous_in.at[part(j)], previous.at[part(j)], load_sem.at[3 + j])
         for j in range(chunks)
     ]
+    scalar_loads = [
+        pltpu.make_async_copy(quadrant_in, quadrant, load_sem.at[3 + chunks]),
+        pltpu.make_async_copy(cross_gain_in, cross_gain, load_sem.at[4 + chunks]),
+    ]
+    for load in scalar_loads:
+        load.start()
     sea_load.start()
     coupling_load.start()
     for j in order:
         previous_loads[j].start()
     boundary_load.start()
+    for load in scalar_loads:
+        load.wait()
     for d in range(dirs):
         marks[d, 0:1] = jnp.full((1, marks.shape[2]), cross_gain[d], f32)
         marks[d, 1:2] = jnp.full((1, marks.shape[2]), quadrant[d].astype(f32), f32)
@@ -353,7 +361,6 @@
     quarter = bands // 4
     boundary = boundary.reshape(dirs, 4, quarter, columns)
     vmem = pl.BlockSpec(memory_space=pltpu.VMEM)
-    smem = pl.BlockSpec(memory_space=pltpu.SMEM)
     part = (dirs, quarter, columns)
     dma = pltpu.SemaphoreType.DMA
     anywhere = pl.BlockSpec(memory_space=pl.ANY)
@@ -365,7 +372,7 @@
 
     return pl.pallas_call(
         functools.partial(scan_kernel, count, dir_count, chunks),
-        in_specs=[smem, smem] + [hbm] * 4,
+        in_specs=[hbm] * 6,
         out_specs=[anywhere] * 6,
         out_shape=[
             jax.ShapeDtypeStruct(previous.shape, bf16),
@@ -376,6 +383,8 @@
             jax.ShapeDtypeStruct((2 * SHIFT,) + marks[1:], f32),
         ],
         scratch_shapes=[
+            pltpu.SMEM((dirs,), jnp.int32),
+            pltpu.SMEM((dirs,), f32),
             pltpu.VMEM((2, 2) + part, f32),
             pltpu.VMEM(previous.shape, bf16),
             pltpu.VMEM((4, quarter, columns), f32),
@@ -403,7 +412,7 @@
             pltpu.VMEM((2,) + part, f32),
             pltpu.VMEM(part, f32),
             pltpu.VMEM((2,) + part, f32),
-            dma((3 + chunks,)),
+            dma((5 + chunks,)),
             dma((3,)), dma((3,)),
             dma((chunks,)), dma((chunks,)),
             dma((chunks,)), dma((chunks,)),

time: 45.2 us -> 44.3 us (0.980)
  Pallas kernels: 44.8 us -> 44.1 us
    pallas_call x1, Pallas kernels: 36.8 us -> 36.1 us  [scan_devices(): pl.pallas_call(functools.partial(scan_kernel, count, dir_count, chunks),...]
where the time goes in v7:
time: 44.3 us; the launch traced here: 44.1 us
  Pallas kernels  44.1 us (100%)
    pallas_call x1, Pallas kernels, scan_devices(): pl.pallas_call(functools.partial(scan_kernel, count, dir_count, chunks),...  36.1 us
    pallas_call x1, Pallas kernels, add_source(): pl.pallas_call(source_kernel, in_specs=[anywhere] * 9, out_specs=anywhere...  7.95 us

profile of v7, /device:TPU:0, one launch (start us, length us, event | category | flops | bytes accessed | tf_op | source)
XLA Modules:
  0.0 44.1 jit_solution(12883862774337401435)
XLA Ops:
  0.0 36.1 %scan_devices.1 = (bf16[12,32,8,512]{3,2,1,0:T(8,128)(2,1)}, bf16[12,32,8,512]{3,2,1,0:T(8,128)(2,1)}, bf16[4,32,8,512]{3,2,1,0:T(8,128)(2,1)}, bf16[2,2,2,2,8,5...) custom-call(s32[12]{0:T(128)} %quadrant_in.1, f32[12]{0:T(128)} %cross_gain_in.1, ...), custom_call_target="tpu_custom_call" | custom-call | bytes 90000000 | tf_op jit(solution)/shard_map/scan_devices/pallas_call | solution.py:373
  36.1 7.9 %add_source.1 = bf16[12,32,8,512]{3,2,1,0:T(8,128)(2,1)} custom-call(f32[4,2,128]{2,1,0:T(2,128)} %get-tuple-element.11.marks_in, f32[32]{0:T(128)} %coef_in.1, s32[8,512]{1,0:T(8,128)} %sea_in.3, s32[4,8]{1,0:T(4,128)} %bitcast.3, bf16[4,32,8,512]{3,2,1,0:T(8,128)(2,1)} %get-tuple-element.12.previous_in, ...), custom_call_target="tpu_custom_call" | custom-call | bytes 18000000 | tf_op jit(solution)/shard_map/add_source/pallas_call | solution.py:752
